TPU v7x, 32 devices: a whole 2x2x4 slice. The times are simulated.
32 devices in a mesh: wide: 8 (over z, x), narrow: 4 (over y, core).
Axes of the slice: x: 2, y: 2, z: 4, core: 2. Of those that a mesh axis runs over, the one named last changes fastest.
Arguments:
- field_a: bfloat16 [96, 4, 180, 768], P('wide', 'narrow'), may hold values from -6 to 6
- field_b: bfloat16 [48, 4, 90, 768], P('wide', 'narrow'), may hold values from -6 to 6
- cotangent_a: bfloat16 [96, 4, 180, 768], P('wide', 'narrow'), may hold values from -6 to 6
- cotangent_b: bfloat16 [48, 4, 90, 768], P('wide', 'narrow'), may hold values from -6 to 6
- offsets_a: int32 [9], replicated, may hold values from 0 to 90, as said below
- offsets_b: int32 [9], replicated, may hold values from 0 to 45, as said below
- first_gain: bfloat16 [768], replicated, may hold values from 0.5 to 1.5
- first_bias: bfloat16 [768], replicated, may hold values from -1.75 to 1.75
- inner_weight: bfloat16 [2, 96, 768], replicated, may hold values from -0.4375 to 0.4375
- inner_bias: bfloat16 [2, 768], replicated, may hold values from -1.75 to 1.75
- outer_weight: bfloat16 [2, 96, 768], replicated, may hold values from -0.4375 to 0.4375
- outer_bias: bfloat16 [2, 768], replicated, may hold values from -1.75 to 1.75
- second_gain: bfloat16 [768], replicated, may hold values from 0.5 to 1.5
- second_norm_bias: bfloat16 [768], replicated, may hold values from -1.75 to 1.75
- expand_weight: bfloat16 [768, 3072], P(None, 'narrow'), may hold values from -0.21875 to 0.21875
- expand_bias: bfloat16 [3072], P('narrow'), may hold values from -1.75 to 1.75
- reduce_weight: bfloat16 [3072, 768], P('narrow'), may hold values from -0.109375 to 0.109375
- reduce_bias: bfloat16 [768], replicated, may hold values from -1.75 to 1.75
Outputs:
- mixed_a: bfloat16 [96, 4, 180, 768], P('wide', 'narrow')
- mixed_b: bfloat16 [48, 4, 90, 768], P('wide', 'narrow')
- grad_field_a: float32 [96, 4, 180, 768], P('wide', 'narrow')
- grad_field_b: float32 [48, 4, 90, 768], P('wide', 'narrow')
- grad_first_gain: float32 [768], replicated
- grad_first_bias: float32 [768], replicated
- grad_inner_weight: float32 [2, 96, 768], replicated
- grad_inner_bias: float32 [2, 768], replicated
- grad_outer_weight: float32 [2, 96, 768], replicated
- grad_outer_bias: float32 [2, 768], replicated
- grad_second_gain: float32 [768], replicated
- grad_second_bias: float32 [768], replicated
- grad_expand_weight: float32 [768, 3072], P(None, 'narrow')
- grad_expand_bias: float32 [3072], P('narrow')
- grad_reduce_weight: float32 [3072, 768], P('narrow')
- grad_reduce_bias: float32 [768], replicated
Inputs may be any that keep to these rules, and one draw needn't show every extreme that they name: offsets_a starts at 0, ends at 90 and never falls; each wide device holds 11 or 12 patch rows, and exactly 90 % 8 devices hold 12. offsets_b starts at 0, ends at 45 and never falls; each wide device holds 5 or 6 patch rows, and exactly 45 % 8 devices hold 6.
All inputs are finite; a program needn't handle non-finite values.
Results may differ from a plain program's by a relative error of at most 0.015.
The roundings to bfloat16 on the way count: a program that leaves them out, or rounds other values in their place, can miss the bound.
Values may be sent and summed in bfloat16 or wider, within the bound.
No kernel may reach another device: no remote copies, remote signals or barrier semaphores. Data moves between devices by JAX's collectives and lax.ppermute only.
A program may use at most 320 MiB of HBM per device.

v0:
```python
import math

import jax
import jax.numpy as jnp
from jax import lax
from jax.sharding import PartitionSpec as P

NBL = 8
BS = 96
H_A = 90
H_B = 45


EPSILON = 1e-05
SHRINK = 0.01
HIGH = lax.Precision.HIGHEST
ROOT_HALF = 0.7071067811865476
ROOT_TWO_PI = 2.5066282746310002


def gelu_value(value):
    return 0.5 * value * (1.0 + lax.erf(value * ROOT_HALF))


def gelu_slope(value):
    return (
        0.5 * (1.0 + lax.erf(value * ROOT_HALF))
        + value * jnp.exp(-0.5 * value * value) / ROOT_TWO_PI
    )


def shrink_value(value):
    return value - SHRINK * jnp.tanh(value / SHRINK)


def shrink_slope(value):
    bent = jnp.tanh(value / SHRINK)
    return bent * bent


def phase(left, right, length):
    turns = left * right % length
    return turns.astype(jnp.float32) * (2.0 * math.pi / length)


def row_slots(offsets, depth, width):
    offset = jnp.arange(depth, dtype=jnp.int32)
    begin = offsets[:width]
    counts = offsets[1:] - begin
    line = (begin[:, None] + offset[None, :]).reshape(-1)
    valid = (offset[None, :] < counts[:, None]).reshape(-1).astype(jnp.float32)
    return (line, valid)


def column_slots(freqs, spread, width):
    edges = jnp.arange(width + 1, dtype=jnp.int32) * freqs // width
    offset = jnp.arange(spread, dtype=jnp.int32)
    begin = edges[:width]
    valid = (offset[None, :] < (edges[1:] - begin)[:, None]).reshape(-1).astype(jnp.float32)
    return ((begin[:, None] + offset[None, :]).reshape(-1), valid)


def forward_w_table(columns, freq, valid, width, spread):
    angle = phase(jnp.arange(columns, dtype=jnp.int32)[:, None], freq[None, :], columns)
    scale = valid[None, :] / math.sqrt(columns)
    table = jnp.stack([jnp.cos(angle) * scale, -jnp.sin(angle) * scale], axis=1)
    return table.reshape(columns, 2, width, spread)


def inverse_w_table(columns, freq, valid, width, spread):
    angle = phase(freq[:, None], jnp.arange(columns, dtype=jnp.int32)[None, :], columns)
    edge = (freq == 0) | (2 * freq == columns)
    weight = jnp.where(edge, 1.0, 2.0) * valid / math.sqrt(columns)
    real = jnp.cos(angle) * weight[:, None]
    imag = jnp.where(edge[:, None], 0.0, -jnp.sin(angle)) * weight[:, None]
    return jnp.stack([real, imag], axis=1).reshape(width, spread, 2, columns)


def forward_h_table(height, line, valid):
    angle = phase(jnp.arange(height, dtype=jnp.int32)[:, None], line[None, :], height)
    scale = valid[None, :] / math.sqrt(height)
    cosine = jnp.cos(angle) * scale
    sine = jnp.sin(angle) * scale
    upper = jnp.stack([cosine, sine], axis=-1)
    lower = jnp.stack([-sine, cosine], axis=-1)
    return jnp.stack([upper, lower], axis=1)


def inverse_h_table(height, line, valid):
    angle = phase(line[:, None], jnp.arange(height, dtype=jnp.int32)[None, :], height)
    scale = valid[:, None] / math.sqrt(height)
    cosine = jnp.cos(angle) * scale
    sine = jnp.sin(angle) * scale
    upper = jnp.stack([cosine, -sine], axis=-1)
    lower = jnp.stack([sine, cosine], axis=-1)
    return jnp.stack([upper, lower], axis=1)


def complex_weight(weight):
    blocked = weight.reshape(2, BS, NBL, BS).transpose(0, 2, 1, 3)
    return jnp.stack([jnp.stack([blocked[0], blocked[1]]), jnp.stack([-blocked[1], blocked[0]])])


def fold_weight(grad):
    folded = jnp.stack([grad[0, 0] + grad[1, 1], grad[0, 1] - grad[1, 0]])
    return folded.transpose(0, 2, 1, 3).reshape(2, BS, NBL * BS)


def on_device(
    field_a,
    field_b,
    cotangent_a,
    cotangent_b,
    offsets_a,
    offsets_b,
    first_gain,
    first_bias,
    inner_weight,
    inner_bias,
    outer_weight,
    outer_bias,
    second_gain,
    second_norm_bias,
    expand_weight,
    expand_bias,
    reduce_weight,
    reduce_bias,
):
    width = lax.axis_size("wide")
    myself = lax.axis_index("wide")
    local = field_a.shape[-1]
    layouts = []
    for field, offsets, height in ((field_a, offsets_a, H_A), (field_b, offsets_b, H_B)):
        depth, snaps, columns = (field.shape[0], field.shape[1], field.shape[2])
        freqs = columns // 2 + 1
        spread = (freqs + width - 1) // width
        line, row_valid = row_slots(offsets, depth, width)
        freq, freq_valid = column_slots(freqs, spread, width)
        layouts.append(
            (
                depth,
                snaps,
                columns,
                spread,
                height,
                forward_w_table(columns, freq, freq_valid, width, spread),
                inverse_w_table(columns, freq, freq_valid, width, spread),
                forward_h_table(height, line, row_valid),
                inverse_h_table(height, line, row_valid),
                lax.dynamic_slice_in_dim(row_valid, myself * depth, depth),
            )
        )
    token_count = layouts[0][0] * layouts[0][1] * layouts[0][2]
    point_count = layouts[0][4] * layouts[0][1] * layouts[0][3]

    def to_grids(tokens):
        return [
            tokens[:token_count].reshape(
                layouts[0][0], layouts[0][1], layouts[0][2], tokens.shape[-1]
            ),
            tokens[token_count:].reshape(
                layouts[1][0], layouts[1][1], layouts[1][2], tokens.shape[-1]
            ),
        ]

    def to_tokens(parts):
        return jnp.concatenate([piece.reshape(-1, piece.shape[-1]) for piece in parts])

    def to_spectra(points):
        pieces = (points[:point_count], points[point_count:])
        return [
            pieces[index].reshape(layouts[index][4], layouts[index][1], layouts[index][3], 2, local)
            for index in range(2)
        ]

    def to_sends(parts):
        return [
            parts[index].reshape(
                width, layouts[index][0], layouts[index][1], layouts[index][3], 2, local
            )
            for index in range(2)
        ]

    mask = to_tokens(
        [
            jnp.broadcast_to(lay[9][:, None, None, None], (lay[0], lay[1], lay[2], 1))
            for lay in layouts
        ]
    )
    first_norm_gain = first_gain.astype(jnp.float32)
    first_norm_bias = first_bias.astype(jnp.float32)
    bias_out = reduce_bias.astype(jnp.float32)
    weight_one = complex_weight(inner_weight)
    weight_two = complex_weight(outer_weight)
    shift_one = inner_bias.astype(jnp.float32).reshape(2, NBL, BS)
    shift_two = outer_bias.astype(jnp.float32).reshape(2, NBL, BS)
    source = jnp.concatenate([field_a.reshape(-1, local), field_b.reshape(-1, local)]).astype(
        jnp.float32
    )
    mean_one = jnp.mean(source, axis=1, keepdims=True)
    first_centered_input = source - mean_one
    first_inverse_deviation = lax.rsqrt(
        jnp.mean(first_centered_input * first_centered_input, axis=1, keepdims=True) + EPSILON
    )
    first_standardized = first_centered_input * first_inverse_deviation
    normalized_rows = first_standardized * first_norm_gain + first_norm_bias
    normed_parts = to_grids(normalized_rows)
    sends = [
        jnp.einsum(
            "rswc,wtjk->jrsktc", normed_parts[index], layouts[index][5], precision=HIGH
        ).astype(jnp.bfloat16)
        for index in range(2)
    ]
    arrived = (
        lax.all_to_all(sends[0], "wide", split_axis=0, concat_axis=1, tiled=True),
        lax.all_to_all(sends[1], "wide", split_axis=0, concat_axis=1, tiled=True),
    )
    spectra = [
        jnp.einsum(
            "kumt,msqtc->ksquc",
            layouts[index][7],
            arrived[index][0].astype(jnp.float32),
            precision=HIGH,
        )
        for index in range(2)
    ]
    zed = jnp.concatenate([piece.reshape(-1, 2, NBL, BS) for piece in spectra]).astype(jnp.bfloat16)
    pre_one = (
        jnp.einsum("pcbi,cdbio->pdbo", zed, weight_one, preferred_element_type=jnp.float32)
        + shift_one
    )
    act_one = gelu_value(pre_one).astype(jnp.bfloat16)
    pre_two = (
        jnp.einsum("pcbi,cdbio->pdbo", act_one, weight_two, preferred_element_type=jnp.float32)
        + shift_two
    )
    shrunk = to_spectra(shrink_value(pre_two))
    outgoing = to_sends(
        [
            jnp.einsum(
                "mukt,ksqtc->msquc", layouts[index][8], shrunk[index], precision=HIGH
            ).astype(jnp.bfloat16)
            for index in range(2)
        ]
    )
    returned = (
        lax.all_to_all(outgoing[0], "wide", split_axis=0, concat_axis=1, tiled=True),
        lax.all_to_all(outgoing[1], "wide", split_axis=0, concat_axis=1, tiled=True),
    )
    field_parts = to_grids(source)
    middle_parts = []
    for index in range(2):
        lay = layouts[index]
        received = (
            returned[index][0].reshape(width, lay[0], lay[1], lay[3], 2, local).astype(jnp.float32)
        )
        middle_parts.append(
            jnp.einsum("jrsktc,jktw->rswc", received, lay[6], precision=HIGH)
            + normed_parts[index]
            + field_parts[index]
        )
    middle = to_tokens(middle_parts)
    mean_two = jnp.mean(middle, axis=1, keepdims=True)
    second_centered_input = middle - mean_two
    second_inverse_deviation = lax.rsqrt(
        jnp.mean(second_centered_input * second_centered_input, axis=1, keepdims=True) + EPSILON
    )
    second_standardized = second_centered_input * second_inverse_deviation
    second_norm_gain = second_gain.astype(jnp.float32)
    input_rows = (
        second_standardized * second_norm_gain + second_norm_bias.astype(jnp.float32)
    ).astype(jnp.bfloat16)
    full_inputs = lax.all_gather(input_rows, "narrow", axis=0, tiled=True)
    pre_three = jnp.dot(
        full_inputs, expand_weight, preferred_element_type=jnp.float32
    ) + expand_bias.astype(jnp.float32)
    act_three = gelu_value(pre_three).astype(jnp.bfloat16)
    partial_value = jnp.dot(act_three, reduce_weight, preferred_element_type=jnp.float32)
    mixed = (
        lax.psum_scatter(
            partial_value.astype(jnp.bfloat16), "narrow", scatter_dimension=0, tiled=True
        ).astype(jnp.float32)
        + bias_out
    )
    result = to_grids((middle + mixed) * mask)
    upstream = jnp.concatenate([cotangent_a.reshape(-1, local), cotangent_b.reshape(-1, local)])
    upstream = jnp.where(mask > 0.0, upstream, jnp.zeros_like(upstream))
    upstream_f = upstream.astype(jnp.float32)
    grad_out_b = jnp.sum(upstream_f, 0)
    full_upstream = lax.all_gather(upstream, "narrow", axis=0, tiled=True)
    grad_act = jnp.einsum(
        "td,fd->tf", full_upstream, reduce_weight, preferred_element_type=jnp.float32
    )
    grad_pre = (grad_act * gelu_slope(pre_three)).astype(jnp.bfloat16)
    grad_reduce = jnp.einsum(
        "tf,td->fd", act_three, full_upstream, preferred_element_type=jnp.float32
    )
    grad_expand = jnp.einsum("td,tf->df", full_inputs, grad_pre, preferred_element_type=jnp.float32)
    grad_expand_b = jnp.sum(grad_pre.astype(jnp.float32), 0)
    grad_terms = jnp.einsum(
        "tf,df->td", grad_pre, expand_weight, preferred_element_type=jnp.float32
    )
    input_gradient = lax.psum_scatter(
        grad_terms.astype(jnp.bfloat16), "narrow", scatter_dimension=0, tiled=True
    ).astype(jnp.float32)
    scaled_rows = input_gradient * second_norm_gain
    gradient_second_norm_gain = jnp.sum(input_gradient * second_standardized, 0)
    grad_bias_two = jnp.sum(input_gradient, 0)
    grad_full = second_inverse_deviation * (
        scaled_rows
        - jnp.mean(scaled_rows, axis=1, keepdims=True)
        - second_standardized * jnp.mean(scaled_rows * second_standardized, axis=1, keepdims=True)
    )
    grad_middle = grad_full + upstream_f
    grad_parts = to_grids(grad_middle)
    sends = [
        jnp.einsum(
            "rswc,jktw->jrsktc", grad_parts[index], layouts[index][6], precision=HIGH
        ).astype(jnp.bfloat16)
        for index in range(2)
    ]
    arrived = (
        lax.all_to_all(sends[0], "wide", split_axis=0, concat_axis=1, tiled=True),
        lax.all_to_all(sends[1], "wide", split_axis=0, concat_axis=1, tiled=True),
    )
    grad_points = jnp.concatenate(
        [
            jnp.einsum(
                "mukt,msquc->ksqtc",
                layouts[index][8],
                arrived[index][0].astype(jnp.float32),
                precision=HIGH,
            ).reshape(-1, 2, NBL, BS)
            for index in range(2)
        ]
    )
    grad_two = (grad_points * shrink_slope(pre_two)).astype(jnp.bfloat16)
    grad_hidden = jnp.einsum(
        "pdbo,cdbio->pcbi", grad_two, weight_two, preferred_element_type=jnp.float32
    )
    grad_weight_two = fold_weight(
        jnp.einsum("pcbi,pdbo->cdbio", act_one, grad_two, preferred_element_type=jnp.float32)
    )
    grad_shift_two = jnp.sum(grad_two.astype(jnp.float32), 0).reshape(2, -1)
    grad_one = (grad_hidden * gelu_slope(pre_one)).astype(jnp.bfloat16)
    grad_zed = jnp.einsum(
        "pdbo,cdbio->pcbi", grad_one, weight_one, preferred_element_type=jnp.float32
    )
    grad_weight_one = fold_weight(
        jnp.einsum("pcbi,pdbo->cdbio", zed, grad_one, preferred_element_type=jnp.float32)
    )
    grad_shift_one = jnp.sum(grad_one.astype(jnp.float32), 0).reshape(2, -1)
    grad_spectra = to_spectra(grad_zed)
    outgoing = to_sends(
        [
            jnp.einsum(
                "kumt,ksquc->msqtc", layouts[index][7], grad_spectra[index], precision=HIGH
            ).astype(jnp.bfloat16)
            for index in range(2)
        ]
    )
    returned = (
        lax.all_to_all(outgoing[0], "wide", split_axis=0, concat_axis=1, tiled=True),
        lax.all_to_all(outgoing[1], "wide", split_axis=0, concat_axis=1, tiled=True),
    )
    grad_normed_parts = []
    for index in range(2):
        lay = layouts[index]
        received = (
            returned[index][0].reshape(width, lay[0], lay[1], lay[3], 2, local).astype(jnp.float32)
        )
        grad_normed_parts.append(
            jnp.einsum("jrsktc,wtjk->rswc", received, lay[5], precision=HIGH) + grad_parts[index]
        )
    normalized_gradient = to_tokens(grad_normed_parts)
    scaled_rows = normalized_gradient * first_norm_gain
    grad_source = (
        first_inverse_deviation
        * (
            scaled_rows
            - jnp.mean(scaled_rows, axis=1, keepdims=True)
            - first_standardized * jnp.mean(scaled_rows * first_standardized, axis=1, keepdims=True)
        )
        + grad_middle
    )
    grad_fields = to_grids(grad_source * mask)
    gradient_first_norm_gain = jnp.sum(normalized_gradient * first_standardized, 0)
    grad_bias_one = jnp.sum(normalized_gradient, 0)
    mlp_sums = lax.psum((grad_expand, grad_expand_b, grad_reduce), "wide")
    shared = lax.psum(
        (
            grad_weight_one,
            grad_shift_one,
            grad_weight_two,
            grad_shift_two,
            gradient_first_norm_gain,
            grad_bias_one,
            gradient_second_norm_gain,
            grad_bias_two,
            grad_out_b,
        ),
        ("wide", "narrow"),
    )
    return (
        result[0].astype(jnp.bfloat16),
        result[1].astype(jnp.bfloat16),
        grad_fields[0],
        grad_fields[1],
        shared[4],
        shared[5],
        shared[0],
        shared[1],
        shared[2],
        shared[3],
        shared[6],
        shared[7],
        mlp_sums[0],
        mlp_sums[1],
        mlp_sums[2],
        shared[8],
    )


def solution(mesh):
    placed = (
        P("wide", "narrow", None, None),
        P("wide", "narrow", None, None),
        P("wide", "narrow", None, None),
        P("wide", "narrow", None, None),
        P(),
        P(),
        P(),
        P(),
        P(),
        P(),
        P(),
        P(),
        P(),
        P(),
        P(None, "narrow"),
        P("narrow"),
        P("narrow", None),
        P(),
    )
    return jax.shard_map(
        on_device,
        mesh=mesh,
        in_specs=placed,
        out_specs=(
            P("wide", "narrow", None, None),
            P("wide", "narrow", None, None),
            P("wide", "narrow", None, None),
            P("wide", "narrow", None, None),
            P(),
            P(),
            P(),
            P(),
            P(),
            P(),
            P(),
            P(),
            P(None, "narrow"),
            P("narrow"),
            P("narrow", None),
            P(),
        ),
        check_vma=False,
    )
```

profile of v0, /device:TPU:0, one launch (start us, length us, event | category | flops | bytes accessed | tf_op | source)
XLA Modules:
  0.0 1656.9 jit_solution(9498598787062637238)
XLA Ops:
  11.1 5.9 reshape.1774
  17.0 6.0 fusion.201
  33.0 6.1 multiply_reduce_fusion.3
  58.5 7.7 all-to-all-start.1
  66.2 6.1 slice.172
  72.3 7.2 reshape.1807
  80.4 10.1 convert_bitcast_fusion.1
  90.5 6.6 copy.262
  97.2 6.3 all-to-all-start
  124.5 57.6 %all-to-all-done = bf16[8,12,1,12,2,768]{5,4,3,2,1,0:T(2,128)(2,1)} async-done(((bf16[8,12,1,12,2,768]{5,4,3,2,1,0:T(2,128)(2,1)}), bf16[8,12,1,12,2,768]{5,4,3,2,1,0:T(2,128)(2,1)}, u32[]{:S(2)}, u32[]{:S(2)}) %all-to-all-start) | async-done | bytes 3538976 | tf_op jit(solution)/shard_map/all_to_all | solution.py:215
  182.0 5.9 fusion.45
  193.1 10.3 reshape.1758
  203.4 6.6 copy.270
  245.9 6.4 slice.174
  252.3 8.9 copy.274
  261.2 11.2 reshape.1762
  272.4 11.0 fusion.46
  288.9 6.0 all-to-all-start.2
  297.7 7.2 reshape.1765
  315.1 7.2 reshape.1766
  328.8 45.0 %all-to-all-done.2 = bf16[8,12,1,12,2,768]{5,4,3,2,1,0:T(2,128)(2,1)} async-done(((bf16[8,12,1,12,2,768]{5,4,3,2,1,0:T(2,128)(2,1)}), bf16[8,12,1,12,2,768]{5,4,3,2,1,0:T(2,128)(2,1)}, u32[]{:S(2)}, u32[]{:S(2)}) %all-to-all-start.2) | async-done | bytes 3538976 | tf_op jit(solution)/shard_map/all_to_all | solution.py:247
  373.7 12.2 fusion.26
  386.0 7.2 reshape.1767
  393.1 6.0 constant_dynamic-update-slice_fusion.1
  417.7 20.8 %reshape.1805 = bf16[10800,768]{1,0:T(8,128)(2,1)} reshape(bf16[4,2700,768]{2,1,0:T(8,128)(2,1)} %all-gather.7.cloned.1.call-done) | data formatting | bytes 33177600
  438.5 80.8 %all-gather.5.cloned.1.call-done = bf16[4,2700,768]{2,1,0:T(8,128)(2,1)} async-done(((bf16[1,2700,768]{2,1,0:T(8,128)(2,1)}), bf16[4,2700,768]{2,1,0:T(8,128)(2,1)}) %all-gather.5.cloned.1.call-update) | async-done | bytes 16588816 | tf_op jit(solution)/shard_map/all_gather | solution.py:273
  519.3 16.4 reshape.1803
  535.7 25.3 %multiply_convert_fusion = (bf16[10800,768]{1,0:T(8,128)(2,1)}, f32[10800,768]{1,0:T(8,128)}) fusion(f32[768]{0:T(1024)S(1)} %convert_element_type.361, bf16[10800,768]{1,0:T(8,128)(2,1)} %reshape.1803, bf16[768,768]{1,0:T(8,128)(2,1)S(1)} %copy-done), kind=kOutput, calls=%fused_computation.8 | convolution fusion | flops 12789964800 | bytes 67537920 | tf_op jit(solution)/shard_map/dot_general | solution.py:274
  561.0 21.9 %convolution_convert_fusion.1 = bf16[10800,768]{1,0:T(8,128)(2,1)} fusion(bf16[10800,768]{1,0:T(8,128)(2,1)} %get-tuple-element.169, bf16[768,768]{1,0:T(8,128)(2,1)S(1)} %copy-done.105), kind=kOutput, calls=%fused_computation.11 | convolution fusion | flops 12748492800 | bytes 34357248 | tf_op jit(solution)/shard_map/dot_general | solution.py:278
  583.0 30.6 %convert_reduce_fusion = (f32[768]{0:T(1024)}, bf16[10800,768]{1,0:T(8,128)(2,1)}) fusion(f32[10800,768]{1,0:T(8,128)} %get-tuple-element.170, f32[768]{0:T(1024)S(1)} %convert_element_type.361, bf16[10800,768]{1,0:T(8,128)(2,1)} %reshape.1805, bf16[768,768]{1,0:T(8,128)(2,1)S(1)} %copy-done.105), kind=kOutput, calls=%fused_computation.7 | convolution fusion | flops 12848024576 | bytes 67540992 | tf_op jit(solution)/shard_map/td,fd->tf/dot_general | solution.py:291
  613.6 21.8 %convolution_convert_fusion = bf16[10800,768]{1,0:T(8,128)(2,1)} fusion(bf16[10800,768]{1,0:T(8,128)(2,1)} %get-tuple-element.174, bf16[768,768]{1,0:T(8,128)(2,1)S(1)} %copy-done), kind=kOutput, calls=%fused_computation.10 | convolution fusion | flops 12748492800 | bytes 34357248 | tf_op jit(solution)/shard_map/tf,df->td/dot_general | solution.py:300
  635.4 143.8 %fusion.1 = bf16[2704,768]{1,0:T(8,128)(2,1)} fusion(bf16[10800,768]{1,0:T(8,128)(2,1)} %convolution_convert_fusion), kind=kCustom, calls=%all-reduce-scatter.1 | all-reduce-scatter fusion | flops 8306689 | bytes 20742656
  781.2 145.9 %fusion = bf16[2704,768]{1,0:T(8,128)(2,1)} fusion(bf16[10800,768]{1,0:T(8,128)(2,1)} %convolution_convert_fusion.1), kind=kCustom, calls=%all-reduce-scatter | all-reduce-scatter fusion | flops 8306689 | bytes 20742656
  929.2 19.8 %concatenate.48 = bf16[2716,768]{1,0:T(8,128)(2,1)} concatenate(bf16[12,768]{1,0:T(8,128)(2,1)S(1)} %collective-permute-done.1, bf16[2704,768]{1,0:T(8,128)(2,1)} %fusion.1), dimensions={0} | concatenate | bytes 8343552
  949.0 8.7 fusion.21
  957.7 19.6 %concatenate.47 = bf16[2716,768]{1,0:T(8,128)(2,1)} concatenate(bf16[12,768]{1,0:T(8,128)(2,1)S(1)} %collective-permute-done, bf16[2704,768]{1,0:T(8,128)(2,1)} %fusion), dimensions={0} | concatenate | bytes 8343552
  977.4 12.4 convert_add_fusion
  999.3 5.9 all-to-all-start.5
  1005.2 6.1 slice.180
  1011.3 7.2 reshape.1830
  1018.6 10.0 convert_bitcast_fusion
  1028.6 6.6 copy.287
  1035.2 6.0 all-to-all-start.4
  1051.8 69.3 %all-to-all-done.4 = bf16[8,12,1,12,2,768]{5,4,3,2,1,0:T(2,128)(2,1)} async-done(((bf16[8,12,1,12,2,768]{5,4,3,2,1,0:T(2,128)(2,1)}), bf16[8,12,1,12,2,768]{5,4,3,2,1,0:T(2,128)(2,1)}, u32[]{:S(2)}, u32[]{:S(2)}) %all-to-all-start.4) | async-done | bytes 3538976 | tf_op jit(solution)/shard_map/all_to_all | solution.py:323
  1121.2 8.0 fusion.56
  1129.2 10.8 copy.290
  1140.0 11.0 reshape.1778
  1151.0 8.8 copy.295
  1159.9 8.2 convert_reduce_fusion.3
  1168.2 9.0 convert_reduce_fusion.4
  1201.2 20.3 %fusion.211 = f32[768,768]{1,0:T(8,128)} fusion(bf16[10800,768]{1,0:T(8,128)(2,1)} %get-tuple-element.169, bf16[10800,768]{1,0:T(8,128)(2,1)} %reshape.1805), kind=kOutput, calls=%fused_computation.323 | convolution fusion | flops 12740198400 | bytes 35536896 | tf_op jit(solution)/shard_map/tf,td->fd/dot_general | solution.py:295
  1225.0 8.9 copy.299
  1233.9 11.2 reshape.1782
  1245.2 11.0 fusion.47
  1261.6 6.0 all-to-all-start.6
  1267.7 20.2 %fusion.210 = f32[768,768]{1,0:T(8,128)} fusion(bf16[10800,768]{1,0:T(8,128)(2,1)} %reshape.1803, bf16[10800,768]{1,0:T(8,128)(2,1)} %get-tuple-element.174), kind=kOutput, calls=%fused_computation.322 | convolution fusion | flops 12740198400 | bytes 35536896 | tf_op jit(solution)/shard_map/td,tf->df/dot_general | solution.py:298
  1287.9 84.1 %psum.93 = f32[768]{0:T(1024)} all-reduce(f32[768]{0:T(1024)S(1)} %copy-done.95), channel_id=1, replica_groups=mesh['wide'=8,'narrow'=4] {'wide'}, use_global_device_ids=true, to_apply=%region_27.28 | all-reduce | flops 768 | bytes 6144 | tf_op jit(solution)/shard_map/psum | solution.py:389
  1379.6 7.4 reshape.1785
  1418.2 6.8 fusion.205
  1425.1 7.3 reshape.1786
  1436.4 8.1 multiply_reduce_fusion
  1458.7 10.2 reshape.1854
  1468.9 73.7 %all-reduce.4 = (f32[768]{0:T(1024)}, f32[768]{0:T(1024)}, f32[2,768]{1,0:T(2,128)}, f32[2,768]{1,0:T(2,128)}, f32[768]{0:T(1024)}, /*index=5*/f32[768]{0:T(1024)}, f32[768]{0:T(1024)}) all-reduce(f32[768]{0:T(1024)S(1)} %get-tuple-element.98, f32[768]{0:T(1024)S(1)} %reduce_sum.163, ...), channel_id=1, replica_groups=mesh['wide'=8,'narrow'=4] {'wide','narrow'}, use_global_device_ids=true, to_apply=%region_11.12 | all-reduce | flops 6912 | bytes 55296 | tf_op jit(solution)/shard_map/psum | solution.py:390
  1542.6 98.9 %all-reduce.10.cloned.1.call-done = (f32[2,96,768]{2,1,0:T(8,128)}, f32[2,96,768]{2,1,0:T(8,128)}) async-done(((f32[2,96,768]{2,1,0:T(8,128)}, f32[2,96,768]{2,1,0:T(8,128)}), (f32[2,96,768]{2,1,0:T(8,128)}, f32[2,96,768]{2,1,0:T(8,128)})) %all-reduce.10.cloned.1.call-update) | async-done | bytes 1179664 | tf_op jit(solution)/shard_map/psum | solution.py:390
  (407 shorter events, 260.6 us)
Async XLA Ops:
  7.2 528.5 %copy-start = (bf16[768,768]{1,0:T(8,128)(2,1)S(1)}, bf16[768,768]{1,0:T(8,128)(2,1)}, u32[]{:S(2)}) copy-start(bf16[768,768]{1,0:T(8,128)(2,1)} %param.32) | copy-start | bytes 3538948
  7.2 410.5 %all-gather.7.cloned.1.call-start = ((), (), s32[]{:S(2)}) async-start(), calls=%async_computation.9 | async-start | bytes 20766720 | tf_op jit(solution)/shard_map/all_gather | solution.py:290
  11.0 12.9 copy-start.37
  17.0 13.0 copy-start.80
  24.1 280.8 %copy-start.7 = (bf16[540,768]{1,0:T(8,128)(2,1)}, bf16[540,768]{1,0:T(8,128)(2,1)S(1)}, u32[]{:S(2)}) copy-start(bf16[540,768]{1,0:T(8,128)(2,1)S(1)} %reshape.1755) | copy-start | bytes 2488324
  32.8 12.7 copy-start.74
  58.5 38.7 %all-to-all-start.1 = ((bf16[8,6,1,6,2,768]{5,4,3,2,1,0:T(2,128)(2,1)}), bf16[8,6,1,6,2,768]{5,4,3,2,1,0:T(2,128)(2,1)S(1)}, u32[]{:S(2)}, u32[]{:S(2)}) async-start(bf16[8,6,1,6,2,768]{5,4,3,2,1,0:T(2,128)(2,1)} %copy.267), calls=%async_computation.1 | async-start | bytes 1769472 | tf_op jit(solution)/shard_map/all_to_all | solution.py:216
  79.6 17.6 %copy-start.93 = (s32[8]{0:T(128)}, s32[8]{0:T(128)S(1)}, u32[]{:S(2)}) copy-start(s32[8]{0:T(128)S(1)} %get-tuple-element.161) | copy-start | bytes 100
  80.4 16.8 %copy-start.38 = (f32[180,1,8,12]{0,3,2,1:T(8,128)}, f32[180,1,8,12]{0,3,2,1:T(8,128)S(1)}, u32[]{:S(2)}) copy-start(f32[180,1,8,12]{0,3,2,1:T(8,128)S(1)} %get-tuple-element.139) | copy-start | bytes 207364
  80.4 16.8 %copy-start.40 = (f32[180,1,8,12]{0,3,2,1:T(8,128)}, f32[180,1,8,12]{0,3,2,1:T(8,128)S(1)}, u32[]{:S(2)}) copy-start(f32[180,1,8,12]{0,3,2,1:T(8,128)S(1)} %get-tuple-element.140) | copy-start | bytes 207364
  90.5 13.6 copy-start.96
  90.5 14.2 copy-start.97
  97.2 84.9 %all-to-all-start = ((bf16[8,12,1,12,2,768]{5,4,3,2,1,0:T(2,128)(2,1)}), bf16[8,12,1,12,2,768]{5,4,3,2,1,0:T(2,128)(2,1)}, u32[]{:S(2)}, u32[]{:S(2)}) async-start(bf16[8,12,1,12,2,768]{5,4,3,2,1,0:T(2,128)(2,1)} %copy.262), calls=%async_computation | async-start | bytes 7077888 | tf_op jit(solution)/shard_map/all_to_all | solution.py:215
  103.8 14.5 copy-start.87
  104.1 14.2 copy-start.89
  104.9 114.5 %copy-start.72 = (f32[2,8,96]{2,0,1:T(2,128)}, f32[2,8,96]{2,0,1:T(2,128)S(1)}, u32[]{:S(2)}) copy-start(f32[2,8,96]{2,0,1:T(2,128)S(1)} %copy.273) | copy-start | bytes 18436
  108.3 101.7 %copy-start.16 = (bf16[2,96,8,96]{1,3,0,2:T(8,128)(2,1)}, bf16[2,96,8,96]{1,3,0,2:T(8,128)(2,1)S(1)}, u32[]{:S(2)}) copy-start(bf16[2,96,8,96]{1,3,0,2:T(8,128)(2,1)S(1)} %copy.260) | copy-start | bytes 884740
  193.1 16.9 %copy-start.23 = (bf16[1,2,8,96,96]{3,4,0,1,2:T(8,128)(2,1)S(1)}, bf16[1,2,8,96,96]{3,4,0,1,2:T(8,128)(2,1)}, u32[]{:S(2)}) copy-start(bf16[1,2,8,96,96]{3,4,0,1,2:T(8,128)(2,1)} %maximum_bitcast_fusion.6) | copy-start | bytes 884740
  223.9 12.8 copy-start.46
  223.9 12.8 copy-start.48
  229.4 16.1 copy-start.88
  229.4 16.1 copy-start.90
  241.7 47.2 %all-to-all-start.3 = ((bf16[8,6,1,6,2,768]{5,4,3,1,2,0:T(2,128)(2,1)}), bf16[8,6,1,6,2,768]{5,4,3,1,2,0:T(2,128)(2,1)S(1)}, u32[]{:S(2)}, u32[]{:S(2)}) async-start(bf16[8,6,1,6,2,768]{5,4,3,1,2,0:T(2,128)(2,1)} %bitcast.462), calls=%async_computation.3 | async-start | bytes 1769472 | tf_op jit(solution)/shard_map/all_to_all | solution.py:248
  245.8 26.6 %copy-start.33 = (f32[96,1,90,2]{2,0,3,1:T(8,128)}, f32[96,1,90,2]{2,0,3,1:T(8,128)S(1)}, u32[]{:S(2)}) copy-start(f32[96,1,90,2]{2,0,3,1:T(8,128)S(1)} %get-tuple-element.127) | copy-start | bytes 207364
  245.9 26.6 %copy-start.35 = (f32[96,1,90,2]{2,0,3,1:T(8,128)}, f32[96,1,90,2]{2,0,3,1:T(8,128)S(1)}, u32[]{:S(2)}) copy-start(f32[96,1,90,2]{2,0,3,1:T(8,128)S(1)} %get-tuple-element.128) | copy-start | bytes 207364
  288.9 16.0 copy-start.20
  288.9 84.9 %all-to-all-start.2 = ((bf16[8,12,1,12,2,768]{5,4,3,2,1,0:T(2,128)(2,1)}), bf16[8,12,1,12,2,768]{5,4,3,2,1,0:T(2,128)(2,1)}, u32[]{:S(2)}, u32[]{:S(2)}) async-start(bf16[8,12,1,12,2,768]{5,4,3,2,1,0:T(2,128)(2,1)} %bitcast.455), calls=%async_computation.2 | async-start | bytes 7077888 | tf_op jit(solution)/shard_map/all_to_all | solution.py:247
  294.9 224.4 %all-gather.5.cloned.1.call-start = ((), (), s32[]{:S(2)}) async-start(), calls=%async_computation.8 | async-start | bytes 20766720 | tf_op jit(solution)/shard_map/all_gather | solution.py:273
  312.3 96.5 %copy-start.76 = (f32[768]{0:T(1024)}, f32[768]{0:T(1024)S(1)}, u32[]{:S(2)}) copy-start(f32[768]{0:T(1024)S(1)} %convert_element_type.358) | copy-start | bytes 9220
  323.2 62.8 %copy-start.66 = (f32[8,12,1,180]{3,1,2,0:T(8,128)}, f32[8,12,1,180]{3,1,2,0:T(8,128)S(1)}, u32[]{:S(2)}) copy-start(f32[8,12,1,180]{3,1,2,0:T(8,128)S(1)} %get-tuple-element.137) | copy-start | bytes 207364
  323.2 62.8 %copy-start.68 = (f32[8,12,1,180]{3,1,2,0:T(8,128)}, f32[8,12,1,180]{3,1,2,0:T(8,128)S(1)}, u32[]{:S(2)}) copy-start(f32[8,12,1,180]{3,1,2,0:T(8,128)S(1)} %get-tuple-element.138) | copy-start | bytes 207364
  535.7 25.3 %copy-start.105 = (bf16[768,768]{1,0:T(8,128)(2,1)S(1)}, bf16[768,768]{1,0:T(8,128)(2,1)}, u32[]{:S(2)}) copy-start(bf16[768,768]{1,0:T(8,128)(2,1)} %param.34) | copy-start | bytes 3538948
  779.9 149.3 %collective-permute-start.1 = (bf16[12,768]{1,0:T(8,128)(2,1)S(1)}, bf16[12,768]{1,0:T(8,128)(2,1)S(1)}, u32[]{:S(2)}, u32[]{:S(2)}) collective-permute-start(bf16[12,768]{1,0:T(8,128)(2,1)S(1)} %slice.195), channel_id=1, source_target_pairs={{0,1},{1,2},{2,3},{4,5},{5,6},{6,7},{8,9},{9,10},{10,11},{12,13},{... | collective-permute-start | bytes 55304
  927.1 21.9 %copy-start.53 = (f32[2700]{0:T(1024)S(1)}, f32[2700]{0:T(1024)}, u32[]{:S(2)}) copy-start(f32[2700]{0:T(1024)} %copy-done.52) | copy-start | bytes 32404
  927.1 21.9 %copy-start.65 = (f32[2700]{0:T(1024)S(1)}, f32[2700]{0:T(1024)}, u32[]{:S(2)}) copy-start(f32[2700]{0:T(1024)} %copy-done.64) | copy-start | bytes 32404
  927.1 21.9 %copy-start.77 = (f32[768]{0:T(1024)S(1)}, f32[768]{0:T(1024)}, u32[]{:S(2)}) copy-start(f32[768]{0:T(1024)} %copy-done.76) | copy-start | bytes 9220
  927.9 29.8 %collective-permute-start = (bf16[12,768]{1,0:T(8,128)(2,1)S(1)}, bf16[12,768]{1,0:T(8,128)(2,1)S(1)}, u32[]{:S(2)}, u32[]{:S(2)}) collective-permute-start(bf16[12,768]{1,0:T(8,128)(2,1)S(1)} %slice.194), channel_id=1, source_target_pairs={{0,1},{1,2},{2,3},{4,5},{5,6},{6,7},{8,9},{9,10},{10,11},{12,13},{... | collective-permute-start | bytes 55304
  949.0 28.4 %copy-start.13 = (bf16[540,768]{1,0:T(8,128)(2,1)S(1)}, bf16[540,768]{1,0:T(8,128)(2,1)}, u32[]{:S(2)}) copy-start(bf16[540,768]{1,0:T(8,128)(2,1)} %copy-done.12) | copy-start | bytes 2488324
  949.0 28.4 %copy-start.70 = (f32[2700]{0:T(1024)S(1)}, f32[2700]{0:T(1024)}, u32[]{:S(2)}) copy-start(f32[2700]{0:T(1024)} %maximum_reduce_fusion) | copy-start | bytes 32404
  949.0 28.3 %copy-start.81 = (pred[2700]{0:T(1024)(128)(4,1)S(1)}, pred[2700]{0:T(1024)(128)(4,1)}, u32[]{:S(2)}) copy-start(pred[2700]{0:T(1024)(128)(4,1)} %copy-done.80) | copy-start | bytes 8104
  949.0 28.3 %copy-start.82 = (f32[768]{0:T(1024)S(1)}, f32[768]{0:T(1024)}, u32[]{:S(2)}) copy-start(f32[768]{0:T(1024)} %convert_element_type.365) | copy-start | bytes 9220
  977.3 17.2 %copy-start.59 = (f32[8,6,1,90]{3,0,2,1:T(8,128)S(1)}, f32[8,6,1,90]{3,0,2,1:T(8,128)}, u32[]{:S(2)}) copy-start(f32[8,6,1,90]{3,0,2,1:T(8,128)} %copy-done.58) | copy-start | bytes 51844
  977.4 17.2 %copy-start.61 = (f32[8,6,1,90]{3,0,2,1:T(8,128)S(1)}, f32[8,6,1,90]{3,0,2,1:T(8,128)}, u32[]{:S(2)}) copy-start(f32[8,6,1,90]{3,0,2,1:T(8,128)} %copy-done.60) | copy-start | bytes 51844
  999.3 35.9 %all-to-all-start.5 = ((bf16[8,6,1,6,2,768]{5,4,3,2,1,0:T(2,128)(2,1)}), bf16[8,6,1,6,2,768]{5,4,3,2,1,0:T(2,128)(2,1)S(1)}, u32[]{:S(2)}, u32[]{:S(2)}) async-start(bf16[8,6,1,6,2,768]{5,4,3,2,1,0:T(2,128)(2,1)} %copy.291), calls=%async_computation.5 | async-start | bytes 1769472 | tf_op jit(solution)/shard_map/all_to_all | solution.py:324
  1028.6 12.6 copy-start.47
  1028.6 12.6 copy-start.49
  1035.2 86.0 %all-to-all-start.4 = ((bf16[8,12,1,12,2,768]{5,4,3,2,1,0:T(2,128)(2,1)}), bf16[8,12,1,12,2,768]{5,4,3,2,1,0:T(2,128)(2,1)}, u32[]{:S(2)}, u32[]{:S(2)}) async-start(bf16[8,12,1,12,2,768]{5,4,3,2,1,0:T(2,128)(2,1)} %copy.287), calls=%async_computation.4 | async-start | bytes 7077888 | tf_op jit(solution)/shard_map/all_to_all | solution.py:323
  1041.2 80.0 %copy-start.34 = (f32[96,1,90,2]{2,0,3,1:T(8,128)S(1)}, f32[96,1,90,2]{2,0,3,1:T(8,128)}, u32[]{:S(2)}) copy-start(f32[96,1,90,2]{2,0,3,1:T(8,128)} %copy-done.33) | copy-start | bytes 207364
  1041.2 80.0 %copy-start.36 = (f32[96,1,90,2]{2,0,3,1:T(8,128)S(1)}, f32[96,1,90,2]{2,0,3,1:T(8,128)}, u32[]{:S(2)}) copy-start(f32[96,1,90,2]{2,0,3,1:T(8,128)} %copy-done.35) | copy-start | bytes 207364
  1197.0 24.5 %slice-start.2 = ((s8[8650752]{0:T(1024)(128)(4,1)}), s8[262144]{0:T(1024)(128)(4,1)S(1)}, s32[]{:S(2)}) async-start(s8[8650752]{0:T(1024)(128)(4,1)} %bitcast.451), calls=%async_computation.14 | async-start | bytes 524288
  1197.0 64.6 %all-to-all-start.7 = ((bf16[8,6,1,6,2,768]{5,4,3,1,2,0:T(2,128)(2,1)}), bf16[8,6,1,6,2,768]{5,4,3,1,2,0:T(2,128)(2,1)S(1)}, u32[]{:S(2)}, u32[]{:S(2)}) async-start(bf16[8,6,1,6,2,768]{5,4,3,1,2,0:T(2,128)(2,1)} %bitcast.139), calls=%async_computation.7 | async-start | bytes 1769472 | tf_op jit(solution)/shard_map/all_to_all | solution.py:364
  1201.2 20.3 %slice-start.3 = ((s8[8650752]{0:T(1024)(128)(4,1)}), s8[4194304]{0:T(1024)(128)(4,1)S(1)}, s32[]{:S(2)}) async-start(s8[8650752]{0:T(1024)(128)(4,1)} %bitcast.451), calls=%async_computation.15 | async-start | bytes 8388608
  1201.2 20.3 %slice-start.4 = ((s8[8650752]{0:T(1024)(128)(4,1)}), s8[4194304]{0:T(1024)(128)(4,1)S(1)}, s32[]{:S(2)}) async-start(s8[8650752]{0:T(1024)(128)(4,1)} %bitcast.451), calls=%async_computation.16 | async-start | bytes 8388608
  1261.6 26.2 %copy-start.21 = (bf16[8,6,1,6,2,768]{5,4,3,1,2,0:T(2,128)(2,1)}, bf16[8,6,1,6,2,768]{5,4,3,1,2,0:T(2,128)(2,1)S(1)}, u32[]{:S(2)}) copy-start(bf16[8,6,1,6,2,768]{5,4,3,1,2,0:T(2,128)(2,1)S(1)} %all-to-all-done.7) | copy-start | bytes 2654212
  1261.6 151.4 %all-to-all-start.6 = ((bf16[8,12,1,12,2,768]{5,4,3,2,1,0:T(2,128)(2,1)}), bf16[8,12,1,12,2,768]{5,4,3,2,1,0:T(2,128)(2,1)}, u32[]{:S(2)}, u32[]{:S(2)}) async-start(bf16[8,12,1,12,2,768]{5,4,3,2,1,0:T(2,128)(2,1)} %bitcast.454), calls=%async_computation.6 | async-start | bytes 7077888 | tf_op jit(solution)/shard_map/all_to_all | solution.py:363
  1267.6 20.3 %copy-start.95 = (f32[768]{0:T(1024)S(1)}, f32[768]{0:T(1024)}, u32[]{:S(2)}) copy-start(f32[768]{0:T(1024)} %get-tuple-element.173) | copy-start | bytes 9220
  1267.6 275.0 %all-reduce.12.cloned.1.call-start = ((), (), s32[]{:S(2)}) async-start(), calls=%async_computation.11 | async-start | bytes 9437184 | tf_op jit(solution)/shard_map/psum | solution.py:389
  1287.9 353.6 %all-reduce.10.cloned.1.call-start = ((), (), s32[]{:S(2)}) async-start(), calls=%async_computation.10 | async-start | bytes 2359296 | tf_op jit(solution)/shard_map/psum | solution.py:390
  1379.6 14.1 copy-start.18
  1454.9 14.0 copy-start.83
  1454.9 14.0 copy-start.84
  1454.9 14.0 copy-start.85
  1458.7 191.2 %copy-start.1 = (bf16[768,768]{1,0:T(8,128)(2,1)S(1)}, bf16[768,768]{1,0:T(8,128)(2,1)}, u32[]{:S(2)}) copy-start(bf16[768,768]{1,0:T(8,128)(2,1)} %param.32) | copy-start | bytes 3538948
  1542.6 105.9 %copy-start.28 = (f32[768,768]{1,0:T(8,128)S(1)}, f32[768,768]{1,0:T(8,128)}, u32[]{:S(2)}) copy-start(f32[768,768]{1,0:T(8,128)} %get-tuple-element.191) | copy-start | bytes 7077892
  (61 other events, 384.3 us)
Sparse Core Ops, SparseCore 0:
  23.2 107.6 all-gather.6
  415.1 104.1 all-gather.4
  1288.0 216.3 all-reduce.11
  1511.0 130.4 all-reduce.9
where the time goes:
time: 1670 us; the launch traced here: 1660 us
  blocking collectives  447 us (27%)
  local copies, waits for them, and re-layouts  427 us (26%)
  waiting for transfers between devices  352 us (21%)
  matrix products  263 us (16%)
  other arithmetic  103 us (6%)
  starting transfers between devices  48.7 us (3%)
    unnamed x2, blocking collectives  290 us
    all_to_all x2, waiting for transfers between devices, on_device(): lax.all_to_all(sends[0], 'wide', split_axis=0, concat_axis=1, tiled=True)  127 us
    unnamed x235, local copies, waits for them, and re-layouts  117 us
    psum x1, waiting for transfers between devices, on_device(): lax.psum((grad_weight_one, grad_shift_one, grad_weight_two, grad_shift_tw...  98.9 us
    psum x1, blocking collectives, on_device(): mlp_sums = lax.psum((grad_expand, grad_expand_b, grad_reduce), 'wide')  84.1 us
    all_gather x1, waiting for transfers between devices, on_device(): full_inputs = lax.all_gather(input_rows, 'narrow', axis=0, tiled=True)  80.8 us
    psum x1, blocking collectives, on_device(): lax.psum((grad_weight_one, grad_shift_one, grad_weight_two, grad_shift_tw...  73.7 us
    all_to_all x2, waiting for transfers between devices, on_device(): lax.all_to_all(outgoing[0], 'wide', split_axis=0, concat_axis=1, tiled=True)  45 us
  transfers between devices with their start and end apart: 14, of which 5 were waited for; matrix products, arithmetic and copies ran while one was open for 40% of the time, Pallas kernels for 0%

commit v1 on v0

--- a/solution.py
+++ b/solution.py
@@ -1,8 +1,12 @@
+import functools
 import math
 
 import jax
 import jax.numpy as jnp
+import numpy as np
 from jax import lax
+from jax.experimental import pallas as pl
+from jax.experimental.pallas import tpu as pltpu
 from jax.sharding import PartitionSpec as P
 
 NBL = 8
@@ -106,7 +110,7 @@
     return folded.transpose(0, 2, 1, 3).reshape(2, BS, NBL * BS)
 
 
-def on_device(
+def general_device(
     field_a,
     field_b,
     cotangent_a,
@@ -421,6 +425,830 @@
     )
 
 
+F32 = jnp.float32
+BF16 = jnp.bfloat16
+MIB = 1024 * 1024
+PAD = 8
+LANES = 128
+
+
+def halves(value):
+    high = lax.reduce_precision(value, 8, 7)
+    return high.astype(BF16), (value - high).astype(BF16)
+
+
+def round_up(value, unit):
+    return -(-value // unit) * unit
+
+
+def call(kernel, grid, in_specs, out_specs, out_shape, scratch=(), limit=56, after=0):
+    first = len(in_specs)
+
+    def body(*refs):
+        kernel(*refs[:first], *refs[first + after :])
+
+    return pl.pallas_call(
+        body,
+        grid=grid,
+        in_specs=in_specs + [pl.BlockSpec(memory_space=pl.ANY)] * after,
+        out_specs=out_specs,
+        out_shape=out_shape,
+        scratch_shapes=list(scratch),
+        compiler_params=pltpu.CompilerParams(vmem_limit_bytes=limit * MIB),
+    )
+
+
+def whole(array):
+    zeros = (0,) * array.ndim
+    return pl.BlockSpec(array.shape, lambda *_: zeros)
+
+
+def dot(left, right):
+    return jnp.dot(left, right, preferred_element_type=F32)
+
+
+def dot_t(left, right):
+    return lax.dot_general(left, right, (((1,), (1,)), ((), ())), preferred_element_type=F32)
+
+
+def column_tables(columns, spread, width, repeat, tokens):
+    freqs = columns // 2 + 1
+    freq = np.arange(width * spread)
+    valid = (freq < freqs).astype(np.float64)
+    angle = 2.0 * np.pi * (np.outer(freq, np.arange(columns)) % columns) / columns
+    scale = valid[:, None] / math.sqrt(columns)
+    weight = np.where((freq == 0) | (2 * freq == columns), 1.0, 2.0)[:, None]
+    parts = np.stack([np.cos(angle) * scale, -np.sin(angle) * scale], axis=1)
+    parts = parts.reshape(width, spread, 2, columns).transpose(0, 2, 1, 3)
+    heavy = np.broadcast_to(weight.reshape(width, 1, spread, 1), parts.shape)
+    forward = np.zeros((width, repeat, 2, spread, tokens))
+    inverse = np.zeros((width, repeat, 2, spread, tokens))
+    for index in range(repeat):
+        span = slice(index * columns, (index + 1) * columns)
+        forward[:, index, :, :, span] = parts
+        inverse[:, index, :, :, span] = parts * heavy
+    return forward.reshape(-1, tokens), inverse.reshape(-1, tokens)
+
+
+def row_table(height, line, valid, padded):
+    angle = phase(jnp.arange(padded, dtype=jnp.int32)[:, None], line[None, :], height)
+    inside = (jnp.arange(padded) < height).astype(F32)[:, None]
+    scale = inside * valid[None, :] / math.sqrt(height)
+    cosine = jnp.cos(angle) * scale
+    sine = jnp.sin(angle) * scale
+    upper = jnp.stack([cosine, sine], axis=-1)
+    lower = jnp.stack([-sine, cosine], axis=-1)
+    return jnp.stack([upper, lower]).reshape(2 * padded, -1)
+
+
+def half_weight(weight, half, blocks):
+    side = blocks * BS
+    pieces = weight[:, :, half * side : (half + 1) * side].reshape(2, BS, blocks, BS)
+    eye = jnp.eye(blocks, dtype=weight.dtype)
+    wide = pieces.transpose(0, 2, 1, 3)[:, :, :, None, :] * eye[None, :, None, :, None]
+    wide = wide.reshape(2, side, side)
+    return jnp.concatenate(
+        [
+            jnp.concatenate([wide[0], wide[1]], axis=1),
+            jnp.concatenate([-wide[1], wide[0]], axis=1),
+        ],
+        axis=0,
+    )
+
+
+def layer_norm(value):
+    mean = jnp.mean(value, axis=1, keepdims=True)
+    centred = value - mean
+    scale = lax.rsqrt(jnp.mean(centred * centred, axis=1, keepdims=True) + EPSILON)
+    return centred * scale, scale
+
+
+def layer_norm_back(grad, gain, standard, scale):
+    scaled = grad * gain
+    return scale * (
+        scaled
+        - jnp.mean(scaled, axis=1, keepdims=True)
+        - standard * jnp.mean(scaled * standard, axis=1, keepdims=True)
+    )
+
+
+def row_sums(*values):
+    rows = [jnp.sum(value, axis=0, keepdims=True) for value in values]
+    blank = jnp.zeros((PAD - len(rows), rows[0].shape[1]), F32)
+    return jnp.concatenate(rows + [blank], axis=0)
+
+
+class Plan:
+    def __init__(self, width, rows_a, columns_a, rows_b, columns_b, local):
+        self.width = width
+        self.rows_a, self.columns_a = rows_a, columns_a
+        self.rows_b, self.columns_b = rows_b, columns_b
+        self.local = local
+        self.half = local // 2
+        self.spread_a = -(-(columns_a // 2 + 1) // width)
+        self.spread_b = -(-(columns_b // 2 + 1) // width)
+        self.piece = 2 * self.spread_a
+        self.units = rows_a + rows_b // 2
+        self.tokens = round_up(columns_a, 8)
+        self.pad_a = round_up(H_A, 16)
+        self.pad_b = round_up(H_B, 16)
+        self.points_a = self.spread_a * self.pad_a
+        self.points = self.points_a + self.spread_b * self.pad_b
+
+    def fits(self):
+        return (
+            self.columns_a == 2 * self.columns_b
+            and self.spread_a == 2 * self.spread_b
+            and self.piece % 8 == 0
+            and self.rows_b % 2 == 0
+            and self.half % 128 == 0
+            and self.half % BS == 0
+        )
+
+    def spec_a(self):
+        last = self.rows_a - 1
+        return pl.BlockSpec(
+            (1, self.columns_a, self.local), lambda i: (jnp.minimum(i, last), 0, 0)
+        )
+
+    def spec_b(self):
+        first = self.rows_a
+        return pl.BlockSpec(
+            (2, self.columns_b, self.local), lambda i: (jnp.maximum(i - first, 0), 0, 0)
+        )
+
+    def unit(self, last=None):
+        return pl.BlockSpec((1, self.tokens, last or self.local), lambda i: (i, 0, 0))
+
+    def sends(self):
+        return pl.BlockSpec((self.width, 1, self.piece, self.half), lambda i: (0, i, 0, 0))
+
+    def table(self, shape):
+        first = self.rows_a
+        zeros = (0,) * len(shape)
+        return pl.BlockSpec((1,) + shape, lambda i: ((i >= first).astype(jnp.int32),) + zeros)
+
+    def exchange_shape(self):
+        return jax.ShapeDtypeStruct((self.width, self.units, self.piece, self.half), BF16)
+
+    def units_shape(self, kind):
+        return jax.ShapeDtypeStruct((self.units, self.tokens, self.local), kind)
+
+    def load(self, step, a_ref, b_ref, scratch):
+        @pl.when(step == 0)
+        def _():
+            scratch[...] = jnp.zeros_like(scratch)
+
+        @pl.when(step < self.rows_a)
+        def _():
+            scratch[: self.columns_a] = a_ref[0].astype(F32)
+
+        @pl.when(step >= self.rows_a)
+        def _():
+            scratch[: self.columns_b] = b_ref[0].astype(F32)
+            scratch[self.columns_b : self.columns_a] = b_ref[1].astype(F32)
+
+        return scratch[...]
+
+    def outs(self):
+        last, first = self.rows_a - 1, self.rows_a
+        return [
+            pl.BlockSpec(
+                (1, 1, self.columns_a, self.local), lambda i: (jnp.minimum(i, last), 0, 0, 0)
+            ),
+            pl.BlockSpec(
+                (2, 1, self.columns_b, self.local), lambda i: (jnp.maximum(i - first, 0), 0, 0, 0)
+            ),
+        ]
+
+    def store(self, step, value, a_ref, b_ref):
+        @pl.when(step < self.rows_a)
+        def _():
+            a_ref[0, 0] = value[: self.columns_a].astype(a_ref.dtype)
+
+        @pl.when(step >= self.rows_a)
+        def _():
+            b_ref[0, 0] = value[: self.columns_b].astype(b_ref.dtype)
+            b_ref[1, 0] = value[self.columns_b : self.columns_a].astype(b_ref.dtype)
+
+    def put_sends(self, product, refs):
+        for index, ref in enumerate(refs):
+            lanes = product[:, index * self.half : (index + 1) * self.half]
+            ref[:, 0] = lanes.reshape(self.width, self.piece, self.half).astype(BF16)
+
+    def get_sends(self, refs):
+        depth = self.width * self.piece
+        return [ref[:, 0].astype(F32).reshape(depth, self.half).astype(BF16) for ref in refs]
+
+    def valid_rows(self, step, counts, shape):
+        token = lax.broadcasted_iota(jnp.int32, shape, 0)
+        second = (token >= self.columns_b).astype(jnp.int32)
+        in_a = (step < counts[0]) & (step < self.rows_a)
+        row_b = 2 * (step - self.rows_a) + second
+        in_b = (row_b < counts[1]) & (step >= self.rows_a)
+        return (in_a | in_b) & (token < self.columns_a)
+
+
+def first_kernel(plan, xa, xb, gain, bias, table, out0, out1, scratch):
+    step = pl.program_id(0)
+    value = plan.load(step, xa, xb, scratch)
+    standard, _ = layer_norm(value)
+    high, low = halves(standard * gain[...] + bias[...])
+    spectrum = dot(table[0, 0], high) + (dot(table[0, 0], low) + dot(table[0, 1], high))
+    plan.put_sends(spectrum, (out0, out1))
+
+
+def cotangent_kernel(plan, counts, ca, cb, out, sums, scratch):
+    step = pl.program_id(0)
+    value = plan.load(step, ca, cb, scratch)
+    value = jnp.where(plan.valid_rows(step, counts, value.shape), value, 0.0)
+    out[0] = value.astype(BF16)
+
+    @pl.when(step == 0)
+    def _():
+        sums[...] = jnp.zeros_like(sums)
+
+    sums[...] += row_sums(value)
+
+
+def middle_kernel(plan, xa, xb, got0, got1, gain, bias, gain2, bias2, table, mid, out, scratch):
+    step = pl.program_id(0)
+    value = plan.load(step, xa, xb, scratch)
+    standard, _ = layer_norm(value)
+    back = jnp.concatenate([dot(table[0], part) for part in plan.get_sends((got0, got1))], axis=1)
+    middle = value + standard * gain[...] + bias[...] + back
+    mid[0] = middle
+    standard2, _ = layer_norm(middle)
+    out[0] = (standard2 * gain2[...] + bias2[...]).astype(BF16)
+
+
+def middle_back_kernel(plan, dv, mid, cot, gain2, table, dmid, out0, out1, sums):
+    step = pl.program_id(0)
+    grad = dv[0].astype(F32)
+    standard, scale = layer_norm(mid[0])
+    total = cot[0].astype(F32) + layer_norm_back(grad, gain2[...], standard, scale)
+    dmid[0] = total
+    plan.put_sends(dot(table[0], total.astype(BF16)), (out0, out1))
+
+    @pl.when(step == 0)
+    def _():
+        sums[...] = jnp.zeros_like(sums)
+
+    sums[...] += row_sums(grad * standard, grad)
+
+
+def mixed_kernel(
+    plan, counts, hidden, weight, bias, mid, dmid, xa, xb, outa, outb, sums, scratch
+):
+    step = pl.program_id(0)
+    standard, _ = layer_norm(plan.load(step, xa, xb, scratch))
+    grad = dmid[0]
+
+    @pl.when(step == 0)
+    def _():
+        sums[...] = jnp.zeros_like(sums)
+
+    sums[...] += row_sums(grad * standard, grad)
+    value = mid[0] + dot(hidden[0], weight[...]) + bias[...]
+    value = jnp.where(plan.valid_rows(step, counts, value.shape), value, 0.0)
+    plan.store(step, value, outa, outb)
+
+
+def last_kernel(plan, xa, xb, got0, got1, dmid, gain, table, outa, outb, scratch):
+    step = pl.program_id(0)
+    value = plan.load(step, xa, xb, scratch)
+    standard, scale = layer_norm(value)
+    back = jnp.concatenate([dot(table[0], part) for part in plan.get_sends((got0, got1))], axis=1)
+    grad = back + dmid[0]
+    total = dmid[0] + layer_norm_back(grad, gain[...], standard, scale)
+    plan.store(step, total, outa, outb)
+
+
+def unpack(plan, got, part_a, part_b):
+    rows_a = plan.rows_a * plan.piece
+    rows_b = (plan.units - plan.rows_a) * plan.piece
+    for j in range(plan.width):
+        value = got[j].astype(F32)
+        for part, rows, piece in (
+            (part_a, rows_a, value[: plan.rows_a]),
+            (part_b, rows_b, value[plan.rows_a :]),
+        ):
+            for g in range(plan.half // LANES):
+                lanes = piece[:, :, g * LANES : (g + 1) * LANES]
+                part[g, j * rows : (j + 1) * rows] = lanes.reshape(rows, LANES)
+
+
+def repack(plan, part_a, part_b, out):
+    rows_a = plan.rows_a * plan.piece
+    rows_b = (plan.units - plan.rows_a) * plan.piece
+    for j in range(plan.width):
+        for part, rows, first, last in (
+            (part_a, rows_a, 0, plan.rows_a),
+            (part_b, rows_b, plan.rows_a, plan.units),
+        ):
+            for g in range(plan.half // LANES):
+                out[j, first:last, :, g * LANES : (g + 1) * LANES] = (
+                    part[g, j * rows : (j + 1) * rows]
+                    .reshape(last - first, plan.piece, LANES)
+                    .astype(BF16)
+                )
+
+
+def grids(plan):
+    return (
+        (plan.spread_a, plan.pad_a, plan.width * 2 * plan.rows_a, 0, 0),
+        (plan.spread_b, plan.pad_b, plan.width * 2 * plan.rows_b, plan.points_a, 1),
+    )
+
+
+def to_points(plan, parts, tables, out, first=None):
+    for spread, pad, depth, base, which in grids(plan):
+        for f in range(spread):
+            lanes = [
+                parts[which][g, pl.ds(f, depth, stride=spread), :].astype(BF16)
+                for g in range(plan.half // LANES)
+            ]
+            column = jnp.concatenate(lanes, axis=1)
+            product = dot(tables[which][0], column)
+            if first is not None:
+                product += dot(tables[which][1], column)
+                if f == 0:
+                    first[which : which + 1] = product[:1]
+            out[base + f * pad : base + (f + 1) * pad, :] = jnp.concatenate(
+                [product[:pad], product[pad:]], axis=1
+            ).astype(out.dtype)
+
+
+def from_points(plan, points, tables, parts):
+    for spread, pad, depth, base, which in grids(plan):
+        for f in range(spread):
+            value = points[base + f * pad : base + (f + 1) * pad, :]
+            column = jnp.concatenate([value[:, : plan.half], value[:, plan.half :]], axis=0)
+            product = dot(tables[which][...], column)
+            for g in range(plan.half // LANES):
+                parts[which][g, pl.ds(f, depth, stride=spread), :] = product[
+                    :, g * LANES : (g + 1) * LANES
+                ]
+
+
+def spectral_kernel(
+    plan, steps, got, ta, tb, tat, tbt, w1, b1, w2, b2, out, zed, act, slope1, slope2, dc, pa, pb, shrunk
+):
+    unpack(plan, got, pa, pb)
+    dc[...] = jnp.zeros_like(dc)
+    to_points(plan, (pa, pb), (ta, tb), zed, dc)
+    size = plan.points // steps
+
+    def body(index, carry):
+        rows = pl.ds(pl.multiple_of(index * size, size), size)
+        pre_one = dot(zed[rows, :], w1[...]) + b1[...]
+        cdf = 0.5 * (1.0 + lax.erf(pre_one * ROOT_HALF))
+        hidden = (pre_one * cdf).astype(BF16)
+        act[rows, :] = hidden
+        slope1[rows, :] = (
+            cdf + pre_one * jnp.exp(-0.5 * pre_one * pre_one) * (1.0 / ROOT_TWO_PI)
+        ).astype(BF16)
+        pre_two = dot(hidden, w2[...]) + b2[...]
+        bent = jnp.tanh(pre_two * (1.0 / SHRINK))
+        shrunk[rows, :] = (pre_two - SHRINK * bent).astype(BF16)
+        slope2[rows, :] = (bent * bent).astype(BF16)
+        return carry
+
+    lax.fori_loop(0, steps, body, 0)
+    from_points(plan, shrunk, (tat, tbt), (pa, pb))
+    repack(plan, pa, pb, out)
+
+
+def spectral_back_kernel(
+    plan, steps, got, ta, tb, tat, tbt, w1, w2, slope1, slope2, zed, out, grad1, grad2, sums, pa, pb, work
+):
+    unpack(plan, got, pa, pb)
+    to_points(plan, (pa, pb), (ta, tb), work)
+    size = plan.points // steps
+    sums[...] = jnp.zeros_like(sums)
+
+    def body(index, carry):
+        rows = pl.ds(pl.multiple_of(index * size, size), size)
+        two = (work[rows, :].astype(F32) * slope2[rows, :].astype(F32)).astype(BF16)
+        grad2[rows, :] = two
+        one = (dot_t(two, w2[...]) * slope1[rows, :].astype(F32)).astype(BF16)
+        grad1[rows, :] = one
+        grad = dot_t(one, w1[...])
+        work[rows, :] = grad.astype(BF16)
+        sums[...] += row_sums(one.astype(F32), two.astype(F32), grad * zed[rows, :].astype(F32))
+        return carry
+
+    lax.fori_loop(0, steps, body, 0)
+    for which, start in enumerate((0, plan.points_a)):
+        sums[3 + which : 4 + which] = work[start : start + 16, :].astype(F32)[:1]
+        sums[5 + which : 6 + which] = zed[start : start + 16, :].astype(F32)[:1]
+    from_points(plan, work, (tat, tbt), (pa, pb))
+    repack(plan, pa, pb, out)
+
+
+def pack_kernel(plan, place, products, backs, dcs, norm2, cot, norm1, shift, gain, bias, out):
+    half, blocks = plan.half, plan.half // BS
+    out[...] = jnp.zeros_like(out)
+    for kind in range(2):
+        for h in range(2):
+            product = products[kind][h]
+            for b in range(blocks):
+                rows = slice(b * BS, (b + 1) * BS)
+                late = slice(half + b * BS, half + (b + 1) * BS)
+                real = product[rows, rows] + product[late, late]
+                imag = product[rows, late] - product[late, rows]
+                lanes = slice(h * half + b * BS, h * half + (b + 1) * BS)
+                out[2 * kind * BS : (2 * kind + 1) * BS, lanes] = real
+                out[(2 * kind + 1) * BS : (2 * kind + 2) * BS, lanes] = imag
+    row = 4 * BS
+    for kind in range(2):
+        for part in range(2):
+            for h in range(2):
+                out[row : row + 1, h * half : (h + 1) * half] = backs[h][
+                    kind : kind + 1, part * half : (part + 1) * half
+                ]
+            row += 1
+    out[row : row + 2] = norm2[0:2]
+    out[row + 2 : row + 3] = cot[0:1]
+    row += 3
+    first = jnp.where(place[0] == 0, 1.0, 0.0)
+    roots = [math.sqrt(H_A * plan.columns_a), math.sqrt(H_B * plan.columns_b)]
+    for h in range(2):
+        lanes = slice(h * half, (h + 1) * half)
+        total = backs[h][2:3, :half] + backs[h][2:3, half:]
+        plain = norm1[1:2, lanes]
+        for which in range(2):
+            grad = backs[h][3 + which : 4 + which, :half] * first
+            exact = dcs[h][which : which + 1] - bias[:, lanes] * roots[which]
+            total += grad * (exact - backs[h][5 + which : 6 + which, :half])
+            plain += grad * roots[which]
+        out[row : row + 1, lanes] = norm1[0:1, lanes] + total / gain[:, lanes]
+        out[row + 1 : row + 2, lanes] = plain
+    row += 2
+    for n in range(4):
+        out[row + n : row + n + 1] = shift[pl.ds(n ^ place[1], 1), :]
+
+
+def swap(value, axis, distance):
+    size = lax.axis_size(axis)
+    return lax.ppermute(value, axis, [(i, i ^ distance) for i in range(size)])
+
+
+def halve(value, axis, distance):
+    size = value.shape[0] // 2
+    bit = (lax.axis_index(axis) // distance) % 2
+    keep = lax.dynamic_slice_in_dim(value, bit * size, size)
+    send = lax.dynamic_slice_in_dim(value, (1 - bit) * size, size)
+    return keep, send
+
+
+def join(value, axis, distance):
+    other = swap(value, axis, distance)
+    bit = (lax.axis_index(axis) // distance) % 2
+    return jnp.where(
+        bit == 0, jnp.concatenate([value, other]), jnp.concatenate([other, value])
+    )
+
+
+def add_up(value, links, kind):
+    for axis, distance in links:
+        keep, send = halve(value, axis, distance)
+        value = keep + swap(send.astype(kind), axis, distance).astype(F32)
+    value = value.astype(kind)
+    for axis, distance in reversed(links):
+        value = join(value, axis, distance)
+    return value
+
+
+def powers(size):
+    return [1 << k for k in range(size.bit_length() - 1)]
+
+
+def fast_device(
+    plan,
+    field_a,
+    field_b,
+    cotangent_a,
+    cotangent_b,
+    offsets_a,
+    offsets_b,
+    first_gain,
+    first_bias,
+    inner_weight,
+    inner_bias,
+    outer_weight,
+    outer_bias,
+    second_gain,
+    second_norm_bias,
+    expand_weight,
+    expand_bias,
+    reduce_weight,
+    reduce_bias,
+):
+    width, local, half = plan.width, plan.local, plan.half
+    blocks = half // BS
+    tokens, units = plan.tokens, plan.units
+    myself = lax.axis_index("wide")
+    xa = field_a.reshape(plan.rows_a, plan.columns_a, local)
+    xb = field_b.reshape(plan.rows_b, plan.columns_b, local)
+    ca = cotangent_a.reshape(plan.rows_a, plan.columns_a, local)
+    cb = cotangent_b.reshape(plan.rows_b, plan.columns_b, local)
+    gain1 = first_gain.astype(F32)[None]
+    bias1 = first_bias.astype(F32)[None]
+    gain2 = second_gain.astype(F32)[None]
+    bias2 = second_norm_bias.astype(F32)[None]
+    tables = [
+        column_tables(plan.columns_a, plan.spread_a, width, 1, tokens),
+        column_tables(plan.columns_b, plan.spread_b, width, 2, tokens),
+    ]
+    forward = np.stack([pair[0] for pair in tables])
+    inverse = np.stack([pair[1] for pair in tables])
+    depth = width * plan.piece
+    fwd_w_t = jnp.asarray(forward.transpose(0, 2, 1).astype(jnp.bfloat16))
+    inv_w_t = jnp.asarray(inverse.astype(jnp.bfloat16))
+    inv_w = jnp.asarray(inverse.transpose(0, 2, 1).astype(jnp.bfloat16))
+    fine = forward.astype(jnp.bfloat16)
+    rest = (forward - fine.astype(np.float64)).astype(jnp.bfloat16)
+    fwd_w = jnp.asarray(np.stack([fine, rest], axis=1))
+    vector = pl.BlockSpec((1, local), lambda i: (0, 0))
+    sums_spec = pl.BlockSpec((PAD, local), lambda i: (0, 0))
+    sums_shape = jax.ShapeDtypeStruct((PAD, local), F32)
+    scratch = pltpu.VMEM((tokens, local), F32)
+    counts = jnp.stack(
+        [offsets_a[myself + 1] - offsets_a[myself], offsets_b[myself + 1] - offsets_b[myself]]
+    )
+    count_spec = pl.BlockSpec(memory_space=pltpu.SMEM)
+
+    def exchange(parts):
+        return [lax.all_to_all(part, "wide", 0, 0, tiled=True) for part in parts]
+
+    sends = call(
+        functools.partial(first_kernel, plan),
+        (units,),
+        [plan.spec_a(), plan.spec_b(), vector, vector, plan.table((2, depth, tokens))],
+        [plan.sends(), plan.sends()],
+        [plan.exchange_shape()] * 2,
+        [scratch],
+    )(xa, xb, gain1, bias1, fwd_w)
+    arrived = exchange(sends)
+
+    own = (expand_weight, expand_bias, reduce_weight)
+    far = tuple(swap(part, "narrow", 2) for part in own)
+    near = tuple(swap(part, "narrow", 1) for part in own)
+    cross = tuple(swap(part, "narrow", 1) for part in far)
+    chunks = (own, near, far, cross)
+    expand = jnp.concatenate([chunk[0] for chunk in chunks], axis=1)
+    expand_b = jnp.concatenate([chunk[1] for chunk in chunks]).astype(F32)
+    reduce = jnp.concatenate([chunk[2] for chunk in chunks], axis=0)
+
+    cot, cot_sums = call(
+        functools.partial(cotangent_kernel, plan),
+        (units,),
+        [count_spec, plan.spec_a(), plan.spec_b()],
+        [plan.unit(), sums_spec],
+        [plan.units_shape(BF16), sums_shape],
+        [scratch],
+    )(counts, ca, cb)
+    cot_rows = cot.reshape(units * tokens, local)
+    grad_hidden = dot_t(cot_rows, reduce).astype(BF16)
+
+    table = []
+    for offsets, height, rows, padded in (
+        (offsets_a, H_A, plan.rows_a, plan.pad_a),
+        (offsets_b, H_B, plan.rows_b, plan.pad_b),
+    ):
+        line, valid = row_slots(offsets, rows, width)
+        table.append(jnp.stack(halves(row_table(height, line, valid, padded))))
+    row_tables = (table[0], table[1], table[0][0].T, table[1][0].T)
+    ones = [half_weight(inner_weight, h, blocks) for h in range(2)]
+    twos = [half_weight(outer_weight, h, blocks) for h in range(2)]
+    shift1 = inner_bias.astype(F32).reshape(2, 2, half)
+    shift2 = outer_bias.astype(F32).reshape(2, 2, half)
+    points_shape = jax.ShapeDtypeStruct((plan.points, 2 * half), BF16)
+    points_spec = pl.BlockSpec((plan.points, 2 * half), lambda: (0, 0))
+    exchange_spec = pl.BlockSpec((width, units, plan.piece, half), lambda: (0, 0, 0, 0))
+    parts_scratch = [
+        pltpu.VMEM((half // LANES, width * plan.rows_a * plan.piece, LANES), F32),
+        pltpu.VMEM((half // LANES, width * (units - plan.rows_a) * plan.piece, LANES), F32),
+        pltpu.VMEM((plan.points, 2 * half), BF16),
+    ]
+    steps = 5 if plan.points % 80 == 0 else 1
+    kept, outgoing = [], []
+    ready = ((far[0], far[2], cot), (expand, reduce))
+    for h in range(2):
+        operands = (
+            arrived[h],
+            *row_tables,
+            ones[h],
+            shift1[:, h].reshape(1, 2 * half),
+            twos[h],
+            shift2[:, h].reshape(1, 2 * half),
+        )
+        got = call(
+            functools.partial(spectral_kernel, plan, steps),
+            (),
+            [whole(item) for item in operands],
+            [exchange_spec] + [points_spec] * 4 + [pl.BlockSpec((PAD, half), lambda: (0, 0))],
+            [plan.exchange_shape()] + [points_shape] * 4 + [jax.ShapeDtypeStruct((PAD, half), F32)],
+            parts_scratch,
+            after=len(ready[h]),
+        )(*operands, *ready[h])
+        outgoing.append(got[0])
+        kept.append(got[1:])
+    returned = exchange(outgoing)
+
+    middle, normed = call(
+        functools.partial(middle_kernel, plan),
+        (units,),
+        [plan.spec_a(), plan.spec_b(), plan.sends(), plan.sends()]
+        + [vector] * 4
+        + [plan.table((tokens, depth))],
+        [plan.unit(), plan.unit()],
+        [plan.units_shape(F32), plan.units_shape(BF16)],
+        [scratch],
+        after=1,
+    )(xa, xb, *returned, gain1, bias1, gain2, bias2, inv_w, grad_hidden)
+    rows = normed.reshape(units * tokens, local)
+    pre = dot(rows, expand) + expand_b
+    cdf = 0.5 * (1.0 + lax.erf(pre * ROOT_HALF))
+    hidden = (pre * cdf).astype(BF16)
+    slope = cdf + pre * jnp.exp(-0.5 * pre * pre) / ROOT_TWO_PI
+    grad_pre = (grad_hidden.astype(F32) * slope).astype(BF16)
+    grad_rows = dot_t(grad_pre, expand).astype(BF16)
+
+    dmid, send0, send1, norm2_sums = call(
+        functools.partial(middle_back_kernel, plan),
+        (units,),
+        [plan.unit(), plan.unit(), plan.unit(), vector, plan.table((depth, tokens))],
+        [plan.unit(), plan.sends(), plan.sends(), sums_spec],
+        [plan.units_shape(F32), plan.exchange_shape(), plan.exchange_shape(), sums_shape],
+    )(grad_rows.reshape(units, tokens, local), middle, cot, gain2, inv_w_t)
+    arrived = exchange((send0, send1))
+
+    hidden_units = hidden.reshape(units, tokens, -1)
+    hidden_size = hidden.shape[-1]
+    over_tokens = (((0,), (0,)), ((), ()))
+    grad_reduce = lax.dot_general(hidden, cot_rows, over_tokens, preferred_element_type=F32)
+    grad_expand = lax.dot_general(rows, grad_pre, over_tokens, preferred_element_type=F32)
+    grad_expand_b = jnp.sum(grad_pre.astype(F32), 0)
+    own_units = hidden_size // 4
+    shares = [
+        (
+            grad_reduce[k * own_units : (k + 1) * own_units],
+            grad_expand[:, k * own_units : (k + 1) * own_units],
+        )
+        for k in range(4)
+    ]
+
+    def add_from(target, source, distance):
+        return tuple(
+            t + swap(s.astype(BF16), "narrow", distance).astype(F32)
+            for t, s in zip(target, source, strict=True)
+        )
+
+    outgoing, products, backs = [], ([], []), []
+    for h in range(2):
+        zed, act, slope1, slope2, _ = kept[h]
+        operands = (
+            arrived[h],
+            *row_tables,
+            ones[h],
+            twos[h],
+            slope1,
+            slope2,
+            zed,
+        )
+        out, grad1, grad2, sums = call(
+            functools.partial(spectral_back_kernel, plan, steps),
+            (),
+            [whole(item) for item in operands],
+            [exchange_spec, points_spec, points_spec, pl.BlockSpec((PAD, 2 * half), lambda: (0, 0))],
+            [
+                plan.exchange_shape(),
+                points_shape,
+                points_shape,
+                jax.ShapeDtypeStruct((PAD, 2 * half), F32),
+            ],
+            parts_scratch,
+        )(*operands)
+        outgoing.append(out)
+        backs.append(sums)
+        for index, (left, right) in enumerate(((zed, grad1), (act, grad2))):
+            products[index].append(
+                lax.dot_general(left, right, over_tokens, preferred_element_type=F32)
+            )
+    returned = exchange(outgoing)
+    mixed_a, mixed_b, norm1_sums = call(
+        functools.partial(mixed_kernel, plan),
+        (units,),
+        [
+            count_spec,
+            plan.unit(hidden_size),
+            pl.BlockSpec((hidden_size, local), lambda i: (0, 0)),
+            vector,
+            plan.unit(),
+            plan.unit(),
+            plan.spec_a(),
+            plan.spec_b(),
+        ],
+        [*plan.outs(), sums_spec],
+        [
+            jax.ShapeDtypeStruct(field_a.shape, BF16),
+            jax.ShapeDtypeStruct(field_b.shape, BF16),
+            sums_shape,
+        ],
+        [scratch],
+        after=1,
+    )(counts, hidden_units, reduce, reduce_bias.astype(F32)[None], middle, dmid, xa, xb, grad1)
+    sum_own = add_from(shares[0], shares[1], 1)
+    sum_far = add_from(shares[2], shares[3], 1)
+    sum_own = add_from(sum_own, sum_far, 2)
+    wide_links = [("wide", d) for d in powers(width)]
+    mlp_sums = add_up(jnp.concatenate(sum_own), wide_links, BF16).astype(F32)
+
+
+    grad_a, grad_b = call(
+        functools.partial(last_kernel, plan),
+        (units,),
+        [plan.spec_a(), plan.spec_b(), plan.sends(), plan.sends(), plan.unit(), vector]
+        + [plan.table((tokens, depth))],
+        plan.outs(),
+        [
+            jax.ShapeDtypeStruct(field_a.shape, F32),
+            jax.ShapeDtypeStruct(field_b.shape, F32),
+        ],
+        [scratch],
+    )(xa, xb, *returned, dmid, gain1, fwd_w_t)
+
+    place = jnp.stack([myself, lax.axis_index("narrow")])
+    flat = (
+        *products[0],
+        *products[1],
+        *backs,
+        kept[0][4],
+        kept[1][4],
+        norm2_sums,
+        cot_sums,
+        norm1_sums,
+        grad_expand_b.reshape(4, -1),
+        gain1,
+        bias1,
+    )
+
+    def pack_body(place, *refs):
+        pack_kernel(
+            plan, place, (refs[0:2], refs[2:4]), refs[4:6], refs[6:8], *refs[8:]
+        )
+
+    links = [("narrow", d) for d in powers(4)] + wide_links
+    rows = round_up(4 * BS + 13, 8 << len(links))
+    pack = call(
+        pack_body,
+        (),
+        [count_spec] + [whole(item) for item in flat],
+        pl.BlockSpec((rows, local), lambda: (0, 0)),
+        jax.ShapeDtypeStruct((rows, local), F32),
+    )(place, *flat)
+    pack = add_up(pack, links, F32)
+    matrices = pack[: 4 * BS].reshape(2, 2, BS, local)
+    small = pack[4 * BS : 4 * BS + 13]
+    own_row = lax.dynamic_slice_in_dim(small, 9 + place[1], 1)[0]
+    own_depth = mlp_sums.shape[0] // 2
+    return (
+        mixed_a,
+        mixed_b,
+        grad_a,
+        grad_b,
+        small[7],
+        small[8],
+        matrices[0],
+        small[0:2],
+        matrices[1],
+        small[2:4],
+        small[4],
+        small[5],
+        mlp_sums[own_depth:],
+        own_row,
+        mlp_sums[:own_depth],
+        small[6],
+    )
+
+
+def choose(field_a, field_b, *rest):
+    plan = Plan(
+        lax.axis_size("wide"),
+        field_a.shape[0],
+        field_a.shape[2],
+        field_b.shape[0],
+        field_b.shape[2],
+        field_a.shape[3],
+    )
+    alone = field_a.shape[1] == 1 and field_b.shape[1] == 1
+    if plan.fits() and alone and lax.axis_size("narrow") == 4:
+        return fast_device(plan, field_a, field_b, *rest)
+    return general_device(field_a, field_b, *rest)
+
+
 def solution(mesh):
     placed = (
         P("wide", "narrow", None, None),
@@ -443,7 +1271,7 @@
         P(),
     )
     return jax.shard_map(
-        on_device,
+        choose,
         mesh=mesh,
         in_specs=placed,
         out_specs=(

time: 1670 us -> 770 us (0.46)
  blocking collectives: 447 us -> 0 us
  local copies, waits for them, and re-layouts: 427 us -> 96.1 us
  Pallas kernels: 0 us -> 164 us
  matrix products: 263 us -> 133 us
  waiting for transfers between devices: 352 us -> 248 us
  other arithmetic: 103 us -> 44.6 us
  starting transfers between devices: 48.7 us -> 65.7 us
    unnamed x2 -> x0, blocking collectives: 290 us -> none
    pallas_call x0 -> x11, Pallas kernels: none -> 164 us  [the longest x1 28.7 us: fast_device(): call(functools.partial(mixed_kernel, plan), (units,), [count_spec, plan.u...]
    psum x2 -> x0, blocking collectives: 158 us -> none  [the longest x1 84.1 us: on_device(): mlp_sums = lax.psum((grad_expand, grad_expand_b, grad_reduce), 'wide')]
    ppermute x0 -> x31, waiting for transfers between devices: none -> 157 us  [swap(): return lax.ppermute(value, axis, [(i, i ^ distance) for i in range(size)])]
    dot_general x28 -> x9, matrix products: 263 us -> 133 us  [the longest x1 39.2 us: dot(): return jnp.dot(left, right, preferred_element_type=F32)]
    reshape x33 -> x9, local copies, waits for them, and re-layouts: 140 us -> 11.7 us  [the longest x4 6.03 us: half_weight(): weight[:, :, half * side:(half + 1) * side].reshape(2, BS, blocks, BS)]
    psum x2 -> x0, waiting for transfers between devices: 98.9 us -> none  [the longest x1 98.9 us: on_device(): lax.psum((grad_weight_one, grad_shift_one, grad_weight_two, grad_shift_tw...]
    unnamed x235 -> x112, local copies, waits for them, and re-layouts: 117 us -> 31.3 us
  transfers between devices with their start and end apart: 14 -> 39, of which waited for: 5 -> 17; matrix products, arithmetic and copies ran while one was open for 40% -> 26% of each run, Pallas kernels for 0% -> 13%
where the time goes in v1:
time: 770 us; the launch traced here: 755 us
  waiting for transfers between devices  248 us (32%)
  Pallas kernels  164 us (21%)
  matrix products  133 us (17%)
  local copies, waits for them, and re-layouts  96.1 us (12%)
  starting transfers between devices  65.7 us (9%)
  other arithmetic  44.6 us (6%)
    ppermute x31, waiting for transfers between devices, swap(): return lax.ppermute(value, axis, [(i, i ^ distance) for i in range(size)])  157 us
    all_to_all x8, waiting for transfers between devices, exchange(): return [lax.all_to_all(part, 'wide', 0, 0, tiled=True) for part in parts]  91.5 us
    all_to_all x8, starting transfers between devices, exchange(): return [lax.all_to_all(part, 'wide', 0, 0, tiled=True) for part in parts]  40.3 us
    dot_general x1, matrix products, dot(): return jnp.dot(left, right, preferred_element_type=F32)  39.2 us
    dot_general x2, matrix products, dot_t(): lax.dot_general(left, right, (((1,), (1,)), ((), ())), preferred_element_...  37.5 us
    unnamed x112, local copies, waits for them, and re-layouts  31.3 us
    pallas_call x1, Pallas kernels, fast_device(): call(functools.partial(mixed_kernel, plan), (units,), [count_spec, plan.u...  28.7 us
    pallas_call x2, Pallas kernels, fast_device(): call(functools.partial(spectral_back_kernel, plan, steps), (), [whole(ite...  27 us
  transfers between devices with their start and end apart: 39, of which 17 were waited for; matrix products, arithmetic and copies ran while one was open for 26% of the time, Pallas kernels for 13%

profile of v1, /device:TPU:0, one launch (start us, length us, event | category | flops | bytes accessed | tf_op | source)
XLA Modules:
  0.0 755.2 jit_solution(4644778017489224644)
XLA Ops:
  3.2 16.0 %shard_map.333 = (bf16[8,15,24,384]{3,2,1,0:T(8,128)(2,1)}, bf16[8,15,24,384]{3,2,1,0:T(8,128)(2,1)}) custom-call(bf16[12,180,768]{2,1,0:T(8,128)(2,1)} %bitcast.74, bf16[6,90,768]{2,1,0:T(8,128)(2,1)} %bitcast.83, f32[1,768]{1,0:T(1,128)} %reshape.794.refs_2_.refs_4_.refs_5_.refs_13_, f32[1,768]{1,0:T(1,128)} %reshape.795.refs_3_.refs_5_.refs_14_, ...), custom_call_target="tpu_custom_call" | custom-call | tf_op jit(solution)/shard_map/pallas_call | solution.py:985
  19.2 7.4 all-to-all-start
  35.2 42.1 %all-to-all-done.refs_0_ = bf16[8,15,24,384]{3,2,1,0:T(8,128)(2,1)S(1)} async-done(((bf16[8,15,24,384]{3,2,1,0:T(8,128)(2,1)}), bf16[8,15,24,384]{3,2,1,0:T(8,128)(2,1)S(1)}, u32[]{:S(2)}, u32[]{:S(2)}) %all-to-all-start) | async-done | bytes 2211872 | tf_op jit(solution)/shard_map/all_to_all | solution.py:983
  78.6 3.6 all-to-all-start.2
  98.2 3.6 broadcast_multiply_fusion
  106.7 2.0 squeeze.61
  127.4 10.4 %shard_map.334 = (bf16[15,184,768]{2,1,0:T(8,128)(2,1)}, f32[8,768]{1,0:T(8,128)}) custom-call(s32[2]{0:T(128)} %pad_add_fusion.refs_0_, bf16[12,180,768]{2,1,0:T(8,128)(2,1)} %bitcast.90, bf16[6,90,768]{2,1,0:T(8,128)(2,1)} %bitcast.95), custom_call_target="tpu_custom_call" | custom-call | tf_op jit(solution)/shard_map/pallas_call | solution.py:1004
  142.5 13.1 %shard_map.335 = (bf16[8,15,24,384]{3,2,1,0:T(8,128)(2,1)}, bf16[1440,768]{1,0:T(8,128)(2,1)}, bf16[1440,768]{1,0:T(8,128)(2,1)}, bf16[1440,768]{1,0:T(8,128)(2,...) custom-call(bf16[8,15,24,384]{3,2,1,0:T(8,128)(2,1)} %copy-done.6, bf16[2,192,192]{2,1,0:T(8,128)(2,1)} %pad_maximum_fusion.1.refs_1_, ...), custom_call_target="tpu_custom_call" | custom-call | tf_op jit(solution)/shard_map/pallas_call | solution.py:1047
  155.6 6.3 all-to-all-start.1
  162.6 3.0 fusion.41
  166.1 2.5 constant_dynamic-update-slice_fusion.3
  182.0 2.2 constant_dynamic-update-slice_fusion.4.refs_10_.refs_2_
  184.2 2.2 copy-done
  186.4 13.1 %shard_map.336 = (bf16[8,15,24,384]{3,2,1,0:T(8,128)(2,1)}, bf16[1440,768]{1,0:T(8,128)(2,1)}, bf16[1440,768]{1,0:T(8,128)(2,1)}, bf16[1440,768]{1,0:T(8,128)(2,...) custom-call(bf16[8,15,24,384]{3,2,1,0:T(8,128)(2,1)} %copy-done.4, bf16[2,192,192]{2,1,0:T(8,128)(2,1)} %pad_maximum_fusion.1.refs_1_, ...), custom_call_target="tpu_custom_call" | custom-call | tf_op jit(solution)/shard_map/pallas_call | solution.py:1047
  199.6 12.7 %all-to-all-done.1.refs_2_ = bf16[8,15,24,384]{3,2,1,0:T(8,128)(2,1)} async-done(((bf16[8,15,24,384]{3,2,1,0:T(8,128)(2,1)}), bf16[8,15,24,384]{3,2,1,0:T(8,128)(2,1)}, u32[]{:S(2)}, u32[]{:S(2)}) %all-to-all-start.1) | async-done | bytes 2211872 | tf_op jit(solution)/shard_map/all_to_all | solution.py:983
  212.3 4.2 all-to-all-start.3
  218.1 2.1 collective-permute-done.7
  221.4 19.9 %convolution_convert_fusion.refs_9_ = bf16[2760,3072]{1,0:T(8,128)(2,1)} fusion(bf16[2760,768]{1,0:T(8,128)(2,1)} %bitcast.81, bf16[3072,768]{1,0:T(8,128)(2,1)} %copy-done), kind=kOutput, calls=%fused_computation.10 | convolution fusion | flops 13031792640 | bytes 25915392 | tf_op jit(solution)/shard_map/dot_general | solution.py:471
  241.3 26.0 %all-to-all-done.3.refs_3_ = bf16[8,15,24,384]{3,2,1,0:T(8,128)(2,1)S(1)} async-done(((bf16[8,15,24,384]{3,2,1,0:T(8,128)(2,1)}), bf16[8,15,24,384]{3,2,1,0:T(8,128)(2,1)S(1)}, u32[]{:S(2)}, u32[]{:S(2)}) %all-to-all-start.3) | async-done | bytes 2211872 | tf_op jit(solution)/shard_map/all_to_all | solution.py:983
  268.7 14.8 %shard_map.337 = (f32[15,184,768]{2,1,0:T(8,128)}, bf16[15,184,768]{2,1,0:T(8,128)(2,1)}) custom-call(bf16[12,180,768]{2,1,0:T(8,128)(2,1)} %bitcast.75, bf16[6,90,768]{2,1,0:T(8,128)(2,1)} %bitcast.84, bf16[8,15,24,384]{3,2,1,0:T(8,128)(2,1)} %all-to-all-done.1.refs_2_, bf16[8,15,24,384]{3,2,1,0:T(8,128)(2,1)} %copy-done.8, ...), custom_call_target="tpu_custom_call" | custom-call | tf_op jit(solution)/shard_map/pallas_call | solution.py:1060
  283.4 39.2 %convert_reduce_fusion = (f32[3072]{0:T(1024)S(1)}, bf16[2760,3072]{1,0:T(8,128)(2,1)}, bf16[2760,3072]{1,0:T(8,128)(2,1)}) fusion(f32[3072]{0:T(1024)S(1)} %maximum_convert_fusion, bf16[2760,3072]{1,0:T(8,128)(2,1)} %convolution_convert_fusion.refs_9_, bf16[2760,768]{1,0:T(8,128)(2,1)} %bitcast.112, bf16[768,3072]{1,0:T(8,128)(2,1)} %copy-done.10), kind=kOutput, calls=%fused_computation.7 | convolution fusion | flops 13158970368 | bytes 59854848 | tf_op jit(solution)/shard_map/dot_general | solution.py:467
  322.7 17.6 %convolution_convert_fusion.1 = bf16[2760,768]{1,0:T(8,128)(2,1)} fusion(bf16[2760,3072]{1,0:T(8,128)(2,1)} %get-tuple-element.140, bf16[768,3072]{1,0:T(8,128)(2,1)S(1)} %bitcast.88), kind=kOutput, calls=%fused_computation.15 | convolution fusion | flops 13025433600 | bytes 25915392 | tf_op jit(solution)/shard_map/dot_general | solution.py:471
  340.2 18.3 %shard_map.338 = (f32[15,184,768]{2,1,0:T(8,128)}, bf16[8,15,24,384]{3,2,1,0:T(8,128)(2,1)}, bf16[8,15,24,384]{3,2,1,0:T(8,128)(2,1)}, f32[8,768]{1,0:T(8,128)}) custom-call(bf16[15,184,768]{2,1,0:T(8,128)(2,1)} %bitcast.89, f32[15,184,768]{2,1,0:T(8,128)} %get-tuple-element.57.refs_1_.refs_4_, bf16[15,184,768]{2,1,0:T(8,128)(2,1)} %get-tuple-element.52.refs_11_.refs_2_, ...), custom_call_target="tpu_custom_call" | custom-call | tf_op jit(solution)/shard_map/pallas_call | solution.py:1079
  358.6 3.8 all-to-all-start.4
  362.4 19.8 %fusion.52 = (bf16[768,3072]{1,0:T(8,128)(2,1)S(1)}, f32[768,3072]{1,0:T(8,128)}) fusion(bf16[2760,768]{1,0:T(8,128)(2,1)} %bitcast.113, bf16[2760,3072]{1,0:T(8,128)(2,1)} %get-tuple-element.140), kind=kOutput, calls=%fused_computation.147 | convolution fusion | flops 13025673216 | bytes 35352576 | tf_op jit(solution)/shard_map/dot_general | solution.py:1092
  383.9 18.8 %fusion.51 = (bf16[3072,768]{1,0:T(8,128)(2,1)}, f32[3072,768]{1,0:T(8,128)}) fusion(bf16[2760,3072]{1,0:T(8,128)(2,1)S(1)} %bitcast.80, bf16[2760,768]{1,0:T(8,128)(2,1)} %bitcast.82), kind=kOutput, calls=%fused_computation.146 | convolution fusion | flops 13025673216 | bytes 35352576 | tf_op jit(solution)/shard_map/dot_general | solution.py:1091
  402.6 10.6 %all-to-all-done.4.refs_0_ = bf16[8,15,24,384]{3,2,1,0:T(8,128)(2,1)S(1)} async-done(((bf16[8,15,24,384]{3,2,1,0:T(8,128)(2,1)}), bf16[8,15,24,384]{3,2,1,0:T(8,128)(2,1)S(1)}, u32[]{:S(2)}, u32[]{:S(2)}) %all-to-all-start.4) | async-done | bytes 2211872 | tf_op jit(solution)/shard_map/all_to_all | solution.py:983
  413.3 4.6 all-to-all-start.5
  417.8 2.8 fusion.38
  421.1 2.2 fusion.10
  425.1 3.0 fusion.12
  431.4 21.0 %collective-permute-done.24 = bf16[768,768]{1,0:T(8,128)(2,1)} collective-permute-done((bf16[768,768]{1,0:T(8,128)(2,1)S(1)}, bf16[768,768]{1,0:T(8,128)(2,1)}, u32[]{:S(2)}, u32[]{:S(2)}) %collective-permute-start.24) | collective-permute-done | bytes 1179680 | tf_op jit(solution)/shard_map/ppermute | solution.py:894
  452.4 2.3 fusion.11
  454.7 22.0 %collective-permute-done.21 = bf16[768,768]{1,0:T(8,128)(2,1)} collective-permute-done((bf16[768,768]{1,0:T(8,128)(2,1)}, bf16[768,768]{1,0:T(8,128)(2,1)}, u32[]{:S(2)}, u32[]{:S(2)}) %collective-permute-start.21) | collective-permute-done | bytes 1179680 | tf_op jit(solution)/shard_map/ppermute | solution.py:894
  476.7 2.6 fusion.13
  483.3 13.6 %shard_map.339 = (bf16[8,15,24,384]{3,2,1,0:T(8,128)(2,1)}, bf16[1440,768]{1,0:T(8,128)(2,1)}, bf16[1440,768]{1,0:T(8,128)(2,1)}, f32[8,768]{1,0:T(8,128)}) custom-call(bf16[8,15,24,384]{3,2,1,0:T(8,128)(2,1)} %copy-done.5, bf16[2,192,192]{2,1,0:T(8,128)(2,1)} %pad_maximum_fusion.1.refs_1_, bf16[2,96,96]{2,1,0:T(8,128)(2,1)} %pad_maximum_fusion.3.refs_2_, ...), custom_call_target="tpu_custom_call" | custom-call | tf_op jit(solution)/shard_map/pallas_call | solution.py:1121
  496.9 5.1 fusion.54.refs_2_
  502.0 13.4 %shard_map.341 = (bf16[8,15,24,384]{3,2,1,0:T(8,128)(2,1)}, bf16[1440,768]{1,0:T(8,128)(2,1)}, bf16[1440,768]{1,0:T(8,128)(2,1)}, f32[8,768]{1,0:T(8,128)}) custom-call(bf16[8,15,24,384]{3,2,1,0:T(8,128)(2,1)} %all-to-all-done.5.refs_0_, bf16[2,192,192]{2,1,0:T(8,128)(2,1)} %pad_maximum_fusion.1.refs_1_, bf16[2,96,96]{2,1,0:T(8,128)(2,1)} %pad_maximum_fusion.3.refs_2_, ...), custom_call_target="tpu_custom_call" | custom-call | tf_op jit(solution)/shard_map/pallas_call | solution.py:1121
  515.4 5.0 all-to-all-start.6
  520.5 28.7 %shard_map.340 = (bf16[12,1,180,768]{3,2,1,0:T(8,128)(2,1)}, bf16[6,1,90,768]{3,2,1,0:T(8,128)(2,1)}, f32[8,768]{1,0:T(8,128)}) custom-call(s32[2]{0:T(128)} %pad_add_fusion.refs_0_, bf16[15,184,3072]{2,1,0:T(8,128)(2,1)} %bitcast.78, bf16[3072,768]{1,0:T(8,128)(2,1)} %copy-done, f32[1,768]{1,0:T(1,128)} %reshape.804.refs_3_, ...), custom_call_target="tpu_custom_call" | custom-call | tf_op jit(solution)/shard_map/pallas_call | solution.py:1141
  549.2 5.2 fusion.53.refs_1_
  554.5 3.5 fusion.56.refs_4_
  557.9 3.5 fusion.55.refs_3_
  561.4 5.3 shard_map.343
  566.8 2.1 constant_dynamic-slice_fusion.5
  568.8 2.5 fusion.9
  578.8 11.2 %collective-permute-done.26 = bf16[384,768]{1,0:T(8,128)(2,1)} collective-permute-done((bf16[384,768]{1,0:T(8,128)(2,1)}, bf16[384,768]{1,0:T(8,128)(2,1)}, u32[]{:S(2)}, u32[]{:S(2)}) %collective-permute-start.26) | collective-permute-done | bytes 589856 | tf_op jit(solution)/shard_map/ppermute | solution.py:894
  591.2 2.7 collective-permute-start.27
  595.0 12.3 %collective-permute-done.27 = bf16[192,768]{1,0:T(8,128)(2,1)S(1)} collective-permute-done((bf16[192,768]{1,0:T(8,128)(2,1)S(1)}, bf16[192,768]{1,0:T(8,128)(2,1)S(1)}, u32[]{:S(2)}, u32[]{:S(2)}) %collective-permute-start.27) | collective-permute-done | bytes 294944 | tf_op jit(solution)/shard_map/ppermute | solution.py:894
  607.5 5.4 all-to-all-start.7
  612.9 2.3 collective-permute-start.12
  615.2 15.2 %collective-permute-done.28 = bf16[192,768]{1,0:T(8,128)(2,1)} collective-permute-done((bf16[192,768]{1,0:T(8,128)(2,1)S(1)}, bf16[192,768]{1,0:T(8,128)(2,1)}, u32[]{:S(2)}, u32[]{:S(2)}) %collective-permute-start.28) | collective-permute-done | bytes 294944 | tf_op jit(solution)/shard_map/ppermute | solution.py:894
  631.7 21.3 %collective-permute-done.12 = f32[32,768]{1,0:T(8,128)S(1)} collective-permute-done((f32[32,768]{1,0:T(8,128)S(1)}, f32[32,768]{1,0:T(8,128)S(1)}, u32[]{:S(2)}, u32[]{:S(2)}) %collective-permute-start.12) | collective-permute-done | bytes 98336 | tf_op jit(solution)/shard_map/ppermute | solution.py:894
  653.1 4.1 collective-permute-start.13
  657.1 15.2 %collective-permute-done.13 = f32[16,768]{1,0:T(8,128)S(1)} collective-permute-done((f32[16,768]{1,0:T(8,128)S(1)}, f32[16,768]{1,0:T(8,128)S(1)}, u32[]{:S(2)}, u32[]{:S(2)}) %collective-permute-start.13) | collective-permute-done | bytes 49184 | tf_op jit(solution)/shard_map/ppermute | solution.py:894
  674.7 2.6 collective-permute-done.14
  677.4 4.6 collective-permute-done.15
  682.7 22.2 %collective-permute-done.16 = f32[64,768]{1,0:T(8,128)} collective-permute-done((f32[64,768]{1,0:T(8,128)}, f32[64,768]{1,0:T(8,128)}, u32[]{:S(2)}, u32[]{:S(2)}) %collective-permute-start.16) | collective-permute-done | bytes 196640 | tf_op jit(solution)/shard_map/ppermute | solution.py:894
  708.5 7.2 collective-permute-done.17
  717.2 2.2 fusion.14
  719.4 2.5 fusion.36
  726.4 16.8 %shard_map.342 = (f32[12,1,180,768]{3,2,1,0:T(8,128)}, f32[6,1,90,768]{3,2,1,0:T(8,128)}) custom-call(bf16[12,180,768]{2,1,0:T(8,128)(2,1)} %bitcast.77, bf16[6,90,768]{2,1,0:T(8,128)(2,1)} %bitcast.86, bf16[8,15,24,384]{3,2,1,0:T(8,128)(2,1)} %all-to-all-done.6.refs_2_, bf16[8,15,24,384]{3,2,1,0:T(8,128)(2,1)} %copy-done.7, ...), custom_call_target="tpu_custom_call" | custom-call | tf_op jit(solution)/shard_map/pallas_call | solution.py:1170
  743.2 9.0 %copy.84 = f32[12,1,180,768]{3,1,2,0:T(1,128)} copy(f32[12,1,180,768]{3,2,1,0:T(8,128)} %get-tuple-element.120) | data formatting | bytes 13271040
  752.2 2.9 copy.85
  (260 shorter events, 107.6 us)
Async XLA Ops:
  19.2 9.4 %copy-start.34 = (s32[9]{0:T(128)S(1)}, s32[9]{0:T(128)}, u32[]{:S(2)}) copy-start(s32[9]{0:T(128)} %param.26) | copy-start | bytes 112
  19.2 58.1 %all-to-all-start = ((bf16[8,15,24,384]{3,2,1,0:T(8,128)(2,1)}), bf16[8,15,24,384]{3,2,1,0:T(8,128)(2,1)S(1)}, u32[]{:S(2)}, u32[]{:S(2)}) async-start(bf16[8,15,24,384]{3,2,1,0:T(8,128)(2,1)} %get-tuple-element.51), calls=%async_computation | async-start | bytes 4423680 | tf_op jit(solution)/shard_map/all_to_all | solution.py:983
  26.6 114.9 %collective-permute-start = (bf16[768,768]{1,0:T(8,128)(2,1)}, bf16[768,768]{1,0:T(8,128)(2,1)}, u32[]{:S(2)}, u32[]{:S(2)}) collective-permute-start(bf16[768,768]{1,0:T(8,128)(2,1)} %param.36), channel_id=1, source_target_pairs={{0,2},{1,3},{2,0},{3,1},{4,6},{5,7},{6,4},{7,5},{8,10},{9,11},{10,... | collective-permute-start | bytes 3538952 | tf_op jit(solution)/shard_map/ppermute | solution.py:894
  28.1 113.4 %collective-permute-start.1 = (bf16[768,768]{1,0:T(8,128)(2,1)}, bf16[768,768]{1,0:T(8,128)(2,1)S(1)}, u32[]{:S(2)}, u32[]{:S(2)}) collective-permute-start(bf16[768,768]{1,0:T(8,128)(2,1)} %param.38), channel_id=1, source_target_pairs={{0,2},{1,3},{2,0},{3,1},{4,6},{5,7},{6,4},{7,5},{8,10},{9,11},{10,... | collective-permute-start | bytes 3538952 | tf_op jit(solution)/shard_map/ppermute | solution.py:894
  33.5 48.8 %copy-start.35 = (s32[9]{0:T(128)S(1)}, s32[9]{0:T(128)}, u32[]{:S(2)}) copy-start(s32[9]{0:T(128)} %param.27) | copy-start | bytes 112
  78.6 77.0 %all-to-all-start.2 = ((bf16[8,15,24,384]{3,2,1,0:T(8,128)(2,1)}), bf16[8,15,24,384]{3,2,1,0:T(8,128)(2,1)S(1)}, u32[]{:S(2)}, u32[]{:S(2)}) async-start(bf16[8,15,24,384]{3,2,1,0:T(8,128)(2,1)} %get-tuple-element.54), calls=%async_computation.2 | async-start | bytes 4423680 | tf_op jit(solution)/shard_map/all_to_all | solution.py:983
  82.3 15.7 %copy-start.36 = (bf16[2,768]{1,0:T(2,128)(2,1)S(1)}, bf16[2,768]{1,0:T(2,128)(2,1)}, u32[]{:S(2)}) copy-start(bf16[2,768]{1,0:T(2,128)(2,1)} %param.31) | copy-start | bytes 9220
  82.3 15.7 %copy-start.37 = (bf16[2,768]{1,0:T(2,128)(2,1)S(1)}, bf16[2,768]{1,0:T(2,128)(2,1)}, u32[]{:S(2)}) copy-start(bf16[2,768]{1,0:T(2,128)(2,1)} %param.33) | copy-start | bytes 9220
  122.9 15.6 %copy-start.33 = (f32[1,192,192]{2,1,0:T(8,128)S(1)}, f32[1,192,192]{2,1,0:T(8,128)}, u32[]{:S(2)}) copy-start(f32[1,192,192]{2,1,0:T(8,128)} %copy.69) | copy-start | bytes 442372
  127.4 11.8 %copy-start.15 = (bf16[384,384]{1,0:T(8,128)(2,1)S(1)}, bf16[384,384]{1,0:T(8,128)(2,1)}, u32[]{:S(2)}) copy-start(bf16[384,384]{1,0:T(8,128)(2,1)} %squeeze.61) | copy-start | bytes 884740
  127.4 11.8 %copy-start.27 = (bf16[384,384]{1,0:T(8,128)(2,1)S(1)}, bf16[384,384]{1,0:T(8,128)(2,1)}, u32[]{:S(2)}) copy-start(bf16[384,384]{1,0:T(8,128)(2,1)} %neg.34) | copy-start | bytes 884740
  127.4 11.8 %copy-start.29 = (bf16[384,384]{1,0:T(8,128)(2,1)S(1)}, bf16[384,384]{1,0:T(8,128)(2,1)}, u32[]{:S(2)}) copy-start(bf16[384,384]{1,0:T(8,128)(2,1)} %squeeze.60) | copy-start | bytes 884740
  155.6 10.0 %copy-start.4 = (bf16[8,15,24,384]{3,2,1,0:T(8,128)(2,1)}, bf16[8,15,24,384]{3,2,1,0:T(8,128)(2,1)S(1)}, u32[]{:S(2)}) copy-start(bf16[8,15,24,384]{3,2,1,0:T(8,128)(2,1)S(1)} %all-to-all-done.2.refs_0_) | copy-start | bytes 6635524
  155.6 56.7 %all-to-all-start.1 = ((bf16[8,15,24,384]{3,2,1,0:T(8,128)(2,1)}), bf16[8,15,24,384]{3,2,1,0:T(8,128)(2,1)}, u32[]{:S(2)}, u32[]{:S(2)}) async-start(bf16[8,15,24,384]{3,2,1,0:T(8,128)(2,1)} %get-tuple-element.53), calls=%async_computation.1 | async-start | bytes 4423680 | tf_op jit(solution)/shard_map/all_to_all | solution.py:983
  162.0 14.2 %collective-permute-start.2 = (bf16[768,768]{1,0:T(8,128)(2,1)}, bf16[768,768]{1,0:T(8,128)(2,1)}, u32[]{:S(2)}, u32[]{:S(2)}) collective-permute-start(bf16[768,768]{1,0:T(8,128)(2,1)} %param.36), channel_id=1, source_target_pairs={{0,1},{1,0},{2,3},{3,2},{4,5},{5,4},{6,7},{7,6},{8,9},{9,8},{10,11... | collective-permute-start | bytes 3538952 | tf_op jit(solution)/shard_map/ppermute | solution.py:894
  162.0 17.0 %collective-permute-start.4 = (bf16[768,768]{1,0:T(8,128)(2,1)}, bf16[768,768]{1,0:T(8,128)(2,1)}, u32[]{:S(2)}, u32[]{:S(2)}) collective-permute-start(bf16[768,768]{1,0:T(8,128)(2,1)} %param.38), channel_id=1, source_target_pairs={{0,1},{1,0},{2,3},{3,2},{4,5},{5,4},{6,7},{7,6},{8,9},{9,8},{10,11... | collective-permute-start | bytes 3538952 | tf_op jit(solution)/shard_map/ppermute | solution.py:894
  162.5 18.0 %collective-permute-start.3 = (bf16[768,768]{1,0:T(8,128)(2,1)}, bf16[768,768]{1,0:T(8,128)(2,1)}, u32[]{:S(2)}, u32[]{:S(2)}) collective-permute-start(bf16[768,768]{1,0:T(8,128)(2,1)} %collective-permute-done.refs_9_), channel_id=1, source_target_pairs={{0,1},{1,0},{2,3},{3,2},{4,5},{5,4},{6,7},{7,6},{8,9},{9,8},{10,11... | collective-permute-start | bytes 3538952 | tf_op jit(solution)/shard_map/ppermute | solution.py:894
  165.6 16.3 %collective-permute-start.5 = (bf16[768,768]{1,0:T(8,128)(2,1)S(1)}, bf16[768,768]{1,0:T(8,128)(2,1)}, u32[]{:S(2)}, u32[]{:S(2)}) collective-permute-start(bf16[768,768]{1,0:T(8,128)(2,1)S(1)} %copy-done.14), channel_id=1, source_target_pairs={{0,1},{1,0},{2,3},{3,2},{4,5},{5,4},{6,7},{7,6},{8,9},{9,8},{10,11... | collective-permute-start | bytes 3538952 | tf_op jit(solution)/shard_map/ppermute | solution.py:894
  199.5 17.0 %copy-start.38 = (bf16[768]{0:T(1024)(128)(2,1)S(1)}, bf16[768]{0:T(1024)(128)(2,1)}, u32[]{:S(2)}) copy-start(bf16[768]{0:T(1024)(128)(2,1)} %param.37) | copy-start | bytes 4612
  199.5 20.6 %copy-start.39 = (bf16[768]{0:T(1024)(128)(2,1)S(1)}, bf16[768]{0:T(1024)(128)(2,1)}, u32[]{:S(2)}) copy-start(bf16[768]{0:T(1024)(128)(2,1)} %param.34) | copy-start | bytes 4612
  199.6 21.2 %copy-start.40 = (bf16[768]{0:T(1024)(128)(2,1)S(1)}, bf16[768]{0:T(1024)(128)(2,1)}, u32[]{:S(2)}) copy-start(bf16[768]{0:T(1024)(128)(2,1)} %param.35) | copy-start | bytes 4612
  212.3 55.0 %all-to-all-start.3 = ((bf16[8,15,24,384]{3,2,1,0:T(8,128)(2,1)}), bf16[8,15,24,384]{3,2,1,0:T(8,128)(2,1)S(1)}, u32[]{:S(2)}, u32[]{:S(2)}) async-start(bf16[8,15,24,384]{3,2,1,0:T(8,128)(2,1)} %get-tuple-element.55), calls=%async_computation.3 | async-start | bytes 4423680 | tf_op jit(solution)/shard_map/all_to_all | solution.py:983
  216.5 3.7 collective-permute-start.7
  218.1 3.2 collective-permute-start.6
  220.2 1.2 collective-permute-start.8
  268.7 53.9 %slice-start.5 = ((s8[4718592]{0:T(1024)(128)(4,1)}), s8[524288]{0:T(1024)(128)(4,1)S(1)}, s32[]{:S(2)}) async-start(s8[4718592]{0:T(1024)(128)(4,1)} %bitcast.87), calls=%async_computation.13 | async-start | bytes 1048576
  283.4 39.2 %slice-start.6 = ((s8[4718592]{0:T(1024)(128)(4,1)}), s8[4194304]{0:T(1024)(128)(4,1)S(1)}, s32[]{:S(2)}) async-start(s8[4718592]{0:T(1024)(128)(4,1)} %bitcast.87), calls=%async_computation.14 | async-start | bytes 8388608
  358.6 25.2 %slice-start = ((s8[16957440]{0:T(1024)(128)(4,1)}), s8[180224]{0:T(1024)(128)(4,1)S(1)}, s32[]{:S(2)}) async-start(s8[16957440]{0:T(1024)(128)(4,1)} %bitcast.79), calls=%async_computation.8 | async-start | bytes 360448
  358.6 54.7 %all-to-all-start.4 = ((bf16[8,15,24,384]{3,2,1,0:T(8,128)(2,1)}), bf16[8,15,24,384]{3,2,1,0:T(8,128)(2,1)S(1)}, u32[]{:S(2)}, u32[]{:S(2)}) async-start(bf16[8,15,24,384]{3,2,1,0:T(8,128)(2,1)} %get-tuple-element.59), calls=%async_computation.4 | async-start | bytes 4423680 | tf_op jit(solution)/shard_map/all_to_all | solution.py:983
  362.4 21.4 %slice-start.1 = ((s8[16957440]{0:T(1024)(128)(4,1)}), s8[4194304]{0:T(1024)(128)(4,1)S(1)}, s32[]{:S(2)}) async-start(s8[16957440]{0:T(1024)(128)(4,1)} %bitcast.79), calls=%async_computation.9 | async-start | bytes 8388608
  362.4 21.4 %slice-start.2 = ((s8[16957440]{0:T(1024)(128)(4,1)}), s8[4194304]{0:T(1024)(128)(4,1)S(1)}, s32[]{:S(2)}) async-start(s8[16957440]{0:T(1024)(128)(4,1)} %bitcast.79), calls=%async_computation.10 | async-start | bytes 8388608
  362.4 21.4 %slice-start.3 = ((s8[16957440]{0:T(1024)(128)(4,1)}), s8[4194304]{0:T(1024)(128)(4,1)S(1)}, s32[]{:S(2)}) async-start(s8[16957440]{0:T(1024)(128)(4,1)} %bitcast.79), calls=%async_computation.11 | async-start | bytes 8388608
  362.4 21.4 %slice-start.4 = ((s8[16957440]{0:T(1024)(128)(4,1)}), s8[4194304]{0:T(1024)(128)(4,1)S(1)}, s32[]{:S(2)}) async-start(s8[16957440]{0:T(1024)(128)(4,1)} %bitcast.79), calls=%async_computation.12 | async-start | bytes 8388608
  383.8 37.3 %collective-permute-start.23 = (bf16[768,768]{1,0:T(8,128)(2,1)}, bf16[768,768]{1,0:T(8,128)(2,1)}, u32[]{:S(2)}, u32[]{:S(2)}) collective-permute-start(bf16[768,768]{1,0:T(8,128)(2,1)} %get-tuple-element.145), channel_id=1, source_target_pairs={{0,1},{1,0},{2,3},{3,2},{4,5},{5,4},{6,7},{7,6},{8,9},{9,8},{10,11... | collective-permute-start | bytes 3538952 | tf_op jit(solution)/shard_map/ppermute | solution.py:894
  413.3 7.4 copy-start.5
  413.3 88.8 %all-to-all-start.5 = ((bf16[8,15,24,384]{3,2,1,0:T(8,128)(2,1)}), bf16[8,15,24,384]{3,2,1,0:T(8,128)(2,1)}, u32[]{:S(2)}, u32[]{:S(2)}) async-start(bf16[8,15,24,384]{3,2,1,0:T(8,128)(2,1)} %get-tuple-element.66), calls=%async_computation.5 | async-start | bytes 4423680 | tf_op jit(solution)/shard_map/all_to_all | solution.py:983
  420.6 4.5 collective-permute-start.20
  420.6 10.8 %collective-permute-start.22 = (bf16[768,768]{1,0:T(8,128)(2,1)}, bf16[768,768]{1,0:T(8,128)(2,1)S(1)}, u32[]{:S(2)}, u32[]{:S(2)}) collective-permute-start(bf16[768,768]{1,0:T(8,128)(2,1)} %get-tuple-element.144), channel_id=1, source_target_pairs={{0,1},{1,0},{2,3},{3,2},{4,5},{5,4},{6,7},{7,6},{8,9},{9,8},{10,11... | collective-permute-start | bytes 3538952 | tf_op jit(solution)/shard_map/ppermute | solution.py:894
  423.4 29.0 %collective-permute-start.24 = (bf16[768,768]{1,0:T(8,128)(2,1)S(1)}, bf16[768,768]{1,0:T(8,128)(2,1)}, u32[]{:S(2)}, u32[]{:S(2)}) collective-permute-start(bf16[768,768]{1,0:T(8,128)(2,1)S(1)} %fusion.10), channel_id=1, source_target_pairs={{0,2},{1,3},{2,0},{3,1},{4,6},{5,7},{6,4},{7,5},{8,10},{9,11},{10,... | collective-permute-start | bytes 3538952 | tf_op jit(solution)/shard_map/ppermute | solution.py:894
  425.0 29.7 %collective-permute-start.19 = (bf16[768,768]{1,0:T(8,128)(2,1)}, bf16[768,768]{1,0:T(8,128)(2,1)}, u32[]{:S(2)}, u32[]{:S(2)}) collective-permute-start(bf16[768,768]{1,0:T(8,128)(2,1)} %get-tuple-element.146), channel_id=1, source_target_pairs={{0,1},{1,0},{2,3},{3,2},{4,5},{5,4},{6,7},{7,6},{8,9},{9,8},{10,11... | collective-permute-start | bytes 3538952 | tf_op jit(solution)/shard_map/ppermute | solution.py:894
  428.1 48.6 %collective-permute-start.21 = (bf16[768,768]{1,0:T(8,128)(2,1)}, bf16[768,768]{1,0:T(8,128)(2,1)}, u32[]{:S(2)}, u32[]{:S(2)}) collective-permute-start(bf16[768,768]{1,0:T(8,128)(2,1)} %fusion.12), channel_id=1, source_target_pairs={{0,2},{1,3},{2,0},{3,1},{4,6},{5,7},{6,4},{7,5},{8,10},{9,11},{10,... | collective-permute-start | bytes 3538952 | tf_op jit(solution)/shard_map/ppermute | solution.py:894
  481.3 87.5 %collective-permute-start.25 = (bf16[768,768]{1,0:T(8,128)(2,1)}, bf16[768,768]{1,0:T(8,128)(2,1)S(1)}, u32[]{:S(2)}, u32[]{:S(2)}) collective-permute-start(bf16[768,768]{1,0:T(8,128)(2,1)} %fusion.7), channel_id=1, source_target_pairs={{0,4},{4,0},{8,12},{12,8},{16,20},{20,16},{24,28},{28,24},{1,5},{5... | collective-permute-start | bytes 3538952 | tf_op jit(solution)/shard_map/ppermute | solution.py:894
  483.3 13.6 %copy-start.3 = (bf16[1440,768]{1,0:T(8,128)(2,1)S(1)}, bf16[1440,768]{1,0:T(8,128)(2,1)}, u32[]{:S(2)}) copy-start(bf16[1440,768]{1,0:T(8,128)(2,1)} %get-tuple-element.62.refs_9_) | copy-start | bytes 6635524
  515.4 92.0 %all-to-all-start.6 = ((bf16[8,15,24,384]{3,2,1,0:T(8,128)(2,1)}), bf16[8,15,24,384]{3,2,1,0:T(8,128)(2,1)}, u32[]{:S(2)}, u32[]{:S(2)}) async-start(bf16[8,15,24,384]{3,2,1,0:T(8,128)(2,1)} %get-tuple-element.70), calls=%async_computation.6 | async-start | bytes 4423680 | tf_op jit(solution)/shard_map/all_to_all | solution.py:983
  520.5 28.7 %copy-start.2 = (bf16[1440,768]{1,0:T(8,128)(2,1)S(1)}, bf16[1440,768]{1,0:T(8,128)(2,1)}, u32[]{:S(2)}) copy-start(bf16[1440,768]{1,0:T(8,128)(2,1)} %get-tuple-element.69.refs_9_) | copy-start | bytes 6635524
  568.8 6.8 collective-permute-start.9
  573.6 16.3 %copy-start.12 = (f32[768,768]{1,0:T(8,128)S(1)}, f32[768,768]{1,0:T(8,128)}, u32[]{:S(2)}) copy-start(f32[768,768]{1,0:T(8,128)} %copy-done.11) | copy-start | bytes 7077892
  573.6 16.3 %collective-permute-start.26 = (bf16[384,768]{1,0:T(8,128)(2,1)}, bf16[384,768]{1,0:T(8,128)(2,1)}, u32[]{:S(2)}, u32[]{:S(2)}) collective-permute-start(bf16[384,768]{1,0:T(8,128)(2,1)} %dynamic-slice_convert_fusion), channel_id=1, source_target_pairs={{0,8},{4,12},{8,0},{12,4},{16,24},{20,28},{24,16},{28,20},{1,9},{5... | collective-permute-start | bytes 1769480 | tf_op jit(solution)/shard_map/ppermute | solution.py:894
  577.2 16.7 %collective-permute-start.10 = (f32[128,768]{1,0:T(8,128)S(1)}, f32[128,768]{1,0:T(8,128)}, u32[]{:S(2)}, u32[]{:S(2)}) collective-permute-start(f32[128,768]{1,0:T(8,128)S(1)} %constant_dynamic-slice_fusion.4), channel_id=1, source_target_pairs={{0,2},{1,3},{2,0},{3,1},{4,6},{5,7},{6,4},{7,5},{8,10},{9,11},{10,... | collective-permute-start | bytes 1179656 | tf_op jit(solution)/shard_map/ppermute | solution.py:894
  591.2 16.1 %collective-permute-start.27 = (bf16[192,768]{1,0:T(8,128)(2,1)S(1)}, bf16[192,768]{1,0:T(8,128)(2,1)S(1)}, u32[]{:S(2)}, u32[]{:S(2)}) collective-permute-start(bf16[192,768]{1,0:T(8,128)(2,1)S(1)} %dynamic-slice_convert_fusion.1), channel_id=1, source_target_pairs={{0,16},{4,20},{8,24},{12,28},{16,0},{20,4},{24,8},{28,12},{1,17},{... | collective-permute-start | bytes 884744 | tf_op jit(solution)/shard_map/ppermute | solution.py:894
  595.0 17.9 %collective-permute-start.11 = (f32[64,768]{1,0:T(8,128)S(1)}, f32[64,768]{1,0:T(8,128)S(1)}, u32[]{:S(2)}, u32[]{:S(2)}) collective-permute-start(f32[64,768]{1,0:T(8,128)S(1)} %constant_dynamic-slice_fusion.3), channel_id=1, source_target_pairs={{0,4},{4,0},{8,12},{12,8},{16,20},{20,16},{24,28},{28,24},{1,5},{5... | collective-permute-start | bytes 589832 | tf_op jit(solution)/shard_map/ppermute | solution.py:894
  607.4 23.0 %collective-permute-start.28 = (bf16[192,768]{1,0:T(8,128)(2,1)S(1)}, bf16[192,768]{1,0:T(8,128)(2,1)}, u32[]{:S(2)}, u32[]{:S(2)}) collective-permute-start(bf16[192,768]{1,0:T(8,128)(2,1)S(1)} %add_convert_fusion), channel_id=1, source_target_pairs={{0,16},{4,20},{8,24},{12,28},{16,0},{20,4},{24,8},{28,12},{1,17},{... | collective-permute-start | bytes 884744 | tf_op jit(solution)/shard_map/ppermute | solution.py:894
  607.5 117.6 %all-to-all-start.7 = ((bf16[8,15,24,384]{3,2,1,0:T(8,128)(2,1)}), bf16[8,15,24,384]{3,2,1,0:T(8,128)(2,1)S(1)}, u32[]{:S(2)}, u32[]{:S(2)}) async-start(bf16[8,15,24,384]{3,2,1,0:T(8,128)(2,1)} %get-tuple-element.71), calls=%async_computation.7 | async-start | bytes 4423680 | tf_op jit(solution)/shard_map/all_to_all | solution.py:983
  612.9 40.1 %collective-permute-start.12 = (f32[32,768]{1,0:T(8,128)S(1)}, f32[32,768]{1,0:T(8,128)S(1)}, u32[]{:S(2)}, u32[]{:S(2)}) collective-permute-start(f32[32,768]{1,0:T(8,128)S(1)} %constant_dynamic-slice_fusion.2), channel_id=1, source_target_pairs={{0,8},{4,12},{8,0},{12,4},{16,24},{20,28},{24,16},{28,20},{1,9},{5... | collective-permute-start | bytes 294920 | tf_op jit(solution)/shard_map/ppermute | solution.py:894
  631.6 40.7 %copy-start.17 = (bf16[384,768]{1,0:T(8,128)(2,1)}, bf16[384,768]{1,0:T(8,128)(2,1)S(1)}, u32[]{:S(2)}) copy-start(bf16[384,768]{1,0:T(8,128)(2,1)S(1)} %maximum_select_fusion.4) | copy-start | bytes 1769476
  631.7 40.7 %collective-permute-start.29 = (bf16[384,768]{1,0:T(8,128)(2,1)S(1)}, bf16[384,768]{1,0:T(8,128)(2,1)}, u32[]{:S(2)}, u32[]{:S(2)}) collective-permute-start(bf16[384,768]{1,0:T(8,128)(2,1)S(1)} %maximum_select_fusion.4), channel_id=1, source_target_pairs={{0,8},{4,12},{8,0},{12,4},{16,24},{20,28},{24,16},{28,20},{1,9},{5... | collective-permute-start | bytes 1769480 | tf_op jit(solution)/shard_map/ppermute | solution.py:894
  653.1 19.2 %collective-permute-start.13 = (f32[16,768]{1,0:T(8,128)S(1)}, f32[16,768]{1,0:T(8,128)S(1)}, u32[]{:S(2)}, u32[]{:S(2)}) collective-permute-start(f32[16,768]{1,0:T(8,128)S(1)} %constant_dynamic-slice_fusion.1), channel_id=1, source_target_pairs={{0,16},{4,20},{8,24},{12,28},{16,0},{20,4},{24,8},{28,12},{1,17},{... | collective-permute-start | bytes 147464 | tf_op jit(solution)/shard_map/ppermute | solution.py:894
  672.3 5.1 collective-permute-start.14
  674.4 42.8 %collective-permute-start.30 = (bf16[768,768]{1,0:T(8,128)(2,1)S(1)}, bf16[768,768]{1,0:T(8,128)(2,1)}, u32[]{:S(2)}, u32[]{:S(2)}) collective-permute-start(bf16[768,768]{1,0:T(8,128)(2,1)S(1)} %maximum_select_fusion.2), channel_id=1, source_target_pairs={{0,4},{4,0},{8,12},{12,8},{16,20},{20,16},{24,28},{28,24},{1,5},{5... | collective-permute-start | bytes 3538952 | tf_op jit(solution)/shard_map/ppermute | solution.py:894
  677.3 4.7 collective-permute-start.15
  682.7 22.2 %collective-permute-start.16 = (f32[64,768]{1,0:T(8,128)}, f32[64,768]{1,0:T(8,128)}, u32[]{:S(2)}, u32[]{:S(2)}) collective-permute-start(f32[64,768]{1,0:T(8,128)} %maximum_select_fusion.6), channel_id=1, source_target_pairs={{0,4},{4,0},{8,12},{12,8},{16,20},{20,16},{24,28},{28,24},{1,5},{5... | collective-permute-start | bytes 589832 | tf_op jit(solution)/shard_map/ppermute | solution.py:894
  707.0 8.7 %collective-permute-start.17 = (f32[128,768]{1,0:T(8,128)}, f32[128,768]{1,0:T(8,128)}, u32[]{:S(2)}, u32[]{:S(2)}) collective-permute-start(f32[128,768]{1,0:T(8,128)} %maximum_select_fusion.5), channel_id=1, source_target_pairs={{0,2},{1,3},{2,0},{3,1},{4,6},{5,7},{6,4},{7,5},{8,10},{9,11},{10,... | collective-permute-start | bytes 1179656 | tf_op jit(solution)/shard_map/ppermute | solution.py:894
  717.1 4.8 collective-permute-start.18
  743.1 9.0 %copy-start.22 = (f32[6,1,90,768]{3,2,1,0:T(8,128)S(1)}, f32[6,1,90,768]{3,2,1,0:T(8,128)}, u32[]{:S(2)}) copy-start(f32[6,1,90,768]{3,2,1,0:T(8,128)} %get-tuple-element.121) | copy-start | bytes 4976644
  (24 other events, 71.0 us)

commit v2 on v1

--- a/solution.py
+++ b/solution.py
@@ -430,6 +430,8 @@
 MIB = 1024 * 1024
 PAD = 8
 LANES = 128
+CHUNK = 256
+NARROW = 4
 
 
 def halves(value):
@@ -459,7 +461,7 @@
 
 
 def whole(array):
-    zeros = (0,) * array.ndim
+    zeros = (0,) * len(array.shape)
     return pl.BlockSpec(array.shape, lambda *_: zeros)
 
 
@@ -501,21 +503,6 @@
     return jnp.stack([upper, lower]).reshape(2 * padded, -1)
 
 
-def half_weight(weight, half, blocks):
-    side = blocks * BS
-    pieces = weight[:, :, half * side : (half + 1) * side].reshape(2, BS, blocks, BS)
-    eye = jnp.eye(blocks, dtype=weight.dtype)
-    wide = pieces.transpose(0, 2, 1, 3)[:, :, :, None, :] * eye[None, :, None, :, None]
-    wide = wide.reshape(2, side, side)
-    return jnp.concatenate(
-        [
-            jnp.concatenate([wide[0], wide[1]], axis=1),
-            jnp.concatenate([-wide[1], wide[0]], axis=1),
-        ],
-        axis=0,
-    )
-
-
 def layer_norm(value):
     mean = jnp.mean(value, axis=1, keepdims=True)
     centred = value - mean
@@ -549,7 +536,10 @@
         self.spread_b = -(-(columns_b // 2 + 1) // width)
         self.piece = 2 * self.spread_a
         self.units = rows_a + rows_b // 2
-        self.tokens = round_up(columns_a, 8)
+        self.group = max(1, math.gcd(rows_a, rows_b // 2))
+        self.steps_a = rows_a // self.group
+        self.steps = self.units // self.group
+        self.tokens = round_up(columns_a, 16)
         self.pad_a = round_up(H_A, 16)
         self.pad_b = round_up(H_B, 16)
         self.points_a = self.spread_a * self.pad_a
@@ -566,103 +556,179 @@
         )
 
     def spec_a(self):
-        last = self.rows_a - 1
+        last = self.steps_a - 1
         return pl.BlockSpec(
-            (1, self.columns_a, self.local), lambda i: (jnp.minimum(i, last), 0, 0)
+            (self.group, self.columns_a, self.local), lambda i: (jnp.minimum(i, last), 0, 0)
         )
 
     def spec_b(self):
-        first = self.rows_a
+        first = self.steps_a
         return pl.BlockSpec(
-            (2, self.columns_b, self.local), lambda i: (jnp.maximum(i - first, 0), 0, 0)
+            (2 * self.group, self.columns_b, self.local),
+            lambda i: (jnp.maximum(i - first, 0), 0, 0),
         )
 
-    def unit(self, last=None):
-        return pl.BlockSpec((1, self.tokens, last or self.local), lambda i: (i, 0, 0))
+    def rows(self):
+        return pl.BlockSpec((self.group * self.tokens, self.local), lambda i: (i, 0))
+
+    def chunks(self):
+        return pl.BlockSpec((NARROW, self.group * self.tokens, self.local), lambda i: (0, i, 0))
 
     def sends(self):
-        return pl.BlockSpec((self.width, 1, self.piece, self.half), lambda i: (0, i, 0, 0))
+        return pl.BlockSpec(
+            (self.width, self.group, self.piece, self.half), lambda i: (0, i, 0, 0)
+        )
 
     def table(self, shape):
-        first = self.rows_a
+        first = self.steps_a
         zeros = (0,) * len(shape)
         return pl.BlockSpec((1,) + shape, lambda i: ((i >= first).astype(jnp.int32),) + zeros)
 
     def exchange_shape(self):
         return jax.ShapeDtypeStruct((self.width, self.units, self.piece, self.half), BF16)
 
-    def units_shape(self, kind):
-        return jax.ShapeDtypeStruct((self.units, self.tokens, self.local), kind)
+    def full_sends(self):
+        return pl.BlockSpec(
+            (self.width, self.group, self.piece, self.local), lambda i: (0, i, 0, 0)
+        )
+
+    def full_shape(self):
+        return jax.ShapeDtypeStruct((self.width, self.units, self.piece, self.local), BF16)
+
+    def rows_shape(self, kind):
+        return jax.ShapeDtypeStruct((self.units * self.tokens, self.local), kind)
+
+    def chunks_shape(self):
+        return jax.ShapeDtypeStruct((NARROW, self.units * self.tokens, self.local), BF16)
+
+    def scratch(self):
+        return pltpu.VMEM((self.group * self.tokens, self.local), F32)
 
     def load(self, step, a_ref, b_ref, scratch):
         @pl.when(step == 0)
         def _():
             scratch[...] = jnp.zeros_like(scratch)
 
-        @pl.when(step < self.rows_a)
+        @pl.when(step < self.steps_a)
         def _():
-            scratch[: self.columns_a] = a_ref[0].astype(F32)
-
-        @pl.when(step >= self.rows_a)
+            for u in range(self.group):
+                base = u * self.tokens
+                scratch[base : base + self.columns_a] = a_ref[u].astype(F32)
+
+        @pl.when(step >= self.steps_a)
         def _():
-            scratch[: self.columns_b] = b_ref[0].astype(F32)
-            scratch[self.columns_b : self.columns_a] = b_ref[1].astype(F32)
+            for u in range(self.group):
+                base = u * self.tokens
+                middle = base + self.columns_b
+                scratch[base:middle] = b_ref[2 * u].astype(F32)
+                scratch[middle : base + self.columns_a] = b_ref[2 * u + 1].astype(F32)
 
         return scratch[...]
 
+    def parts(self, value):
+        return [value[u * self.tokens : (u + 1) * self.tokens] for u in range(self.group)]
+
     def outs(self):
-        last, first = self.rows_a - 1, self.rows_a
+        last, first = self.steps_a - 1, self.steps_a
         return [
             pl.BlockSpec(
-                (1, 1, self.columns_a, self.local), lambda i: (jnp.minimum(i, last), 0, 0, 0)
+                (self.group, 1, self.columns_a, self.local),
+                lambda i: (jnp.minimum(i, last), 0, 0, 0),
             ),
             pl.BlockSpec(
-                (2, 1, self.columns_b, self.local), lambda i: (jnp.maximum(i - first, 0), 0, 0, 0)
+                (2 * self.group, 1, self.columns_b, self.local),
+                lambda i: (jnp.maximum(i - first, 0), 0, 0, 0),
             ),
         ]
 
+    def flat_outs(self):
+        last, first = self.steps_a - 1, self.steps_a
+        return [
+            pl.BlockSpec(
+                (self.group, self.columns_a, 1, self.local),
+                lambda i: (jnp.minimum(i, last), 0, 0, 0),
+            ),
+            pl.BlockSpec(
+                (2 * self.group, self.columns_b, 1, self.local),
+                lambda i: (jnp.maximum(i - first, 0), 0, 0, 0),
+            ),
+        ]
+
     def store(self, step, value, a_ref, b_ref):
-        @pl.when(step < self.rows_a)
+        units = self.parts(value)
+
+        @pl.when(step < self.steps_a)
         def _():
-            a_ref[0, 0] = value[: self.columns_a].astype(a_ref.dtype)
-
-        @pl.when(step >= self.rows_a)
+            for u in range(self.group):
+                a_ref[u, 0] = units[u][: self.columns_a].astype(a_ref.dtype)
+
+        @pl.when(step >= self.steps_a)
         def _():
-            b_ref[0, 0] = value[: self.columns_b].astype(b_ref.dtype)
-            b_ref[1, 0] = value[self.columns_b : self.columns_a].astype(b_ref.dtype)
-
-    def put_sends(self, product, refs):
+            for u in range(self.group):
+                b_ref[2 * u, 0] = units[u][: self.columns_b].astype(b_ref.dtype)
+                b_ref[2 * u + 1, 0] = units[u][self.columns_b : self.columns_a].astype(b_ref.dtype)
+
+    def store_flat(self, step, value, a_ref, b_ref):
+        units = self.parts(value)
+
+        @pl.when(step < self.steps_a)
+        def _():
+            for u in range(self.group):
+                a_ref[u, :, 0, :] = units[u][: self.columns_a]
+
+        @pl.when(step >= self.steps_a)
+        def _():
+            for u in range(self.group):
+                b_ref[2 * u, :, 0, :] = units[u][: self.columns_b]
+                b_ref[2 * u + 1, :, 0, :] = units[u][self.columns_b : self.columns_a]
+
+    def put_sends(self, product, unit, refs):
+        size = self.local // len(refs)
         for index, ref in enumerate(refs):
-            lanes = product[:, index * self.half : (index + 1) * self.half]
-            ref[:, 0] = lanes.reshape(self.width, self.piece, self.half).astype(BF16)
-
-    def get_sends(self, refs):
+            lanes = product[:, index * size : (index + 1) * size]
+            ref[:, unit] = lanes.reshape(self.width, self.piece, size).astype(BF16)
+
+    def from_sends(self, table, refs):
         depth = self.width * self.piece
-        return [ref[:, 0].astype(F32).reshape(depth, self.half).astype(BF16) for ref in refs]
+        units = []
+        for u in range(self.group):
+            size = self.local // len(refs)
+            parts = [ref[:, u].astype(F32).reshape(depth, size).astype(BF16) for ref in refs]
+            units.append(jnp.concatenate([dot(table, part) for part in parts], axis=1))
+        return jnp.concatenate(units, axis=0)
 
     def valid_rows(self, step, counts, shape):
-        token = lax.broadcasted_iota(jnp.int32, shape, 0)
-        second = (token >= self.columns_b).astype(jnp.int32)
-        in_a = (step < counts[0]) & (step < self.rows_a)
-        row_b = 2 * (step - self.rows_a) + second
-        in_b = (row_b < counts[1]) & (step >= self.rows_a)
-        return (in_a | in_b) & (token < self.columns_a)
+        row = lax.broadcasted_iota(jnp.int32, shape, 0)
+        inside = row >= 0
+        used = row < 0
+        for u in range(self.group):
+            token = row - u * self.tokens
+            here = (token >= 0) & (token < self.columns_a)
+            in_a = (step < self.steps_a) & (step * self.group + u < counts[0])
+            pair = 2 * ((step - self.steps_a) * self.group + u)
+            in_b0 = (step >= self.steps_a) & (pair < counts[1])
+            in_b1 = (step >= self.steps_a) & (pair + 1 < counts[1])
+            first = (in_a | in_b0).astype(jnp.int32)
+            second = (in_a | in_b1).astype(jnp.int32)
+            flag = jnp.where(token < self.columns_b, first, second)
+            used = used | (here & (flag > 0))
+        return used
 
 
 def first_kernel(plan, xa, xb, gain, bias, table, out0, out1, scratch):
     step = pl.program_id(0)
-    value = plan.load(step, xa, xb, scratch)
-    standard, _ = layer_norm(value)
-    high, low = halves(standard * gain[...] + bias[...])
-    spectrum = dot(table[0, 0], high) + (dot(table[0, 0], low) + dot(table[0, 1], high))
-    plan.put_sends(spectrum, (out0, out1))
+    standard, _ = layer_norm(plan.load(step, xa, xb, scratch))
+    for u, part in enumerate(plan.parts(standard * gain[...] + bias[...])):
+        high, low = halves(part)
+        spectrum = dot(table[0, 0], high) + (dot(table[0, 0], low) + dot(table[0, 1], high))
+        plan.put_sends(spectrum, u, (out0, out1))
 
 
 def cotangent_kernel(plan, counts, ca, cb, out, sums, scratch):
     step = pl.program_id(0)
     value = plan.load(step, ca, cb, scratch)
     value = jnp.where(plan.valid_rows(step, counts, value.shape), value, 0.0)
-    out[0] = value.astype(BF16)
+    out[...] = value.astype(BF16)
 
     @pl.when(step == 0)
     def _():
@@ -671,57 +737,271 @@
     sums[...] += row_sums(value)
 
 
-def middle_kernel(plan, xa, xb, got0, got1, gain, bias, gain2, bias2, table, mid, out, scratch):
+def gelu_both(value):
+    bell = jnp.exp(-0.5 * value * value)
+    cdf = 0.5 * (1.0 + lax.erf(value * ROOT_HALF))
+    return value * cdf, cdf + value * bell * (1.0 / ROOT_TWO_PI)
+
+
+def hidden_kernel(cot, w0, w1, w2, w3, out):
+    for k, weight in enumerate((w0, w1, w2, w3)):
+        out[k] = dot_t(cot[...], weight[...]).astype(BF16)
+
+
+def middle_kernel(
+    plan, xa, xb, got0, got1, gain, bias, gain2, bias2, inv, inv_t, w0, w1, w2, w3, shift, back,
+    cot, mid, rows, hidden, grad_pre, dmid, out, sums, shift_sums, scratch,
+):
     step = pl.program_id(0)
-    value = plan.load(step, xa, xb, scratch)
-    standard, _ = layer_norm(value)
-    back = jnp.concatenate([dot(table[0], part) for part in plan.get_sends((got0, got1))], axis=1)
-    middle = value + standard * gain[...] + bias[...] + back
-    mid[0] = middle
-    standard2, _ = layer_norm(middle)
-    out[0] = (standard2 * gain2[...] + bias2[...]).astype(BF16)
-
-
-def middle_back_kernel(plan, dv, mid, cot, gain2, table, dmid, out0, out1, sums):
-    step = pl.program_id(0)
-    grad = dv[0].astype(F32)
-    standard, scale = layer_norm(mid[0])
-    total = cot[0].astype(F32) + layer_norm_back(grad, gain2[...], standard, scale)
-    dmid[0] = total
-    plan.put_sends(dot(table[0], total.astype(BF16)), (out0, out1))
 
     @pl.when(step == 0)
     def _():
         sums[...] = jnp.zeros_like(sums)
-
+        shift_sums[...] = jnp.zeros_like(shift_sums)
+
+    value = plan.load(step, xa, xb, scratch)
+    standard, _ = layer_norm(value)
+    middle = value + standard * gain[...] + bias[...]
+    middle += plan.from_sends(inv[0], (got0, got1))
+    mid[...] = middle
+    standard, scale = layer_norm(middle)
+    flat = (standard * gain2[...] + bias2[...]).astype(BF16)
+    rows[...] = flat
+    weights = (w0, w1, w2, w3)
+    grad = None
+    for k, weight in enumerate(weights):
+        for start in range(0, plan.local, CHUNK):
+            lanes = slice(start, start + CHUNK)
+            act, slope = gelu_both(dot(flat, weight[:, lanes]) + shift[k : k + 1, lanes])
+            hidden[k, :, lanes] = act.astype(BF16)
+            pre = back[k, :, lanes].astype(F32) * slope
+            grad_pre[k, :, lanes] = pre.astype(BF16)
+            shift_sums[k, :1, lanes] += jnp.sum(pre, axis=0, keepdims=True)
+        part = dot_t(grad_pre[k], weight[...])
+        grad = part if grad is None else grad + part
     sums[...] += row_sums(grad * standard, grad)
+    result = cot[...].astype(F32) + layer_norm_back(grad, gain2[...], standard, scale)
+    dmid[...] = result
+    for u, part in enumerate(plan.parts(result)):
+        plan.put_sends(dot(inv_t[0], part.astype(BF16)), u, (out,))
 
 
 def mixed_kernel(
-    plan, counts, hidden, weight, bias, mid, dmid, xa, xb, outa, outb, sums, scratch
+    plan, counts, hidden, w0, w1, w2, w3, bias, mid, dmid, xa, xb, outa, outb, sums, scratch
 ):
     step = pl.program_id(0)
     standard, _ = layer_norm(plan.load(step, xa, xb, scratch))
-    grad = dmid[0]
+    grad = dmid[...]
 
     @pl.when(step == 0)
     def _():
         sums[...] = jnp.zeros_like(sums)
 
     sums[...] += row_sums(grad * standard, grad)
-    value = mid[0] + dot(hidden[0], weight[...]) + bias[...]
+    value = mid[...] + bias[...]
+    for k, weight in enumerate((w0, w1, w2, w3)):
+        value += dot(hidden[k], weight[...])
     value = jnp.where(plan.valid_rows(step, counts, value.shape), value, 0.0)
     plan.store(step, value, outa, outb)
 
 
-def last_kernel(plan, xa, xb, got0, got1, dmid, gain, table, outa, outb, scratch):
+def products(plan, chunked, plain, first, chunk_left, got=None):
+    count, local = plain.shape
+    square = (1, local, local)
+    chunk = pl.BlockSpec((1, count, local), lambda i: (2 * i + first, 0, 0))
+    flat = pl.BlockSpec((count, local), lambda i: (0, 0))
+    each = pl.BlockSpec(square, lambda i: (i, 0, 0))
+    whole_out = pl.BlockSpec((local, local), lambda i: (0, 0))
+    one = jax.ShapeDtypeStruct((local, local), BF16)
+
+    def kernel(chunk_ref, plain_ref, *refs):
+        pair = (chunk_ref[0], plain_ref[...])
+        value = lax.dot_general(
+            *(pair if chunk_left else pair[::-1]),
+            (((0,), (0,)), ((), ())),
+            preferred_element_type=F32,
+        )
+        if got is None:
+            refs[0][0] = value.astype(BF16)
+            return
+        value += refs[0][0].astype(F32)
+        for k in range(2):
+
+            @pl.when(pl.program_id(0) == k)
+            def _(k=k):
+                refs[1 + k][...] = value.astype(BF16)
+
+    if got is None:
+        return call(
+            kernel, (2,), [chunk, flat], each, jax.ShapeDtypeStruct((2, local, local), BF16)
+        )(chunked, plain)
+    return call(kernel, (2,), [chunk, flat, each], [whole_out] * 2, [one] * 2)(
+        chunked, plain, got
+    )
+
+
+def last_kernel(plan, xa, xb, got, dmid, gain, table, outa, outb, scratch):
     step = pl.program_id(0)
-    value = plan.load(step, xa, xb, scratch)
-    standard, scale = layer_norm(value)
-    back = jnp.concatenate([dot(table[0], part) for part in plan.get_sends((got0, got1))], axis=1)
-    grad = back + dmid[0]
-    total = dmid[0] + layer_norm_back(grad, gain[...], standard, scale)
-    plan.store(step, total, outa, outb)
+    standard, scale = layer_norm(plan.load(step, xa, xb, scratch))
+    passed = dmid[...]
+    grad = plan.from_sends(table[0], (got,)) + passed
+    total = passed + layer_norm_back(grad, gain[...], standard, scale)
+    plan.store_flat(step, total, outa, outb)
+
+
+def weights_kernel(plan, inner, outer, inner0, inner1, outer0, outer1):
+    half = plan.half
+    for weight, outs in ((inner, (inner0, inner1)), (outer, (outer0, outer1))):
+        parts = [weight[k].astype(F32) for k in range(2)]
+        for h, out in enumerate(outs):
+            out[...] = jnp.zeros_like(out)
+            for b in range(half // BS):
+                lanes = slice(h * half + b * BS, h * half + (b + 1) * BS)
+                near = slice(b * BS, (b + 1) * BS)
+                late = slice(half + b * BS, half + (b + 1) * BS)
+                real, imag = parts[0][:, lanes].astype(BF16), parts[1][:, lanes].astype(BF16)
+                out[near, near] = real
+                out[late, late] = real
+                out[near, late] = imag
+                out[late, near] = -imag
+
+
+def nothing(*refs):
+    return None
+
+
+def hold(value, *before):
+    anywhere = pl.BlockSpec(memory_space=pl.ANY)
+    return pl.pallas_call(
+        nothing,
+        in_specs=[anywhere] * (1 + len(before)),
+        out_specs=anywhere,
+        out_shape=jax.ShapeDtypeStruct(value.shape, value.dtype),
+        input_output_aliases={0: 0},
+    )(value, *before)
+
+
+def bit_of(place, link):
+    return (place[link[0]] // link[1]) % 2
+
+
+def fold_kernel(link, place, left, right, keep, send):
+    total = left[...].astype(F32) + right[...].astype(F32)
+    size = keep.shape[-2]
+    near, far = total[..., :size, :], total[..., size:, :]
+    bit = bit_of(place, link)
+
+    @pl.when(bit == 0)
+    def _():
+        keep[...] = near.astype(keep.dtype)
+        send[...] = far.astype(send.dtype)
+
+    @pl.when(bit == 1)
+    def _():
+        keep[...] = far.astype(keep.dtype)
+        send[...] = near.astype(send.dtype)
+
+
+SMEM = pl.BlockSpec(memory_space=pltpu.SMEM)
+
+
+def flat_call(kernel, place, operands, shapes, before=()):
+    def spec(item):
+        zeros = (0,) * len(item.shape)
+        return pl.BlockSpec(item.shape, lambda: zeros)
+
+    return call(
+        kernel,
+        (),
+        [SMEM] + [spec(item) for item in operands],
+        [spec(item) for item in shapes],
+        list(shapes),
+        after=len(before),
+    )(place, *operands, *before)
+
+
+def fold(place, link, left, right, *before):
+    shape = left.shape[:-2] + (left.shape[-2] // 2, left.shape[-1])
+    half = jax.ShapeDtypeStruct(shape, left.dtype)
+    return flat_call(
+        functools.partial(fold_kernel, link), place, (left, right), (half, half), before
+    )
+
+
+def add_pairs(place, lefts, rights, *before):
+    count = len(lefts)
+
+    def kernel(_, *refs):
+        for k in range(count):
+            value = refs[k][...].astype(F32) + refs[count + k][...].astype(F32)
+            refs[2 * count + k][...] = value.astype(BF16)
+
+    shapes = [jax.ShapeDtypeStruct(item.shape, BF16) for item in lefts]
+    return flat_call(kernel, place, (*lefts, *rights), shapes, before)
+
+
+def total(place, parts, *before, kind=None):
+    def kernel(_, *refs):
+        values = [ref[...].astype(F32) for ref in refs[:-1]]
+        while len(values) > 1:
+            values = [a + b for a, b in zip(values[::2], values[1::2], strict=True)]
+        refs[-1][...] = values[0].astype(refs[-1].dtype)
+
+    return flat_call(
+        kernel, place, parts, [jax.ShapeDtypeStruct(parts[0].shape, kind or parts[0].dtype)], before
+    )[0]
+
+
+def join(place, link, mine, other, *before, kind=None):
+    size = mine.shape[-2]
+    shape = mine.shape[:-2] + (2 * size, mine.shape[-1])
+
+    def kernel(place, mine, other, out):
+        bit = bit_of(place, link)
+
+        def put(low, high):
+            out[..., :size, :] = low[...].astype(out.dtype)
+            out[..., size:, :] = high[...].astype(out.dtype)
+
+        @pl.when(bit == 0)
+        def _():
+            put(mine, other)
+
+        @pl.when(bit == 1)
+        def _():
+            put(other, mine)
+
+    return flat_call(
+        kernel, place, (mine, other), [jax.ShapeDtypeStruct(shape, kind or mine.dtype)], before
+    )[0]
+
+
+def last_join(place, link, mine, other):
+    size, local = mine.shape
+
+    def kernel(place, mine, other, inner, outer, small, whole_pack):
+        bit = bit_of(place, link)
+        whole_pack[pl.ds(pl.multiple_of(bit * size, size), size), :] = mine[...].astype(F32)
+        whole_pack[pl.ds(pl.multiple_of((1 - bit) * size, size), size), :] = other[...].astype(F32)
+        for k in range(2):
+            inner[k] = whole_pack[k * BS : (k + 1) * BS]
+            outer[k] = whole_pack[(2 + k) * BS : (3 + k) * BS]
+        small[...] = whole_pack[4 * BS : 4 * BS + small.shape[0]]
+
+    def spec(item):
+        zeros = (0,) * len(item.shape)
+        return pl.BlockSpec(item.shape, lambda: zeros)
+
+    matrix = jax.ShapeDtypeStruct((2, BS, local), F32)
+    shapes = [matrix, matrix, jax.ShapeDtypeStruct((16, local), F32)]
+    return call(
+        kernel,
+        (),
+        [SMEM, spec(mine), spec(other)],
+        [spec(item) for item in shapes],
+        shapes,
+        [pltpu.VMEM((2 * size, local), F32)],
+    )(place, mine, other)
 
 
 def unpack(plan, got, part_a, part_b):
@@ -820,8 +1100,9 @@
 
 
 def spectral_back_kernel(
-    plan, steps, got, ta, tb, tat, tbt, w1, w2, slope1, slope2, zed, out, grad1, grad2, sums, pa, pb, work
+    plan, steps, skip, got, ta, tb, tat, tbt, w1, w2, slope1, slope2, zed, *refs
 ):
+    out, grad1, grad2, sums, pa, pb, work = refs[skip:]
     unpack(plan, got, pa, pb)
     to_points(plan, (pa, pb), (ta, tb), work)
     size = plan.points // steps
@@ -846,7 +1127,9 @@
     repack(plan, pa, pb, out)
 
 
-def pack_kernel(plan, place, products, backs, dcs, norm2, cot, norm1, shift, gain, bias, out):
+def pack_kernel(
+    plan, place, products, backs, dcs, norm2, cot, norm1, shift, gain, bias, keep, send, out
+):
     half, blocks = plan.half, plan.half // BS
     out[...] = jnp.zeros_like(out)
     for kind in range(2):
@@ -886,42 +1169,16 @@
         out[row + 1 : row + 2, lanes] = plain
     row += 2
     for n in range(4):
-        out[row + n : row + n + 1] = shift[pl.ds(n ^ place[1], 1), :]
+        out[row + n : row + n + 1] = shift[n ^ place[1], :1]
+    size = keep.shape[0]
+    mine = pl.multiple_of((place[1] % 2) * size, size)
+    keep[...] = out[pl.ds(mine, size), :]
+    send[...] = out[pl.ds(size - mine, size), :]
 
 
 def swap(value, axis, distance):
     size = lax.axis_size(axis)
     return lax.ppermute(value, axis, [(i, i ^ distance) for i in range(size)])
-
-
-def halve(value, axis, distance):
-    size = value.shape[0] // 2
-    bit = (lax.axis_index(axis) // distance) % 2
-    keep = lax.dynamic_slice_in_dim(value, bit * size, size)
-    send = lax.dynamic_slice_in_dim(value, (1 - bit) * size, size)
-    return keep, send
-
-
-def join(value, axis, distance):
-    other = swap(value, axis, distance)
-    bit = (lax.axis_index(axis) // distance) % 2
-    return jnp.where(
-        bit == 0, jnp.concatenate([value, other]), jnp.concatenate([other, value])
-    )
-
-
-def add_up(value, links, kind):
-    for axis, distance in links:
-        keep, send = halve(value, axis, distance)
-        value = keep + swap(send.astype(kind), axis, distance).astype(F32)
-    value = value.astype(kind)
-    for axis, distance in reversed(links):
-        value = join(value, axis, distance)
-    return value
-
-
-def powers(size):
-    return [1 << k for k in range(size.bit_length() - 1)]
 
 
 def fast_device(
@@ -946,7 +1203,6 @@
     reduce_bias,
 ):
     width, local, half = plan.width, plan.local, plan.half
-    blocks = half // BS
     tokens, units = plan.tokens, plan.units
     myself = lax.axis_index("wide")
     xa = field_a.reshape(plan.rows_a, plan.columns_a, local)
@@ -973,7 +1229,7 @@
     vector = pl.BlockSpec((1, local), lambda i: (0, 0))
     sums_spec = pl.BlockSpec((PAD, local), lambda i: (0, 0))
     sums_shape = jax.ShapeDtypeStruct((PAD, local), F32)
-    scratch = pltpu.VMEM((tokens, local), F32)
+    scratch = plan.scratch()
     counts = jnp.stack(
         [offsets_a[myself + 1] - offsets_a[myself], offsets_b[myself + 1] - offsets_b[myself]]
     )
@@ -984,33 +1240,41 @@
 
     sends = call(
         functools.partial(first_kernel, plan),
-        (units,),
+        (plan.steps,),
         [plan.spec_a(), plan.spec_b(), vector, vector, plan.table((2, depth, tokens))],
         [plan.sends(), plan.sends()],
         [plan.exchange_shape()] * 2,
         [scratch],
     )(xa, xb, gain1, bias1, fwd_w)
-    arrived = exchange(sends)
 
     own = (expand_weight, expand_bias, reduce_weight)
     far = tuple(swap(part, "narrow", 2) for part in own)
     near = tuple(swap(part, "narrow", 1) for part in own)
     cross = tuple(swap(part, "narrow", 1) for part in far)
     chunks = (own, near, far, cross)
-    expand = jnp.concatenate([chunk[0] for chunk in chunks], axis=1)
-    expand_b = jnp.concatenate([chunk[1] for chunk in chunks]).astype(F32)
-    reduce = jnp.concatenate([chunk[2] for chunk in chunks], axis=0)
+    expand = [chunk[0] for chunk in chunks]
+    expand_b = jnp.stack([chunk[1] for chunk in chunks]).astype(F32)
+    reduce = [chunk[2] for chunk in chunks]
+    square = pl.BlockSpec(own[0].shape, lambda i: (0, 0), pipeline_mode=pl.Buffered(1))
 
     cot, cot_sums = call(
         functools.partial(cotangent_kernel, plan),
-        (units,),
+        (plan.steps,),
         [count_spec, plan.spec_a(), plan.spec_b()],
-        [plan.unit(), sums_spec],
-        [plan.units_shape(BF16), sums_shape],
+        [plan.rows(), sums_spec],
+        [plan.rows_shape(BF16), sums_shape],
         [scratch],
     )(counts, ca, cb)
-    cot_rows = cot.reshape(units * tokens, local)
-    grad_hidden = dot_t(cot_rows, reduce).astype(BF16)
+    block_shape = jax.ShapeDtypeStruct((2 * half, 2 * half), BF16)
+    block_spec = pl.BlockSpec((2 * half, 2 * half), lambda: (0, 0))
+    *ones, two0, two1 = call(
+        functools.partial(weights_kernel, plan),
+        (),
+        [whole(inner_weight), whole(outer_weight)],
+        [block_spec] * 4,
+        [block_shape] * 4,
+    )(inner_weight, outer_weight)
+    twos = (two0, two1)
 
     table = []
     for offsets, height, rows, padded in (
@@ -1020,8 +1284,7 @@
         line, valid = row_slots(offsets, rows, width)
         table.append(jnp.stack(halves(row_table(height, line, valid, padded))))
     row_tables = (table[0], table[1], table[0][0].T, table[1][0].T)
-    ones = [half_weight(inner_weight, h, blocks) for h in range(2)]
-    twos = [half_weight(outer_weight, h, blocks) for h in range(2)]
+    arrived = exchange([sends[0], hold(sends[1], *ones, cot, *row_tables, far[0], far[2])])
     shift1 = inner_bias.astype(F32).reshape(2, 2, half)
     shift2 = outer_bias.astype(F32).reshape(2, 2, half)
     points_shape = jax.ShapeDtypeStruct((plan.points, 2 * half), BF16)
@@ -1034,7 +1297,7 @@
     ]
     steps = 5 if plan.points % 80 == 0 else 1
     kept, outgoing = [], []
-    ready = ((far[0], far[2], cot), (expand, reduce))
+    ready = ((), (near[0], near[2], cross[0], cross[2], expand_b))
     for h in range(2):
         operands = (
             arrived[h],
@@ -1056,101 +1319,80 @@
         outgoing.append(got[0])
         kept.append(got[1:])
     returned = exchange(outgoing)
-
-    middle, normed = call(
+    grad_hidden = call(
+        hidden_kernel,
+        (plan.steps,),
+        [plan.rows()] + [square] * 4,
+        plan.chunks(),
+        plan.chunks_shape(),
+        after=1,
+    )(cot, *reduce, returned[0])
+
+    (
+        middle, rows, hidden, grad_pre, dmid, send, norm2_sums, shift_sums
+    ) = call(
         functools.partial(middle_kernel, plan),
-        (units,),
+        (plan.steps,),
         [plan.spec_a(), plan.spec_b(), plan.sends(), plan.sends()]
         + [vector] * 4
-        + [plan.table((tokens, depth))],
-        [plan.unit(), plan.unit()],
-        [plan.units_shape(F32), plan.units_shape(BF16)],
+        + [plan.table((tokens, depth)), plan.table((depth, tokens))]
+        + [square] * 4
+        + [
+            pl.BlockSpec(expand_b.shape, lambda i: (0, 0)),
+            plan.chunks(),
+            plan.rows(),
+        ],
+        [
+            plan.rows(),
+            plan.rows(),
+            plan.chunks(),
+            plan.chunks(),
+            plan.rows(),
+            plan.full_sends(),
+            sums_spec,
+            pl.BlockSpec((NARROW, PAD, local), lambda i: (0, 0, 0)),
+        ],
+        [
+            plan.rows_shape(F32),
+            plan.rows_shape(BF16),
+            plan.chunks_shape(),
+            plan.chunks_shape(),
+            plan.rows_shape(F32),
+            plan.full_shape(),
+            sums_shape,
+            jax.ShapeDtypeStruct((NARROW, PAD, local), F32),
+        ],
         [scratch],
-        after=1,
-    )(xa, xb, *returned, gain1, bias1, gain2, bias2, inv_w, grad_hidden)
-    rows = normed.reshape(units * tokens, local)
-    pre = dot(rows, expand) + expand_b
-    cdf = 0.5 * (1.0 + lax.erf(pre * ROOT_HALF))
-    hidden = (pre * cdf).astype(BF16)
-    slope = cdf + pre * jnp.exp(-0.5 * pre * pre) / ROOT_TWO_PI
-    grad_pre = (grad_hidden.astype(F32) * slope).astype(BF16)
-    grad_rows = dot_t(grad_pre, expand).astype(BF16)
-
-    dmid, send0, send1, norm2_sums = call(
-        functools.partial(middle_back_kernel, plan),
-        (units,),
-        [plan.unit(), plan.unit(), plan.unit(), vector, plan.table((depth, tokens))],
-        [plan.unit(), plan.sends(), plan.sends(), sums_spec],
-        [plan.units_shape(F32), plan.exchange_shape(), plan.exchange_shape(), sums_shape],
-    )(grad_rows.reshape(units, tokens, local), middle, cot, gain2, inv_w_t)
-    arrived = exchange((send0, send1))
-
-    hidden_units = hidden.reshape(units, tokens, -1)
-    hidden_size = hidden.shape[-1]
-    over_tokens = (((0,), (0,)), ((), ()))
-    grad_reduce = lax.dot_general(hidden, cot_rows, over_tokens, preferred_element_type=F32)
-    grad_expand = lax.dot_general(rows, grad_pre, over_tokens, preferred_element_type=F32)
-    grad_expand_b = jnp.sum(grad_pre.astype(F32), 0)
-    own_units = hidden_size // 4
-    shares = [
-        (
-            grad_reduce[k * own_units : (k + 1) * own_units],
-            grad_expand[:, k * own_units : (k + 1) * own_units],
-        )
-        for k in range(4)
-    ]
-
-    def add_from(target, source, distance):
-        return tuple(
-            t + swap(s.astype(BF16), "narrow", distance).astype(F32)
-            for t, s in zip(target, source, strict=True)
-        )
-
-    outgoing, products, backs = [], ([], []), []
-    for h in range(2):
-        zed, act, slope1, slope2, _ = kept[h]
-        operands = (
-            arrived[h],
-            *row_tables,
-            ones[h],
-            twos[h],
-            slope1,
-            slope2,
-            zed,
-        )
-        out, grad1, grad2, sums = call(
-            functools.partial(spectral_back_kernel, plan, steps),
-            (),
-            [whole(item) for item in operands],
-            [exchange_spec, points_spec, points_spec, pl.BlockSpec((PAD, 2 * half), lambda: (0, 0))],
-            [
-                plan.exchange_shape(),
-                points_shape,
-                points_shape,
-                jax.ShapeDtypeStruct((PAD, 2 * half), F32),
-            ],
-            parts_scratch,
-        )(*operands)
-        outgoing.append(out)
-        backs.append(sums)
-        for index, (left, right) in enumerate(((zed, grad1), (act, grad2))):
-            products[index].append(
-                lax.dot_general(left, right, over_tokens, preferred_element_type=F32)
-            )
-    returned = exchange(outgoing)
+        limit=60,
+    )(
+        xa, xb, *returned, gain1, bias1, gain2, bias2, inv_w, inv_w_t, *expand, expand_b,
+        grad_hidden, cot,
+    )
+    place = jnp.stack([myself, lax.axis_index("narrow")])
+    row_link = ("wide", 1)
+    axes = ("wide", "narrow")
+
+    def over(value, link):
+        return swap(value, *link)
+
+    def at(link):
+        return axes.index(link[0]), link[1]
+
+    core_link, column_link = ("narrow", 1), ("narrow", 2)
+    reduce_got = over(products(plan, hidden, cot, 1, True), core_link)
+    expand_got = over(products(plan, grad_pre, rows, 1, False), core_link)
+    reduce_keep, reduce_send = products(plan, hidden, cot, 0, True, reduce_got)
+    expand_keep, expand_send = products(plan, grad_pre, rows, 0, False, expand_got)
+    reduce_got = over(reduce_send, column_link)
+    expand_got = over(expand_send, column_link)
+    (arrived,) = exchange([send])
+
     mixed_a, mixed_b, norm1_sums = call(
         functools.partial(mixed_kernel, plan),
-        (units,),
-        [
-            count_spec,
-            plan.unit(hidden_size),
-            pl.BlockSpec((hidden_size, local), lambda i: (0, 0)),
-            vector,
-            plan.unit(),
-            plan.unit(),
-            plan.spec_a(),
-            plan.spec_b(),
-        ],
+        (plan.steps,),
+        [count_spec, plan.chunks()]
+        + [square] * 4
+        + [vector, plan.rows(), plan.rows(), plan.spec_a(), plan.spec_b()],
         [*plan.outs(), sums_spec],
         [
             jax.ShapeDtypeStruct(field_a.shape, BF16),
@@ -1159,38 +1401,55 @@
         ],
         [scratch],
         after=1,
-    )(counts, hidden_units, reduce, reduce_bias.astype(F32)[None], middle, dmid, xa, xb, grad1)
-    sum_own = add_from(shares[0], shares[1], 1)
-    sum_far = add_from(shares[2], shares[3], 1)
-    sum_own = add_from(sum_own, sum_far, 2)
-    wide_links = [("wide", d) for d in powers(width)]
-    mlp_sums = add_up(jnp.concatenate(sum_own), wide_links, BF16).astype(F32)
-
-
-    grad_a, grad_b = call(
-        functools.partial(last_kernel, plan),
-        (units,),
-        [plan.spec_a(), plan.spec_b(), plan.sends(), plan.sends(), plan.unit(), vector]
-        + [plan.table((tokens, depth))],
-        plan.outs(),
-        [
-            jax.ShapeDtypeStruct(field_a.shape, F32),
-            jax.ShapeDtypeStruct(field_b.shape, F32),
-        ],
-        [scratch],
-    )(xa, xb, *returned, dmid, gain1, fwd_w_t)
-
-    place = jnp.stack([myself, lax.axis_index("narrow")])
+    )(
+        counts, hidden, *reduce, reduce_bias.astype(F32)[None], middle, dmid, xa, xb,
+        reduce_send,
+    )
+    backs = []
+    back_shape = jax.ShapeDtypeStruct((PAD, 2 * half), F32)
+    weight_sums, pairs = ([], []), []
+    over_points = (((0,), (0,)), ((), ()))
+    for h in range(2):
+        zed, act, slope1, slope2, _ = kept[h]
+        operands = (*row_tables, ones[h], twos[h], slope1, slope2, zed)
+        block = pl.BlockSpec((width, units, plan.piece, half), lambda i, h=h: (0, 0, 0, h))
+        earlier = [mixed_a, expand_send] if h == 0 else [outgoing]
+        outgoing, grad1, grad2, sums = pl.pallas_call(
+            functools.partial(spectral_back_kernel, plan, steps, len(earlier)),
+            grid=(1,),
+            in_specs=[block]
+            + [whole(item) for item in operands]
+            + [pl.BlockSpec(memory_space=pl.ANY)] * len(earlier),
+            out_specs=[block] + [whole(points_shape)] * 2 + [whole(back_shape)],
+            out_shape=[plan.full_shape(), points_shape, points_shape, back_shape],
+            input_output_aliases={1 + len(operands): 0} if h else {},
+            scratch_shapes=parts_scratch,
+            compiler_params=pltpu.CompilerParams(vmem_limit_bytes=60 * MIB),
+        )(arrived, *operands, *earlier)
+        backs.append(sums)
+        pairs.append(((zed, grad1), (act, grad2)))
+    for h in range(2):
+        for index, (left, right) in enumerate(pairs[h]):
+            if h == 0:
+                right = hold(right, outgoing)
+            weight_sums[index].append(
+                lax.dot_general(left, right, over_points, preferred_element_type=F32)
+            )
+    reduce_sum_own, expand_sum_own = add_pairs(
+        place, (reduce_keep, expand_keep), (reduce_got, expand_got), outgoing
+    )
+    reduce_sum, expand_sum = lax.psum((reduce_sum_own, expand_sum_own), "wide")
+
     flat = (
-        *products[0],
-        *products[1],
+        *weight_sums[0],
+        *weight_sums[1],
         *backs,
         kept[0][4],
         kept[1][4],
         norm2_sums,
         cot_sums,
         norm1_sums,
-        grad_expand_b.reshape(4, -1),
+        shift_sums,
         gain1,
         bias1,
     )
@@ -1200,36 +1459,59 @@
             plan, place, (refs[0:2], refs[2:4]), refs[4:6], refs[6:8], *refs[8:]
         )
 
-    links = [("narrow", d) for d in powers(4)] + wide_links
-    rows = round_up(4 * BS + 13, 8 << len(links))
-    pack = call(
+    pack_links = (core_link, column_link, row_link)
+    pack_rows = round_up(4 * BS + 13, 8 << (len(pack_links) + 1)) // 2
+    pack_half = jax.ShapeDtypeStruct((pack_rows, local), F32)
+    pack_keep, pack_send = call(
         pack_body,
         (),
         [count_spec] + [whole(item) for item in flat],
-        pl.BlockSpec((rows, local), lambda: (0, 0)),
-        jax.ShapeDtypeStruct((rows, local), F32),
+        [pl.BlockSpec((pack_rows, local), lambda: (0, 0))] * 2,
+        [pack_half] * 2,
+        [pltpu.VMEM((2 * pack_rows, local), F32)],
     )(place, *flat)
-    pack = add_up(pack, links, F32)
-    matrices = pack[: 4 * BS].reshape(2, 2, BS, local)
-    small = pack[4 * BS : 4 * BS + 13]
+    for link in pack_links[1:]:
+        before = pack_links[pack_links.index(link) - 1]
+        pack_keep, pack_send = fold(place, at(link), pack_keep, over(pack_send, before))
+    pack = total(place, (pack_keep, over(pack_send, pack_links[-1])))
+    (returned,) = exchange([outgoing])
+    pack = hold(pack, returned)
+    layers = [over(pack, ("wide", 2 * k)) for k in range(1, width // 2)]
+
+    grad_a, grad_b = call(
+        functools.partial(last_kernel, plan),
+        (plan.steps,),
+        [plan.spec_a(), plan.spec_b(), plan.full_sends(), plan.rows(), vector]
+        + [plan.table((tokens, depth))],
+        plan.flat_outs(),
+        [
+            jax.ShapeDtypeStruct((plan.rows_a, plan.columns_a, 1, local), F32),
+            jax.ShapeDtypeStruct((plan.rows_b, plan.columns_b, 1, local), F32),
+        ],
+        [scratch],
+    )(xa, xb, returned, dmid, gain1, fwd_w_t)
+
+    pack = total(place, [pack] + layers, grad_a, kind=BF16)
+    for link in pack_links[:0:-1]:
+        pack = join(place, at(link), pack, over(pack, link))
+    inner_grad, outer_grad, small = last_join(place, at(core_link), pack, over(pack, core_link))
     own_row = lax.dynamic_slice_in_dim(small, 9 + place[1], 1)[0]
-    own_depth = mlp_sums.shape[0] // 2
     return (
         mixed_a,
         mixed_b,
-        grad_a,
-        grad_b,
+        grad_a.transpose(0, 2, 1, 3),
+        grad_b.transpose(0, 2, 1, 3),
         small[7],
         small[8],
-        matrices[0],
+        inner_grad,
         small[0:2],
-        matrices[1],
+        outer_grad,
         small[2:4],
         small[4],
         small[5],
-        mlp_sums[own_depth:],
+        expand_sum.astype(F32),
         own_row,
-        mlp_sums[:own_depth],
+        reduce_sum.astype(F32),
         small[6],
     )
 

time: 770 us -> 666 us (0.86)
  matrix products: 133 us -> 15.7 us
  Pallas kernels: 164 us -> 269 us
  local copies, waits for them, and re-layouts: 96.1 us -> 34.7 us
  other arithmetic: 44.6 us -> 9.94 us
  between operations: 4.3 us -> 17.5 us
  starting transfers between devices: 65.7 us -> 56.6 us
    dot_general x9 -> x4, matrix products: 133 us -> 15.7 us  [fast_device(): lax.dot_general(left, right, over_points, preferred_element_type=F32)]
    pallas_call x9 -> x26, Pallas kernels: 137 us -> 242 us  [the longest x1 59.8 us: fast_device(): call(functools.partial(middle_kernel, plan), (plan.steps,), [plan.spec_a(...]
    ppermute x31 -> x22, waiting for transfers between devices: 157 us -> 102 us  [swap(): return lax.ppermute(value, axis, [(i, i ^ distance) for i in range(size)])]
    all_to_all x8 -> x6, waiting for transfers between devices: 91.5 us -> 124 us  [exchange(): return [lax.all_to_all(part, 'wide', 0, 0, tiled=True) for part in parts]]
    psum x0 -> x1, waiting for transfers between devices: none -> 28.5 us  [fast_device(): reduce_sum, expand_sum = lax.psum((reduce_sum_own, expand_sum_own), 'wide')]
    slice x9 -> x0, local copies, waits for them, and re-layouts: 16 us -> none  [the longest x2 4.63 us: half_weight(): wide[1]]
    unnamed x112 -> x84, local copies, waits for them, and re-layouts: 31.3 us -> 15.4 us
    add x9 -> x0, other arithmetic: 11.2 us -> none  [the longest x7 6.22 us: add_up(): value = keep + swap(send.astype(kind), axis, distance).astype(F32)]
  transfers between devices with their start and end apart: 39 -> 29, of which waited for: 17 -> 18; matrix products, arithmetic and copies ran while one was open for 26% -> 6% of each run, Pallas kernels for 13% -> 25%
where the time goes in v2:
time: 666 us; the launch traced here: 658 us
  Pallas kernels  269 us (40%)
  waiting for transfers between devices  255 us (38%)
  starting transfers between devices  56.6 us (8%)
  local copies, waits for them, and re-layouts  34.7 us (5%)
  between operations  17.5 us (3%)
  matrix products  15.7 us (2%)
  other arithmetic  9.94 us (1%)
    all_to_all x6, waiting for transfers between devices, exchange(): return [lax.all_to_all(part, 'wide', 0, 0, tiled=True) for part in parts]  124 us
    ppermute x22, waiting for transfers between devices, swap(): return lax.ppermute(value, axis, [(i, i ^ distance) for i in range(size)])  102 us
    pallas_call x1, Pallas kernels, fast_device(): call(functools.partial(middle_kernel, plan), (plan.steps,), [plan.spec_a(...  59.8 us
    all_to_all x6, starting transfers between devices, exchange(): return [lax.all_to_all(part, 'wide', 0, 0, tiled=True) for part in parts]  38.8 us
    psum x1, waiting for transfers between devices, fast_device(): reduce_sum, expand_sum = lax.psum((reduce_sum_own, expand_sum_own), 'wide')  28.5 us
    pallas_call x2, Pallas kernels, fast_device(): pl.pallas_call(functools.partial(spectral_back_kernel, plan, steps, len(e...  26.8 us
    pallas_call x2, Pallas kernels, products(): call(kernel, (2,), [chunk, flat, each], [whole_out] * 2, [one] * 2)  26.7 us
    pallas_call x2, Pallas kernels, fast_device(): call(functools.partial(spectral_kernel, plan, steps), (), [whole(item) fo...  26.2 us
  transfers between devices with their start and end apart: 29, of which 18 were waited for; matrix products, arithmetic and copies ran while one was open for 6% of the time, Pallas kernels for 25%

profile of v2, /device:TPU:0, one launch (start us, length us, event | category | flops | bytes accessed | tf_op | source)
XLA Modules:
  0.0 657.8 jit_solution(3682524116768266654)
XLA Ops:
  9.7 11.9 %shard_map.333 = (bf16[8,15,24,384]{3,2,1,0:T(8,128)(2,1)}, bf16[8,15,24,384]{3,2,1,0:T(8,128)(2,1)}) custom-call(bf16[12,180,768]{2,1,0:T(8,128)(2,1)} %bitcast.56, bf16[6,90,768]{2,1,0:T(8,128)(2,1)} %bitcast.60, f32[1,768]{1,0:T(1,128)} %reshape.692.refs_2_.refs_4_.refs_13_, f32[1,768]{1,0:T(1,128)} %reshape.693.refs_3_.refs_5_.refs_14_, ...), custom_call_target="tpu_custom_call" | custom-call | tf_op jit(solution)/shard_map/pallas_call | solution.py:1241
  21.6 7.4 %all-to-all-start = ((bf16[8,15,24,384]{3,2,1,0:T(8,128)(2,1)}), bf16[8,15,24,384]{3,2,1,0:T(8,128)(2,1)S(1)}, u32[]{:S(2)}, u32[]{:S(2)}) async-start(bf16[8,15,24,384]{3,2,1,0:T(8,128)(2,1)} %get-tuple-element.72), calls=%async_computation | async-start | bytes 4423680 | tf_op jit(solution)/shard_map/all_to_all | solution.py:1239
  29.0 1.5 collective-permute-start.1
  32.4 1.7 copy.61
  34.1 1.8 reshape.684
  35.9 1.7 copy.62
  44.8 3.6 shard_map.334
  52.2 6.1 shard_map.336
  59.7 22.3 %collective-permute-done.refs_8_.refs_12_ = bf16[768,768]{1,0:T(8,128)(2,1)} collective-permute-done((bf16[768,768]{1,0:T(8,128)(2,1)}, bf16[768,768]{1,0:T(8,128)(2,1)}, u32[]{:S(2)}, u32[]{:S(2)}) %collective-permute-start) | collective-permute-done | bytes 1179680 | tf_op jit(solution)/shard_map/ppermute | solution.py:1181
  82.0 5.7 all-to-all-start.2
  89.0 13.1 %shard_map.335 = (bf16[8,15,24,384]{3,2,1,0:T(8,128)(2,1)}, bf16[1440,768]{1,0:T(8,128)(2,1)}, bf16[1440,768]{1,0:T(8,128)(2,1)}, bf16[1440,768]{1,0:T(8,128)(2,...) custom-call(bf16[8,15,24,384]{3,2,1,0:T(8,128)(2,1)} %copy-done.7, ...), custom_call_target="tpu_custom_call" | custom-call | tf_op jit(solution)/shard_map/pallas_call | solution.py:1310
  102.1 35.0 %all-to-all-done.2.refs_0_ = bf16[8,15,24,384]{3,2,1,0:T(8,128)(2,1)} async-done(((bf16[8,15,24,384]{3,2,1,0:T(8,128)(2,1)}), bf16[8,15,24,384]{3,2,1,0:T(8,128)(2,1)}, u32[]{:S(2)}, u32[]{:S(2)}) %all-to-all-start.2) | async-done | bytes 2211872 | tf_op jit(solution)/shard_map/all_to_all | solution.py:1239
  137.1 4.1 all-to-all-start.1
  142.2 1.5 collective-permute-start.7
  143.8 2.1 collective-permute-done.7
  145.8 1.6 collective-permute-done.6
  151.9 13.1 %shard_map.338 = (bf16[8,15,24,384]{3,2,1,0:T(8,128)(2,1)}, bf16[1440,768]{1,0:T(8,128)(2,1)}, bf16[1440,768]{1,0:T(8,128)(2,1)}, bf16[1440,768]{1,0:T(8,128)(2,...) custom-call(bf16[8,15,24,384]{3,2,1,0:T(8,128)(2,1)} %all-to-all-done.2.refs_0_, ...), custom_call_target="tpu_custom_call" | custom-call | tf_op jit(solution)/shard_map/pallas_call | solution.py:1310
  165.0 27.0 %all-to-all-done.1.refs_5_.refs_2_ = bf16[8,15,24,384]{3,2,1,0:T(8,128)(2,1)S(1)} async-done(((bf16[8,15,24,384]{3,2,1,0:T(8,128)(2,1)}), bf16[8,15,24,384]{3,2,1,0:T(8,128)(2,1)S(1)}, u32[]{:S(2)}, u32[]{:S(2)}) %all-to-all-start.1) | async-done | bytes 2211872 | tf_op jit(solution)/shard_map/all_to_all | solution.py:1239
  193.3 4.4 all-to-all-start.3
  198.9 19.2 %shard_map.339.refs_15_ = bf16[4,2880,768]{2,1,0:T(8,128)(2,1)} custom-call(bf16[2880,768]{1,0:T(8,128)(2,1)} %get-tuple-element.78.refs_3_.refs_0_.refs_16_.refs_1_, bf16[768,768]{1,0:T(8,128)(2,1)} %refs_2_.1, bf16[768,768]{1,0:T(8,128)(2,1)} %copy-done.3, bf16[768,768]{1,0:T(8,128)(2,1)} %copy-done.1, bf16[768,768]{1,0:T(8,128)(2,1)} %copy-done.4, ...), custom_call_target="tpu_custom_call" | custom-call | tf_op jit(solution)/shard_map/pallas_call | solution.py:1322
  218.1 29.8 %all-to-all-done.3.refs_3_ = bf16[8,15,24,384]{3,2,1,0:T(8,128)(2,1)} async-done(((bf16[8,15,24,384]{3,2,1,0:T(8,128)(2,1)}), bf16[8,15,24,384]{3,2,1,0:T(8,128)(2,1)}, u32[]{:S(2)}, u32[]{:S(2)}) %all-to-all-start.3) | async-done | bytes 2211872 | tf_op jit(solution)/shard_map/all_to_all | solution.py:1239
  248.0 59.8 %shard_map.340 = (f32[2880,768]{1,0:T(8,128)}, bf16[2880,768]{1,0:T(8,128)(2,1)}, bf16[4,2880,768]{2,1,0:T(8,128)(2,1)}, bf16[4,2880,768]{2,1,0:T(8,128)(2,1)}, ...) custom-call(bf16[12,180,768]{2,1,0:T(8,128)(2,1)} %bitcast.57, ...), custom_call_target="tpu_custom_call" | custom-call | tf_op jit(solution)/shard_map/pallas_call | solution.py:1333
  307.8 12.5 %all-to-all-start.4 = ((bf16[8,15,24,768]{3,2,1,0:T(8,128)(2,1)}), bf16[8,15,24,768]{3,2,1,0:T(8,128)(2,1)}, u32[]{:S(2)}, u32[]{:S(2)}) async-start(bf16[8,15,24,768]{3,2,1,0:T(8,128)(2,1)} %get-tuple-element.87), calls=%async_computation.4 | async-start | bytes 8847360 | tf_op jit(solution)/shard_map/all_to_all | solution.py:1239
  320.3 12.5 %shard_map.344 = bf16[2,768,768]{2,1,0:T(8,128)(2,1)} custom-call(bf16[4,2880,768]{2,1,0:T(8,128)(2,1)} %get-tuple-element.94.refs_0_, bf16[2880,768]{1,0:T(8,128)(2,1)} %get-tuple-element.95.refs_1_), custom_call_target="tpu_custom_call" | custom-call | tf_op jit(solution)/shard_map/pallas_call | solution.py:835
  332.7 12.4 %shard_map.341 = bf16[2,768,768]{2,1,0:T(8,128)(2,1)} custom-call(bf16[4,2880,768]{2,1,0:T(8,128)(2,1)} %get-tuple-element.81.refs_0_.refs_1_, bf16[2880,768]{1,0:T(8,128)(2,1)} %get-tuple-element.78.refs_3_.refs_0_.refs_16_.refs_1_), custom_call_target="tpu_custom_call" | custom-call | tf_op jit(solution)/shard_map/pallas_call | solution.py:835
  347.6 13.4 %shard_map.345 = (bf16[768,768]{1,0:T(8,128)(2,1)}, bf16[768,768]{1,0:T(8,128)(2,1)}) custom-call(bf16[4,2880,768]{2,1,0:T(8,128)(2,1)} %get-tuple-element.94.refs_0_, bf16[2880,768]{1,0:T(8,128)(2,1)} %get-tuple-element.95.refs_1_, bf16[2,768,768]{2,1,0:T(8,128)(2,1)} %copy-done.13), custom_call_target="tpu_custom_call" | custom-call | tf_op jit(solution)/shard_map/pallas_call | solution.py:838
  362.4 13.4 %shard_map.342 = (bf16[768,768]{1,0:T(8,128)(2,1)}, bf16[768,768]{1,0:T(8,128)(2,1)}) custom-call(bf16[4,2880,768]{2,1,0:T(8,128)(2,1)} %get-tuple-element.81.refs_0_.refs_1_, bf16[2880,768]{1,0:T(8,128)(2,1)} %get-tuple-element.78.refs_3_.refs_0_.refs_16_.refs_1_, bf16[2,768,768]{2,1,0:T(8,128)(2,1)} %copy-done.12), custom_call_target="tpu_custom_call" | custom-call | tf_op jit(solution)/shard_map/pallas_call | solution.py:838
  375.8 25.9 %shard_map.343 = (bf16[12,1,180,768]{3,2,1,0:T(8,128)(2,1)}, bf16[6,1,90,768]{3,2,1,0:T(8,128)(2,1)}, f32[8,768]{1,0:T(8,128)}) custom-call(s32[2]{0:T(128)} %pad_add_fusion.refs_0_, bf16[4,2880,768]{2,1,0:T(8,128)(2,1)} %get-tuple-element.81.refs_0_.refs_1_, bf16[768,768]{1,0:T(8,128)(2,1)} %refs_2_.1, bf16[768,768]{1,0:T(8,128)(2,1)} %copy-done.3, ...), custom_call_target="tpu_custom_call" | custom-call | tf_op jit(solution)/shard_map/pallas_call | solution.py:1390
  401.7 15.9 %all-to-all-done.4.got = bf16[8,15,24,768]{3,2,1,0:T(8,128)(2,1)} async-done(((bf16[8,15,24,768]{3,2,1,0:T(8,128)(2,1)}), bf16[8,15,24,768]{3,2,1,0:T(8,128)(2,1)}, u32[]{:S(2)}, u32[]{:S(2)}) %all-to-all-start.4) | async-done | bytes 4423712 | tf_op jit(solution)/shard_map/all_to_all | solution.py:1239
  417.5 13.4 %shard_map.346 = (bf16[8,15,24,768]{3,2,1,0:T(8,128)(2,1)}, bf16[1440,768]{1,0:T(8,128)(2,1)}, bf16[1440,768]{1,0:T(8,128)(2,1)}, f32[8,768]{1,0:T(8,128)}) custom-call(bf16[8,15,24,768]{3,2,1,0:T(8,128)(2,1)} %all-to-all-done.4.got, bf16[2,192,192]{2,1,0:T(8,128)(2,1)} %pad_maximum_fusion.1.refs_1_.refs_4_.ta, ...), custom_call_target="tpu_custom_call" | custom-call | tf_op jit(solution)/shard_map/pallas_call | solution.py:1417
  430.9 13.4 %shard_map.347 = (bf16[8,15,24,768]{3,2,1,0:T(8,128)(2,1)}, bf16[1440,768]{1,0:T(8,128)(2,1)}, bf16[1440,768]{1,0:T(8,128)(2,1)}, f32[8,768]{1,0:T(8,128)}) custom-call(bf16[8,15,24,768]{3,2,1,0:T(8,128)(2,1)} %all-to-all-done.4.got, bf16[2,192,192]{2,1,0:T(8,128)(2,1)} %pad_maximum_fusion.1.refs_1_.refs_4_.ta, ...), custom_call_target="tpu_custom_call", output_to_operand_aliasing={{0}: (10, {})} | custom-call | tf_op jit(solution)/shard_map/pallas_call | solution.py:1417
  444.4 4.7 all-to-all-start.5
  449.4 1.6 collective-permute-start.21
  452.1 26.3 %collective-permute-done.21.refs_4_ = bf16[768,768]{1,0:T(8,128)(2,1)S(1)} collective-permute-done((bf16[768,768]{1,0:T(8,128)(2,1)S(1)}, bf16[768,768]{1,0:T(8,128)(2,1)S(1)}, u32[]{:S(2)}, u32[]{:S(2)}) %collective-permute-start.21) | collective-permute-done | bytes 1179680 | tf_op jit(solution)/shard_map/ppermute | solution.py:1181
  478.4 23.0 %collective-permute-done.20.refs_3_ = bf16[768,768]{1,0:T(8,128)(2,1)} collective-permute-done((bf16[768,768]{1,0:T(8,128)(2,1)S(1)}, bf16[768,768]{1,0:T(8,128)(2,1)}, u32[]{:S(2)}, u32[]{:S(2)}) %collective-permute-start.20) | collective-permute-done | bytes 1179680 | tf_op jit(solution)/shard_map/ppermute | solution.py:1181
  501.4 4.0 shard_map.360
  505.4 1.6 copy-done.9
  507.0 5.2 fusion.24.refs_2_
  512.3 3.5 fusion.23.refs_1_
  515.8 3.5 fusion.26.refs_4_
  519.3 3.5 fusion.25.refs_3_
  522.8 5.5 shard_map.351
  528.3 2.5 collective-permute-done.11.refs_2_
  531.6 2.4 shard_map.352
  534.0 1.5 collective-permute-start.12
  535.6 9.8 %collective-permute-done.12.refs_2_ = f32[128,768]{1,0:T(8,128)S(1)} collective-permute-done((f32[128,768]{1,0:T(8,128)}, f32[128,768]{1,0:T(8,128)S(1)}, u32[]{:S(2)}, u32[]{:S(2)}) %collective-permute-start.12) | collective-permute-done | bytes 393248 | tf_op jit(solution)/shard_map/ppermute | solution.py:1181
  546.1 2.2 shard_map.353
  548.4 1.7 collective-permute-start.13
  550.1 5.6 collective-permute-done.13.refs_2_
  556.3 1.7 shard_map.354.refs_0_
  558.1 16.1 %all-to-all-done.5.refs_2_.refs_1_ = bf16[8,15,24,768]{3,2,1,0:T(8,128)(2,1)} async-done(((bf16[8,15,24,768]{3,2,1,0:T(8,128)(2,1)}), bf16[8,15,24,768]{3,2,1,0:T(8,128)(2,1)}, u32[]{:S(2)}, u32[]{:S(2)}) %all-to-all-start.5) | async-done | bytes 4423712 | tf_op jit(solution)/shard_map/all_to_all | solution.py:1239
  574.2 3.1 collective-permute-start.15
  578.6 13.9 %shard_map.348 = (f32[12,180,1,768]{3,2,1,0:T(1,128)}, f32[6,90,1,768]{3,2,1,0:T(1,128)}) custom-call(bf16[12,180,768]{2,1,0:T(8,128)(2,1)} %bitcast.59, bf16[6,90,768]{2,1,0:T(8,128)(2,1)} %bitcast.63, bf16[8,15,24,768]{3,2,1,0:T(8,128)(2,1)} %all-to-all-done.5.refs_2_.refs_1_, f32[2880,768]{1,0:T(8,128)} %get-tuple-element.83.refs_8_.refs_3_, ...), custom_call_target="tpu_custom_call" | custom-call | tf_op jit(solution)/shard_map/pallas_call | solution.py:1481
  594.0 1.9 shard_map.356.refs_1_
  596.9 3.8 collective-permute-done.17.refs_2_
  601.3 1.7 shard_map.357.refs_1_
  603.0 1.5 collective-permute-start.18
  604.5 4.4 collective-permute-done.18.refs_2_
  609.5 1.9 shard_map.358.refs_1_
  611.4 28.5 %all-reduce.3.cloned.1.call-done = (bf16[768,768]{1,0:T(8,128)(2,1)}, bf16[768,768]{1,0:T(8,128)(2,1)}) async-done(((bf16[768,768]{1,0:T(8,128)(2,1)}, bf16[768,768]{1,0:T(8,128)(2,1)}), (bf16[768,768]{1,0:T(8,128)(2,1)}, bf16[768,768]{1,0:T(8,128)(2,1)})) %all-reduce.3.cloned.1.call-update) | async-done | bytes 2359312 | tf_op jit(solution)/shard_map/psum | solution.py:1441
  639.9 2.9 convert_element_type.153
  642.9 1.6 convert_element_type.154
  645.2 2.3 shard_map.359
  648.9 1.5 slice_reduce_fusion
  (162 shorter events, 38.2 us)
Async XLA Ops:
  21.6 9.4 %copy-start.31 = (s32[9]{0:T(128)S(1)}, s32[9]{0:T(128)}, u32[]{:S(2)}) copy-start(s32[9]{0:T(128)} %param.26) | copy-start | bytes 112
  21.6 16.0 %copy-start.32 = (s32[9]{0:T(128)S(1)}, s32[9]{0:T(128)}, u32[]{:S(2)}) copy-start(s32[9]{0:T(128)} %param.27) | copy-start | bytes 112
  21.6 60.4 %all-to-all-start = ((bf16[8,15,24,384]{3,2,1,0:T(8,128)(2,1)}), bf16[8,15,24,384]{3,2,1,0:T(8,128)(2,1)S(1)}, u32[]{:S(2)}, u32[]{:S(2)}) async-start(bf16[8,15,24,384]{3,2,1,0:T(8,128)(2,1)} %get-tuple-element.72), calls=%async_computation | async-start | bytes 4423680 | tf_op jit(solution)/shard_map/all_to_all | solution.py:1239
  29.0 30.7 %collective-permute-start.1 = (bf16[768,768]{1,0:T(8,128)(2,1)}, bf16[768,768]{1,0:T(8,128)(2,1)S(1)}, u32[]{:S(2)}, u32[]{:S(2)}) collective-permute-start(bf16[768,768]{1,0:T(8,128)(2,1)} %refs_2_.1), channel_id=1, source_target_pairs={{0,2},{1,3},{2,0},{3,1},{4,6},{5,7},{6,4},{7,5},{8,10},{9,11},{10,... | collective-permute-start | bytes 3538952 | tf_op jit(solution)/shard_map/ppermute | solution.py:1181
  30.5 51.5 %collective-permute-start = (bf16[768,768]{1,0:T(8,128)(2,1)}, bf16[768,768]{1,0:T(8,128)(2,1)}, u32[]{:S(2)}, u32[]{:S(2)}) collective-permute-start(bf16[768,768]{1,0:T(8,128)(2,1)} %refs_10_.1), channel_id=1, source_target_pairs={{0,2},{1,3},{2,0},{3,1},{4,6},{5,7},{6,4},{7,5},{8,10},{9,11},{10,... | collective-permute-start | bytes 3538952 | tf_op jit(solution)/shard_map/ppermute | solution.py:1181
  52.2 6.7 %copy-start.22 = (f32[1,192,192]{2,1,0:T(8,128)S(1)}, f32[1,192,192]{2,1,0:T(8,128)}, u32[]{:S(2)}) copy-start(f32[1,192,192]{2,1,0:T(8,128)} %copy.62) | copy-start | bytes 442372
  59.7 22.3 %copy-start.1 = (bf16[768,768]{1,0:T(8,128)(2,1)}, bf16[768,768]{1,0:T(8,128)(2,1)S(1)}, u32[]{:S(2)}) copy-start(bf16[768,768]{1,0:T(8,128)(2,1)S(1)} %collective-permute-done.1.refs_9_.refs_3_.refs_4_) | copy-start | bytes 3538948
  82.0 5.8 copy-start.33
  82.0 6.4 copy-start.34
  82.0 5.7 copy-start.7
  82.0 55.1 %all-to-all-start.2 = ((bf16[8,15,24,384]{3,2,1,0:T(8,128)(2,1)}), bf16[8,15,24,384]{3,2,1,0:T(8,128)(2,1)}, u32[]{:S(2)}, u32[]{:S(2)}) async-start(bf16[8,15,24,384]{3,2,1,0:T(8,128)(2,1)} %shard_map.337), calls=%async_computation.2 | async-start | bytes 4423680 | tf_op jit(solution)/shard_map/all_to_all | solution.py:1239
  137.1 4.6 copy-start.2
  137.1 5.2 copy-start.35
  137.1 54.9 %all-to-all-start.1 = ((bf16[8,15,24,384]{3,2,1,0:T(8,128)(2,1)}), bf16[8,15,24,384]{3,2,1,0:T(8,128)(2,1)S(1)}, u32[]{:S(2)}, u32[]{:S(2)}) async-start(bf16[8,15,24,384]{3,2,1,0:T(8,128)(2,1)} %get-tuple-element.75), calls=%async_computation.1 | async-start | bytes 4423680 | tf_op jit(solution)/shard_map/all_to_all | solution.py:1239
  141.2 8.6 %collective-permute-start.3 = (bf16[768,768]{1,0:T(8,128)(2,1)}, bf16[768,768]{1,0:T(8,128)(2,1)S(1)}, u32[]{:S(2)}, u32[]{:S(2)}) collective-permute-start(bf16[768,768]{1,0:T(8,128)(2,1)} %refs_2_.1), channel_id=1, source_target_pairs={{0,1},{1,0},{2,3},{3,2},{4,5},{5,4},{6,7},{7,6},{8,9},{9,8},{10,11... | collective-permute-start | bytes 3538952 | tf_op jit(solution)/shard_map/ppermute | solution.py:1181
  141.2 8.5 %collective-permute-start.2 = (bf16[768,768]{1,0:T(8,128)(2,1)}, bf16[768,768]{1,0:T(8,128)(2,1)S(1)}, u32[]{:S(2)}, u32[]{:S(2)}) collective-permute-start(bf16[768,768]{1,0:T(8,128)(2,1)} %refs_10_.1), channel_id=1, source_target_pairs={{0,1},{1,0},{2,3},{3,2},{4,5},{5,4},{6,7},{7,6},{8,9},{9,8},{10,11... | collective-permute-start | bytes 3538952 | tf_op jit(solution)/shard_map/ppermute | solution.py:1181
  141.7 8.0 %collective-permute-start.5 = (bf16[768,768]{1,0:T(8,128)(2,1)S(1)}, bf16[768,768]{1,0:T(8,128)(2,1)S(1)}, u32[]{:S(2)}, u32[]{:S(2)}) collective-permute-start(bf16[768,768]{1,0:T(8,128)(2,1)S(1)} %copy-done.2), channel_id=1, source_target_pairs={{0,1},{1,0},{2,3},{3,2},{4,5},{5,4},{6,7},{7,6},{8,9},{9,8},{10,11... | collective-permute-start | bytes 3538952 | tf_op jit(solution)/shard_map/ppermute | solution.py:1181
  141.8 8.0 %collective-permute-start.4 = (bf16[768,768]{1,0:T(8,128)(2,1)}, bf16[768,768]{1,0:T(8,128)(2,1)S(1)}, u32[]{:S(2)}, u32[]{:S(2)}) collective-permute-start(bf16[768,768]{1,0:T(8,128)(2,1)} %collective-permute-done.refs_8_.refs_12_), channel_id=1, source_target_pairs={{0,1},{1,0},{2,3},{3,2},{4,5},{5,4},{6,7},{7,6},{8,9},{9,8},{10,11... | collective-permute-start | bytes 3538952 | tf_op jit(solution)/shard_map/ppermute | solution.py:1181
  142.2 3.6 collective-permute-start.7
  145.8 1.6 collective-permute-start.6
  147.4 1.7 collective-permute-start.8
  149.8 1.0 copy-start.3
  149.8 1.4 copy-start.10
  149.8 1.7 copy-start.4
  149.8 2.1 copy-start.11
  192.0 1.4 copy-start
  192.0 5.7 copy-start.36
  192.0 6.3 copy-start.37
  193.3 54.6 %all-to-all-start.3 = ((bf16[8,15,24,384]{3,2,1,0:T(8,128)(2,1)}), bf16[8,15,24,384]{3,2,1,0:T(8,128)(2,1)}, u32[]{:S(2)}, u32[]{:S(2)}) async-start(bf16[8,15,24,384]{3,2,1,0:T(8,128)(2,1)} %get-tuple-element.80), calls=%async_computation.3 | async-start | bytes 4423680 | tf_op jit(solution)/shard_map/all_to_all | solution.py:1239
  307.8 109.7 %all-to-all-start.4 = ((bf16[8,15,24,768]{3,2,1,0:T(8,128)(2,1)}), bf16[8,15,24,768]{3,2,1,0:T(8,128)(2,1)}, u32[]{:S(2)}, u32[]{:S(2)}) async-start(bf16[8,15,24,768]{3,2,1,0:T(8,128)(2,1)} %get-tuple-element.87), calls=%async_computation.4 | async-start | bytes 8847360 | tf_op jit(solution)/shard_map/all_to_all | solution.py:1239
  332.7 13.5 %collective-permute-start.10 = (bf16[2,768,768]{2,1,0:T(8,128)(2,1)}, bf16[2,768,768]{2,1,0:T(8,128)(2,1)S(1)}, u32[]{:S(2)}, u32[]{:S(2)}) collective-permute-start(bf16[2,768,768]{2,1,0:T(8,128)(2,1)} %shard_map.344), channel_id=1, source_target_pairs={{0,1},{1,0},{2,3},{3,2},{4,5},{5,4},{6,7},{7,6},{8,9},{9,8},{10,11... | collective-permute-start | bytes 7077896 | tf_op jit(solution)/shard_map/ppermute | solution.py:1181
  332.7 12.9 %copy-start.38 = (bf16[768]{0:T(1024)(128)(2,1)S(1)}, bf16[768]{0:T(1024)(128)(2,1)}, u32[]{:S(2)}) copy-start(bf16[768]{0:T(1024)(128)(2,1)} %param.39) | copy-start | bytes 4612
  345.1 15.9 %collective-permute-start.9 = (bf16[2,768,768]{2,1,0:T(8,128)(2,1)}, bf16[2,768,768]{2,1,0:T(8,128)(2,1)S(1)}, u32[]{:S(2)}, u32[]{:S(2)}) collective-permute-start(bf16[2,768,768]{2,1,0:T(8,128)(2,1)} %shard_map.341), channel_id=1, source_target_pairs={{0,1},{1,0},{2,3},{3,2},{4,5},{5,4},{6,7},{7,6},{8,9},{9,8},{10,11... | collective-permute-start | bytes 7077896 | tf_op jit(solution)/shard_map/ppermute | solution.py:1181
  346.2 1.4 copy-start.13
  361.0 1.4 copy-start.12
  444.4 5.1 copy-start.17
  444.4 6.6 %copy-start.18 = (bf16[768,768]{1,0:T(8,128)(2,1)S(1)}, bf16[768,768]{1,0:T(8,128)(2,1)}, u32[]{:S(2)}) copy-start(bf16[768,768]{1,0:T(8,128)(2,1)} %get-tuple-element.84.refs_11_) | copy-start | bytes 3538948
  444.4 129.8 %all-to-all-start.5 = ((bf16[8,15,24,768]{3,2,1,0:T(8,128)(2,1)}), bf16[8,15,24,768]{3,2,1,0:T(8,128)(2,1)}, u32[]{:S(2)}, u32[]{:S(2)}) async-start(bf16[8,15,24,768]{3,2,1,0:T(8,128)(2,1)} %get-tuple-element.98.refs_1_.refs_5_), calls=%async_computation.5 | async-start | bytes 8847360 | tf_op jit(solution)/shard_map/all_to_all | solution.py:1239
  449.1 190.8 %all-reduce.3.cloned.1.call-start = ((), (), s32[]{:S(2)}) async-start(), calls=%async_computation.6 | async-start | bytes 4718592 | tf_op jit(solution)/shard_map/psum | solution.py:1441
  449.4 29.0 %collective-permute-start.21 = (bf16[768,768]{1,0:T(8,128)(2,1)S(1)}, bf16[768,768]{1,0:T(8,128)(2,1)S(1)}, u32[]{:S(2)}, u32[]{:S(2)}) collective-permute-start(bf16[768,768]{1,0:T(8,128)(2,1)S(1)} %copy-done.17), channel_id=1, source_target_pairs={{0,2},{1,3},{2,0},{3,1},{4,6},{5,7},{6,4},{7,5},{8,10},{9,11},{10,... | collective-permute-start | bytes 3538952 | tf_op jit(solution)/shard_map/ppermute | solution.py:1181
  451.0 50.4 %collective-permute-start.20 = (bf16[768,768]{1,0:T(8,128)(2,1)S(1)}, bf16[768,768]{1,0:T(8,128)(2,1)}, u32[]{:S(2)}, u32[]{:S(2)}) collective-permute-start(bf16[768,768]{1,0:T(8,128)(2,1)S(1)} %copy-done.18), channel_id=1, source_target_pairs={{0,2},{1,3},{2,0},{3,1},{4,6},{5,7},{6,4},{7,5},{8,10},{9,11},{10,... | collective-permute-start | bytes 3538952 | tf_op jit(solution)/shard_map/ppermute | solution.py:1181
  478.4 23.0 %copy-start.19 = (bf16[768,768]{1,0:T(8,128)(2,1)}, bf16[768,768]{1,0:T(8,128)(2,1)S(1)}, u32[]{:S(2)}) copy-start(bf16[768,768]{1,0:T(8,128)(2,1)S(1)} %collective-permute-done.21.refs_4_) | copy-start | bytes 3538948
  505.4 1.6 copy-start.9
  507.0 5.2 copy-start.5
  507.0 5.2 copy-start.8
  512.3 3.5 copy-start.15
  512.3 3.5 copy-start.16
  515.8 3.5 copy-start.6
  515.8 3.5 copy-start.14
  528.3 2.5 collective-permute-start.11
  530.8 0.9 copy-start.21
  534.0 11.4 %collective-permute-start.12 = (f32[128,768]{1,0:T(8,128)}, f32[128,768]{1,0:T(8,128)S(1)}, u32[]{:S(2)}, u32[]{:S(2)}) collective-permute-start(f32[128,768]{1,0:T(8,128)} %get-tuple-element.118), channel_id=1, source_target_pairs={{0,2},{1,3},{2,0},{3,1},{4,6},{5,7},{6,4},{7,5},{8,10},{9,11},{10,... | collective-permute-start | bytes 1179656 | tf_op jit(solution)/shard_map/ppermute | solution.py:1181
  545.4 0.7 copy-start.24
  548.4 7.3 %collective-permute-start.13 = (f32[64,768]{1,0:T(8,128)}, f32[64,768]{1,0:T(8,128)S(1)}, u32[]{:S(2)}, u32[]{:S(2)}) collective-permute-start(f32[64,768]{1,0:T(8,128)} %get-tuple-element.120), channel_id=1, source_target_pairs={{0,4},{4,0},{8,12},{12,8},{16,20},{20,16},{24,28},{28,24},{1,5},{5... | collective-permute-start | bytes 589832 | tf_op jit(solution)/shard_map/ppermute | solution.py:1181
  574.2 18.3 %collective-permute-start.14 = (f32[64,768]{1,0:T(8,128)}, f32[64,768]{1,0:T(8,128)S(1)}, u32[]{:S(2)}, u32[]{:S(2)}) collective-permute-start(f32[64,768]{1,0:T(8,128)} %shard_map.355.refs_1_), channel_id=1, source_target_pairs={{0,8},{4,12},{8,0},{12,4},{16,24},{20,28},{24,16},{28,20},{1,9},{5... | collective-permute-start | bytes 589832 | tf_op jit(solution)/shard_map/ppermute | solution.py:1181
  574.2 19.0 %collective-permute-start.15 = (f32[64,768]{1,0:T(8,128)}, f32[64,768]{1,0:T(8,128)S(1)}, u32[]{:S(2)}, u32[]{:S(2)}) collective-permute-start(f32[64,768]{1,0:T(8,128)} %shard_map.355.refs_1_), channel_id=1, source_target_pairs={{0,16},{4,20},{8,24},{12,28},{16,0},{20,4},{24,8},{28,12},{1,17},{... | collective-permute-start | bytes 589832 | tf_op jit(solution)/shard_map/ppermute | solution.py:1181
  577.3 15.9 %collective-permute-start.16 = (f32[64,768]{1,0:T(8,128)}, f32[64,768]{1,0:T(8,128)S(1)}, u32[]{:S(2)}, u32[]{:S(2)}) collective-permute-start(f32[64,768]{1,0:T(8,128)} %shard_map.355.refs_1_), channel_id=1, source_target_pairs={{0,24},{4,28},{8,16},{12,20},{16,8},{20,12},{24,0},{28,4},{1,25},{... | collective-permute-start | bytes 589832 | tf_op jit(solution)/shard_map/ppermute | solution.py:1181
  592.5 0.7 copy-start.27
  593.2 0.7 copy-start.29
  595.9 4.8 collective-permute-start.17
  603.0 5.9 collective-permute-start.18
  611.4 33.0 %collective-permute-start.19 = (bf16[256,768]{1,0:T(8,128)(2,1)}, bf16[256,768]{1,0:T(8,128)(2,1)S(1)}, u32[]{:S(2)}, u32[]{:S(2)}) collective-permute-start(bf16[256,768]{1,0:T(8,128)(2,1)} %shard_map.358.refs_1_), channel_id=1, source_target_pairs={{0,1},{1,0},{2,3},{3,2},{4,5},{5,4},{6,7},{7,6},{8,9},{9,8},{10,11... | collective-permute-start | bytes 1179656 | tf_op jit(solution)/shard_map/ppermute | solution.py:1181
  639.9 2.9 copy-start.20
  644.5 0.7 copy-start.23
  (4 other events, 2.7 us)
Sparse Core Ops, SparseCore 0:
  505.6 134.3 all-reduce.2

commit v3 on v2

--- a/solution.py
+++ b/solution.py
@@ -718,7 +718,8 @@
 def first_kernel(plan, xa, xb, gain, bias, table, out0, out1, scratch):
     step = pl.program_id(0)
     standard, _ = layer_norm(plan.load(step, xa, xb, scratch))
-    for u, part in enumerate(plan.parts(standard * gain[...] + bias[...])):
+    scale, shift = (ref[...].astype(F32).reshape(1, plan.local) for ref in (gain, bias))
+    for u, part in enumerate(plan.parts(standard * scale + shift)):
         high, low = halves(part)
         spectrum = dot(table[0, 0], high) + (dot(table[0, 0], low) + dot(table[0, 1], high))
         plan.put_sends(spectrum, u, (out0, out1))
@@ -928,16 +929,30 @@
     )
 
 
-def add_pairs(place, lefts, rights, *before):
-    count = len(lefts)
-
-    def kernel(_, *refs):
-        for k in range(count):
-            value = refs[k][...].astype(F32) + refs[count + k][...].astype(F32)
-            refs[2 * count + k][...] = value.astype(BF16)
-
-    shapes = [jax.ShapeDtypeStruct(item.shape, BF16) for item in lefts]
-    return flat_call(kernel, place, (*lefts, *rights), shapes, before)
+def both_fold(place, link, lefts, rights, *before):
+    rows, local = lefts[0].shape
+    half = jax.ShapeDtypeStruct((2, rows // 2, local), lefts[0].dtype)
+
+    def kernel(place, left0, left1, right0, right1, keep, send):
+        for k, (left, right) in enumerate(((left0, right0), (left1, right1))):
+            fold_kernel(link, place, left, right, keep.at[k], send.at[k])
+
+    return flat_call(kernel, place, (*lefts, *rights), (half, half), before)
+
+
+def corners(place, links, pieces, *before):
+    _, size, local = pieces[0].shape
+    shape = jax.ShapeDtypeStruct((4 * size, local), F32)
+
+    def kernel(place, *refs):
+        outer, inner = (bit_of(place, link) for link in links)
+        for k, piece in enumerate(refs[:4]):
+            start = 2 * (outer ^ (k % 2)) + (inner ^ (k // 2))
+            rows = pl.ds(pl.multiple_of(start * size, size), size)
+            for j, out in enumerate(refs[4:]):
+                out[rows, :] = piece[j].astype(F32)
+
+    return flat_call(kernel, place, pieces, (shape, shape), before)
 
 
 def total(place, parts, *before, kind=None):
@@ -976,7 +991,7 @@
     )[0]
 
 
-def last_join(place, link, mine, other):
+def last_join(place, link, mine, other, *before):
     size, local = mine.shape
 
     def kernel(place, mine, other, inner, outer, small, whole_pack):
@@ -1001,7 +1016,8 @@
         [spec(item) for item in shapes],
         shapes,
         [pltpu.VMEM((2 * size, local), F32)],
-    )(place, mine, other)
+        after=len(before),
+    )(place, mine, other, *before)
 
 
 def unpack(plan, got, part_a, part_b):
@@ -1227,6 +1243,7 @@
     rest = (forward - fine.astype(np.float64)).astype(jnp.bfloat16)
     fwd_w = jnp.asarray(np.stack([fine, rest], axis=1))
     vector = pl.BlockSpec((1, local), lambda i: (0, 0))
+    plain = pl.BlockSpec((local,), lambda i: (0,))
     sums_spec = pl.BlockSpec((PAD, local), lambda i: (0, 0))
     sums_shape = jax.ShapeDtypeStruct((PAD, local), F32)
     scratch = plan.scratch()
@@ -1241,11 +1258,11 @@
     sends = call(
         functools.partial(first_kernel, plan),
         (plan.steps,),
-        [plan.spec_a(), plan.spec_b(), vector, vector, plan.table((2, depth, tokens))],
+        [plan.spec_a(), plan.spec_b(), plain, plain, plan.table((2, depth, tokens))],
         [plan.sends(), plan.sends()],
         [plan.exchange_shape()] * 2,
         [scratch],
-    )(xa, xb, gain1, bias1, fwd_w)
+    )(xa, xb, first_gain, first_bias, fwd_w)
 
     own = (expand_weight, expand_bias, reduce_weight)
     far = tuple(swap(part, "narrow", 2) for part in own)
@@ -1369,7 +1386,7 @@
         grad_hidden, cot,
     )
     place = jnp.stack([myself, lax.axis_index("narrow")])
-    row_link = ("wide", 1)
+    row_link, low_link, high_link = ("wide", 1), ("wide", 2), ("wide", 4)
     axes = ("wide", "narrow")
 
     def over(value, link):
@@ -1405,6 +1422,15 @@
         counts, hidden, *reduce, reduce_bias.astype(F32)[None], middle, dmid, xa, xb,
         reduce_send,
     )
+    keep, send = both_fold(
+        place,
+        at(row_link),
+        (reduce_keep, expand_keep),
+        (reduce_got, expand_got),
+        mixed_a,
+    )
+    row_got = over(send, row_link)
+
     backs = []
     back_shape = jax.ShapeDtypeStruct((PAD, 2 * half), F32)
     weight_sums, pairs = ([], []), []
@@ -1413,7 +1439,7 @@
         zed, act, slope1, slope2, _ = kept[h]
         operands = (*row_tables, ones[h], twos[h], slope1, slope2, zed)
         block = pl.BlockSpec((width, units, plan.piece, half), lambda i, h=h: (0, 0, 0, h))
-        earlier = [mixed_a, expand_send] if h == 0 else [outgoing]
+        earlier = [keep] if h == 0 else [outgoing]
         outgoing, grad1, grad2, sums = pl.pallas_call(
             functools.partial(spectral_back_kernel, plan, steps, len(earlier)),
             grid=(1,),
@@ -1431,15 +1457,12 @@
     for h in range(2):
         for index, (left, right) in enumerate(pairs[h]):
             if h == 0:
-                right = hold(right, outgoing)
+                right = hold(right, sums)
             weight_sums[index].append(
                 lax.dot_general(left, right, over_points, preferred_element_type=F32)
             )
-    reduce_sum_own, expand_sum_own = add_pairs(
-        place, (reduce_keep, expand_keep), (reduce_got, expand_got), outgoing
-    )
-    reduce_sum, expand_sum = lax.psum((reduce_sum_own, expand_sum_own), "wide")
-
+    keep, send = fold(place, at(low_link), keep, row_got, sums)
+    outgoing = hold(outgoing, send)
     flat = (
         *weight_sums[0],
         *weight_sums[1],
@@ -1470,12 +1493,14 @@
         [pack_half] * 2,
         [pltpu.VMEM((2 * pack_rows, local), F32)],
     )(place, *flat)
-    for link in pack_links[1:]:
-        before = pack_links[pack_links.index(link) - 1]
-        pack_keep, pack_send = fold(place, at(link), pack_keep, over(pack_send, before))
+    pack_keep, pack_send = fold(place, at(column_link), pack_keep, over(pack_send, core_link))
+    pack_keep, pack_send = fold(place, at(row_link), pack_keep, over(pack_send, column_link))
+    keep, send = fold(place, at(high_link), keep, over(send, low_link), pack_send)
+    shared = total(place, (keep, over(send, high_link)))
+    high_got = over(shared, high_link)
+
     pack = total(place, (pack_keep, over(pack_send, pack_links[-1])))
     (returned,) = exchange([outgoing])
-    pack = hold(pack, returned)
     layers = [over(pack, ("wide", 2 * k)) for k in range(1, width // 2)]
 
     grad_a, grad_b = call(
@@ -1489,12 +1514,23 @@
             jax.ShapeDtypeStruct((plan.rows_b, plan.columns_b, 1, local), F32),
         ],
         [scratch],
-    )(xa, xb, returned, dmid, gain1, fwd_w_t)
-
+        after=2,
+    )(xa, xb, returned, dmid, gain1, fwd_w_t, pack, shared)
+
+    shared = join(place, at(high_link), shared, high_got, grad_a)
+    low_got = over(shared, low_link)
+    row_got = over(shared, row_link)
+    reduce_sum, expand_sum = corners(
+        place,
+        (at(row_link), at(low_link)),
+        (shared, row_got, low_got, over(low_got, row_link)),
+    )
     pack = total(place, [pack] + layers, grad_a, kind=BF16)
-    for link in pack_links[:0:-1]:
-        pack = join(place, at(link), pack, over(pack, link))
-    inner_grad, outer_grad, small = last_join(place, at(core_link), pack, over(pack, core_link))
+    pack = join(place, at(row_link), pack, over(pack, row_link), row_got)
+    pack = join(place, at(column_link), pack, over(pack, column_link), low_got)
+    inner_grad, outer_grad, small = last_join(
+        place, at(core_link), pack, over(pack, core_link), reduce_sum
+    )
     own_row = lax.dynamic_slice_in_dim(small, 9 + place[1], 1)[0]
     return (
         mixed_a,
@@ -1509,9 +1545,9 @@
         small[2:4],
         small[4],
         small[5],
-        expand_sum.astype(F32),
+        expand_sum,
         own_row,
-        reduce_sum.astype(F32),
+        reduce_sum,
         small[6],
     )
 

time: 666 us -> 650 us (0.976)
  waiting for transfers between devices: 255 us -> 232 us
  Pallas kernels: 269 us -> 283 us
  between operations: 17.5 us -> 3.84 us
    ppermute x22 -> x29, waiting for transfers between devices: 102 us -> 141 us  [swap(): return lax.ppermute(value, axis, [(i, i ^ distance) for i in range(size)])]
    all_to_all x6, waiting for transfers between devices: 124 us -> 90.6 us  [exchange(): return [lax.all_to_all(part, 'wide', 0, 0, tiled=True) for part in parts]]
    psum x1 -> x0, waiting for transfers between devices: 28.5 us -> none  [fast_device(): reduce_sum, expand_sum = lax.psum((reduce_sum_own, expand_sum_own), 'wide')]
    pallas_call x7 -> x12, Pallas kernels: 15.8 us -> 30.5 us  [flat_call(): call(kernel, (), [SMEM] + [spec(item) for item in operands], [spec(item)...]
    ppermute x22 -> x29, starting transfers between devices: 17.5 us -> 30.9 us  [swap(): return lax.ppermute(value, axis, [(i, i ^ distance) for i in range(size)])]
    all_to_all x6, starting transfers between devices: 38.8 us -> 31.1 us  [exchange(): return [lax.all_to_all(part, 'wide', 0, 0, tiled=True) for part in parts]]
    unnamed x84 -> x104, local copies, waits for them, and re-layouts: 15.4 us -> 21.2 us
  transfers between devices with their start and end apart: 29 -> 35, of which waited for: 18 -> 18; matrix products, arithmetic and copies ran while one was open for 6% -> 6% of each run, Pallas kernels for 25% -> 32%
where the time goes in v3:
time: 650 us; the launch traced here: 642 us
  Pallas kernels  283 us (44%)
  waiting for transfers between devices  232 us (36%)
  starting transfers between devices  62 us (10%)
  local copies, waits for them, and re-layouts  39.2 us (6%)
  matrix products  15.8 us (2%)
    ppermute x29, waiting for transfers between devices, swap(): return lax.ppermute(value, axis, [(i, i ^ distance) for i in range(size)])  141 us
    all_to_all x6, waiting for transfers between devices, exchange(): return [lax.all_to_all(part, 'wide', 0, 0, tiled=True) for part in parts]  90.6 us
    pallas_call x1, Pallas kernels, fast_device(): call(functools.partial(middle_kernel, plan), (plan.steps,), [plan.spec_a(...  59.8 us
    all_to_all x6, starting transfers between devices, exchange(): return [lax.all_to_all(part, 'wide', 0, 0, tiled=True) for part in parts]  31.1 us
    ppermute x29, starting transfers between devices, swap(): return lax.ppermute(value, axis, [(i, i ^ distance) for i in range(size)])  30.9 us
    pallas_call x12, Pallas kernels, flat_call(): call(kernel, (), [SMEM] + [spec(item) for item in operands], [spec(item)...  30.5 us
    pallas_call x2, Pallas kernels, fast_device(): pl.pallas_call(functools.partial(spectral_back_kernel, plan, steps, len(e...  26.8 us
    pallas_call x2, Pallas kernels, products(): call(kernel, (2,), [chunk, flat, each], [whole_out] * 2, [one] * 2)  26.7 us
  transfers between devices with their start and end apart: 35, of which 18 were waited for; matrix products, arithmetic and copies ran while one was open for 6% of the time, Pallas kernels for 32%

profile of v3, /device:TPU:0, one launch (start us, length us, event | category | flops | bytes accessed | tf_op | source)
XLA Modules:
  0.0 641.7 jit_solution(3137433914066575480)
XLA Ops:
  0.6 11.9 %shard_map.333 = (bf16[8,15,24,384]{3,2,1,0:T(8,128)(2,1)}, bf16[8,15,24,384]{3,2,1,0:T(8,128)(2,1)}) custom-call(bf16[12,180,768]{2,1,0:T(8,128)(2,1)} %bitcast.56, bf16[6,90,768]{2,1,0:T(8,128)(2,1)} %bitcast.61, bf16[768]{0:T(1024)(128)(2,1)} %refs_2_.2, bf16[768]{0:T(1024)(128)(2,1)} %refs_3_.1, bf16[2,2,192,192]{3,2,1,0:T(8,128)(2,1)} %constant.65.clone.refs_4_), custom_call_target="tpu_custom_call" | custom-call | tf_op jit(solution)/shard_map/pallas_call | solution.py:1258
  12.5 7.4 %all-to-all-start = ((bf16[8,15,24,384]{3,2,1,0:T(8,128)(2,1)}), bf16[8,15,24,384]{3,2,1,0:T(8,128)(2,1)S(1)}, u32[]{:S(2)}, u32[]{:S(2)}) async-start(bf16[8,15,24,384]{3,2,1,0:T(8,128)(2,1)} %get-tuple-element.78), calls=%async_computation | async-start | bytes 4423680 | tf_op jit(solution)/shard_map/all_to_all | solution.py:1256
  23.3 1.7 copy.61
  25.1 1.8 reshape.684
  26.8 1.7 copy.62
  35.7 3.6 shard_map.334
  43.2 6.1 shard_map.336
  50.6 22.3 %collective-permute-done.refs_8_.refs_12_ = bf16[768,768]{1,0:T(8,128)(2,1)} collective-permute-done((bf16[768,768]{1,0:T(8,128)(2,1)}, bf16[768,768]{1,0:T(8,128)(2,1)}, u32[]{:S(2)}, u32[]{:S(2)}) %collective-permute-start) | collective-permute-done | bytes 1179680 | tf_op jit(solution)/shard_map/ppermute | solution.py:1197
  73.0 5.7 all-to-all-start.2
  79.9 13.1 %shard_map.335 = (bf16[8,15,24,384]{3,2,1,0:T(8,128)(2,1)}, bf16[1440,768]{1,0:T(8,128)(2,1)}, bf16[1440,768]{1,0:T(8,128)(2,1)}, bf16[1440,768]{1,0:T(8,128)(2,...) custom-call(bf16[8,15,24,384]{3,2,1,0:T(8,128)(2,1)} %copy-done.8, ...), custom_call_target="tpu_custom_call" | custom-call | tf_op jit(solution)/shard_map/pallas_call | solution.py:1327
  93.1 35.0 %all-to-all-done.2.refs_0_ = bf16[8,15,24,384]{3,2,1,0:T(8,128)(2,1)} async-done(((bf16[8,15,24,384]{3,2,1,0:T(8,128)(2,1)}), bf16[8,15,24,384]{3,2,1,0:T(8,128)(2,1)}, u32[]{:S(2)}, u32[]{:S(2)}) %all-to-all-start.2) | async-done | bytes 2211872 | tf_op jit(solution)/shard_map/all_to_all | solution.py:1256
  128.0 4.3 all-to-all-start.1
  134.9 2.1 collective-permute-done.7
  143.1 13.1 %shard_map.338 = (bf16[8,15,24,384]{3,2,1,0:T(8,128)(2,1)}, bf16[1440,768]{1,0:T(8,128)(2,1)}, bf16[1440,768]{1,0:T(8,128)(2,1)}, bf16[1440,768]{1,0:T(8,128)(2,...) custom-call(bf16[8,15,24,384]{3,2,1,0:T(8,128)(2,1)} %all-to-all-done.2.refs_0_, ...), custom_call_target="tpu_custom_call" | custom-call | tf_op jit(solution)/shard_map/pallas_call | solution.py:1327
  156.1 27.0 %all-to-all-done.1.refs_5_.refs_2_ = bf16[8,15,24,384]{3,2,1,0:T(8,128)(2,1)S(1)} async-done(((bf16[8,15,24,384]{3,2,1,0:T(8,128)(2,1)}), bf16[8,15,24,384]{3,2,1,0:T(8,128)(2,1)S(1)}, u32[]{:S(2)}, u32[]{:S(2)}) %all-to-all-start.1) | async-done | bytes 2211872 | tf_op jit(solution)/shard_map/all_to_all | solution.py:1256
  184.5 4.4 all-to-all-start.3
  191.2 19.2 %shard_map.339.refs_15_ = bf16[4,2880,768]{2,1,0:T(8,128)(2,1)} custom-call(bf16[2880,768]{1,0:T(8,128)(2,1)} %get-tuple-element.84.refs_3_.refs_0_.refs_16_.refs_1_, bf16[768,768]{1,0:T(8,128)(2,1)} %refs_2_.3, bf16[768,768]{1,0:T(8,128)(2,1)} %copy-done.3, bf16[768,768]{1,0:T(8,128)(2,1)} %copy-done.1, bf16[768,768]{1,0:T(8,128)(2,1)} %copy-done.4, ...), custom_call_target="tpu_custom_call" | custom-call | tf_op jit(solution)/shard_map/pallas_call | solution.py:1339
  210.4 28.7 %all-to-all-done.3.refs_3_ = bf16[8,15,24,384]{3,2,1,0:T(8,128)(2,1)} async-done(((bf16[8,15,24,384]{3,2,1,0:T(8,128)(2,1)}), bf16[8,15,24,384]{3,2,1,0:T(8,128)(2,1)}, u32[]{:S(2)}, u32[]{:S(2)}) %all-to-all-start.3) | async-done | bytes 2211872 | tf_op jit(solution)/shard_map/all_to_all | solution.py:1256
  239.1 59.8 %shard_map.340 = (f32[2880,768]{1,0:T(8,128)}, bf16[2880,768]{1,0:T(8,128)(2,1)}, bf16[4,2880,768]{2,1,0:T(8,128)(2,1)}, bf16[4,2880,768]{2,1,0:T(8,128)(2,1)}, ...) custom-call(bf16[12,180,768]{2,1,0:T(8,128)(2,1)} %bitcast.57, ...), custom_call_target="tpu_custom_call" | custom-call | tf_op jit(solution)/shard_map/pallas_call | solution.py:1350
  298.9 4.8 all-to-all-start.4
  303.7 12.4 %shard_map.344 = bf16[2,768,768]{2,1,0:T(8,128)(2,1)} custom-call(bf16[4,2880,768]{2,1,0:T(8,128)(2,1)} %get-tuple-element.101.refs_0_, bf16[2880,768]{1,0:T(8,128)(2,1)} %get-tuple-element.102.refs_1_), custom_call_target="tpu_custom_call" | custom-call | tf_op jit(solution)/shard_map/pallas_call | solution.py:836
  316.1 12.4 %shard_map.341 = bf16[2,768,768]{2,1,0:T(8,128)(2,1)} custom-call(bf16[4,2880,768]{2,1,0:T(8,128)(2,1)} %get-tuple-element.87.refs_0_.refs_1_, bf16[2880,768]{1,0:T(8,128)(2,1)} %get-tuple-element.84.refs_3_.refs_0_.refs_16_.refs_1_), custom_call_target="tpu_custom_call" | custom-call | tf_op jit(solution)/shard_map/pallas_call | solution.py:836
  330.4 13.4 %shard_map.345 = (bf16[768,768]{1,0:T(8,128)(2,1)}, bf16[768,768]{1,0:T(8,128)(2,1)}) custom-call(bf16[4,2880,768]{2,1,0:T(8,128)(2,1)} %get-tuple-element.101.refs_0_, bf16[2880,768]{1,0:T(8,128)(2,1)} %get-tuple-element.102.refs_1_, bf16[2,768,768]{2,1,0:T(8,128)(2,1)} %copy-done.13), custom_call_target="tpu_custom_call" | custom-call | tf_op jit(solution)/shard_map/pallas_call | solution.py:839
  346.7 13.4 %shard_map.342 = (bf16[768,768]{1,0:T(8,128)(2,1)}, bf16[768,768]{1,0:T(8,128)(2,1)}) custom-call(bf16[4,2880,768]{2,1,0:T(8,128)(2,1)} %get-tuple-element.87.refs_0_.refs_1_, bf16[2880,768]{1,0:T(8,128)(2,1)} %get-tuple-element.84.refs_3_.refs_0_.refs_16_.refs_1_, bf16[2,768,768]{2,1,0:T(8,128)(2,1)} %copy-done.12), custom_call_target="tpu_custom_call" | custom-call | tf_op jit(solution)/shard_map/pallas_call | solution.py:839
  361.8 25.9 %shard_map.343 = (bf16[12,1,180,768]{3,2,1,0:T(8,128)(2,1)}, bf16[6,1,90,768]{3,2,1,0:T(8,128)(2,1)}, f32[8,768]{1,0:T(8,128)}) custom-call(s32[2]{0:T(128)} %pad_add_fusion.refs_0_, bf16[4,2880,768]{2,1,0:T(8,128)(2,1)} %get-tuple-element.87.refs_0_.refs_1_, bf16[768,768]{1,0:T(8,128)(2,1)} %refs_2_.3, bf16[768,768]{1,0:T(8,128)(2,1)} %copy-done.3, ...), custom_call_target="tpu_custom_call" | custom-call | tf_op jit(solution)/shard_map/pallas_call | solution.py:1407
  387.7 9.5 %collective-permute-done.11.refs_3_ = bf16[768,768]{1,0:T(8,128)(2,1)S(1)} collective-permute-done((bf16[768,768]{1,0:T(8,128)(2,1)}, bf16[768,768]{1,0:T(8,128)(2,1)S(1)}, u32[]{:S(2)}, u32[]{:S(2)}) %collective-permute-start.11) | collective-permute-done | bytes 1179680 | tf_op jit(solution)/shard_map/ppermute | solution.py:1197
  398.2 5.0 shard_map.346
  403.2 2.0 collective-permute-start.13
  405.1 13.4 %shard_map.347 = (bf16[8,15,24,768]{3,2,1,0:T(8,128)(2,1)}, bf16[1440,768]{1,0:T(8,128)(2,1)}, bf16[1440,768]{1,0:T(8,128)(2,1)}, f32[8,768]{1,0:T(8,128)}) custom-call(bf16[8,15,24,768]{3,2,1,0:T(8,128)(2,1)} %all-to-all-done.4.got, bf16[2,192,192]{2,1,0:T(8,128)(2,1)} %pad_maximum_fusion.1.refs_1_.refs_4_.ta, ...), custom_call_target="tpu_custom_call" | custom-call | tf_op jit(solution)/shard_map/pallas_call | solution.py:1443
  418.5 13.4 %shard_map.348 = (bf16[8,15,24,768]{3,2,1,0:T(8,128)(2,1)}, bf16[1440,768]{1,0:T(8,128)(2,1)}, bf16[1440,768]{1,0:T(8,128)(2,1)}, f32[8,768]{1,0:T(8,128)}) custom-call(bf16[8,15,24,768]{3,2,1,0:T(8,128)(2,1)} %all-to-all-done.4.got, bf16[2,192,192]{2,1,0:T(8,128)(2,1)} %pad_maximum_fusion.1.refs_1_.refs_4_.ta, ...), custom_call_target="tpu_custom_call", output_to_operand_aliasing={{0}: (10, {})} | custom-call | tf_op jit(solution)/shard_map/pallas_call | solution.py:1443
  433.0 3.7 shard_map.349
  436.6 4.6 all-to-all-start.5
  442.9 5.2 fusion.24.refs_2_
  448.1 3.5 fusion.23.refs_1_
  451.6 3.5 fusion.26.refs_4_
  455.1 3.6 fusion.25.refs_3_
  458.7 5.5 shard_map.353
  464.2 2.1 collective-permute-start.17
  467.6 2.4 shard_map.354
  471.5 9.8 %collective-permute-done.15.refs_2_ = f32[128,768]{1,0:T(8,128)S(1)} collective-permute-done((f32[128,768]{1,0:T(8,128)}, f32[128,768]{1,0:T(8,128)S(1)}, u32[]{:S(2)}, u32[]{:S(2)}) %collective-permute-start.15) | collective-permute-done | bytes 393248 | tf_op jit(solution)/shard_map/ppermute | solution.py:1197
  482.1 1.9 shard_map.355
  484.0 41.2 %collective-permute-done.17.refs_2_ = bf16[2,192,768]{2,1,0:T(8,128)(2,1)S(1)} collective-permute-done((bf16[2,192,768]{2,1,0:T(8,128)(2,1)S(1)}, bf16[2,192,768]{2,1,0:T(8,128)(2,1)S(1)}, u32[]{:S(2)}, u32[]{:S(2)}) %collective-permute-start.17) | collective-permute-done | bytes 589856 | tf_op jit(solution)/shard_map/ppermute | solution.py:1197
  526.1 2.5 shard_map.357
  528.6 3.9 collective-permute-start.18
  532.5 18.8 %collective-permute-done.18.refs_2_ = bf16[2,96,768]{2,1,0:T(8,128)(2,1)S(1)} collective-permute-done((bf16[2,96,768]{2,1,0:T(8,128)(2,1)}, bf16[2,96,768]{2,1,0:T(8,128)(2,1)S(1)}, u32[]{:S(2)}, u32[]{:S(2)}) %collective-permute-start.18) | collective-permute-done | bytes 294944 | tf_op jit(solution)/shard_map/ppermute | solution.py:1197
  552.0 1.8 shard_map.358.refs_7_.refs_1_
  555.3 4.2 collective-permute-done.16.refs_2_
  560.2 1.7 shard_map.356.refs_6_.refs_1_
  561.9 13.9 %shard_map.359 = (f32[12,180,1,768]{3,2,1,0:T(1,128)}, f32[6,90,1,768]{3,2,1,0:T(1,128)}) custom-call(bf16[12,180,768]{2,1,0:T(8,128)(2,1)} %bitcast.59, bf16[6,90,768]{2,1,0:T(8,128)(2,1)} %bitcast.64, bf16[8,15,24,768]{3,2,1,0:T(8,128)(2,1)} %all-to-all-done.5.refs_2_, f32[2880,768]{1,0:T(8,128)} %get-tuple-element.89.refs_8_.refs_3_, ...), custom_call_target="tpu_custom_call" | custom-call | tf_op jit(solution)/shard_map/pallas_call | solution.py:1506
  576.6 2.0 shard_map.361.refs_1_
  578.5 1.6 collective-permute-start.24
  580.2 2.7 collective-permute-start.26
  582.9 2.0 collective-permute-start.20
  585.0 2.3 collective-permute-start.21
  587.3 18.4 %collective-permute-done.19.refs_2_ = f32[64,768]{1,0:T(8,128)S(1)} collective-permute-done((f32[64,768]{1,0:T(8,128)S(1)}, f32[64,768]{1,0:T(8,128)S(1)}, u32[]{:S(2)}, u32[]{:S(2)}) %collective-permute-start.19) | collective-permute-done | bytes 196640 | tf_op jit(solution)/shard_map/ppermute | solution.py:1197
  605.7 2.4 collective-permute-done.21.refs_4_
  608.8 1.9 shard_map.360.refs_1_
  611.8 3.6 collective-permute-done.22.refs_2_
  616.9 1.7 shard_map.362.refs_1_
  621.3 3.2 collective-permute-done.25.refs_2_
  625.2 1.8 shard_map.363.refs_1_
  627.0 3.6 collective-permute-done.28.refs_4_
  631.4 4.1 shard_map.364
  636.2 2.3 shard_map.365
  (196 shorter events, 56.1 us)
Async XLA Ops:
  12.5 9.4 %copy-start.41 = (s32[9]{0:T(128)S(1)}, s32[9]{0:T(128)}, u32[]{:S(2)}) copy-start(s32[9]{0:T(128)} %param.26) | copy-start | bytes 112
  12.5 16.0 %copy-start.42 = (s32[9]{0:T(128)S(1)}, s32[9]{0:T(128)}, u32[]{:S(2)}) copy-start(s32[9]{0:T(128)} %param.27) | copy-start | bytes 112
  12.5 60.4 %all-to-all-start = ((bf16[8,15,24,384]{3,2,1,0:T(8,128)(2,1)}), bf16[8,15,24,384]{3,2,1,0:T(8,128)(2,1)S(1)}, u32[]{:S(2)}, u32[]{:S(2)}) async-start(bf16[8,15,24,384]{3,2,1,0:T(8,128)(2,1)} %get-tuple-element.78), calls=%async_computation | async-start | bytes 4423680 | tf_op jit(solution)/shard_map/all_to_all | solution.py:1256
  19.9 30.7 %collective-permute-start.1 = (bf16[768,768]{1,0:T(8,128)(2,1)}, bf16[768,768]{1,0:T(8,128)(2,1)S(1)}, u32[]{:S(2)}, u32[]{:S(2)}) collective-permute-start(bf16[768,768]{1,0:T(8,128)(2,1)} %refs_2_.3), channel_id=1, source_target_pairs={{0,2},{1,3},{2,0},{3,1},{4,6},{5,7},{6,4},{7,5},{8,10},{9,11},{10,... | collective-permute-start | bytes 3538952 | tf_op jit(solution)/shard_map/ppermute | solution.py:1197
  21.4 51.5 %collective-permute-start = (bf16[768,768]{1,0:T(8,128)(2,1)}, bf16[768,768]{1,0:T(8,128)(2,1)}, u32[]{:S(2)}, u32[]{:S(2)}) collective-permute-start(bf16[768,768]{1,0:T(8,128)(2,1)} %refs_10_.1), channel_id=1, source_target_pairs={{0,2},{1,3},{2,0},{3,1},{4,6},{5,7},{6,4},{7,5},{8,10},{9,11},{10,... | collective-permute-start | bytes 3538952 | tf_op jit(solution)/shard_map/ppermute | solution.py:1197
  43.2 6.7 %copy-start.24 = (f32[1,192,192]{2,1,0:T(8,128)S(1)}, f32[1,192,192]{2,1,0:T(8,128)}, u32[]{:S(2)}) copy-start(f32[1,192,192]{2,1,0:T(8,128)} %copy.62) | copy-start | bytes 442372
  50.6 22.3 %copy-start.1 = (bf16[768,768]{1,0:T(8,128)(2,1)}, bf16[768,768]{1,0:T(8,128)(2,1)S(1)}, u32[]{:S(2)}) copy-start(bf16[768,768]{1,0:T(8,128)(2,1)S(1)} %collective-permute-done.1.refs_9_.refs_3_.refs_4_) | copy-start | bytes 3538948
  72.9 5.8 copy-start.43
  72.9 6.4 copy-start.44
  73.0 5.7 copy-start.8
  73.0 55.1 %all-to-all-start.2 = ((bf16[8,15,24,384]{3,2,1,0:T(8,128)(2,1)}), bf16[8,15,24,384]{3,2,1,0:T(8,128)(2,1)}, u32[]{:S(2)}, u32[]{:S(2)}) async-start(bf16[8,15,24,384]{3,2,1,0:T(8,128)(2,1)} %shard_map.337), calls=%async_computation.2 | async-start | bytes 4423680 | tf_op jit(solution)/shard_map/all_to_all | solution.py:1256
  128.0 4.9 copy-start.2
  128.0 5.4 copy-start.45
  128.0 55.1 %all-to-all-start.1 = ((bf16[8,15,24,384]{3,2,1,0:T(8,128)(2,1)}), bf16[8,15,24,384]{3,2,1,0:T(8,128)(2,1)S(1)}, u32[]{:S(2)}, u32[]{:S(2)}) async-start(bf16[8,15,24,384]{3,2,1,0:T(8,128)(2,1)} %get-tuple-element.81), calls=%async_computation.1 | async-start | bytes 4423680 | tf_op jit(solution)/shard_map/all_to_all | solution.py:1256
  132.3 8.6 %collective-permute-start.3 = (bf16[768,768]{1,0:T(8,128)(2,1)}, bf16[768,768]{1,0:T(8,128)(2,1)S(1)}, u32[]{:S(2)}, u32[]{:S(2)}) collective-permute-start(bf16[768,768]{1,0:T(8,128)(2,1)} %refs_2_.3), channel_id=1, source_target_pairs={{0,1},{1,0},{2,3},{3,2},{4,5},{5,4},{6,7},{7,6},{8,9},{9,8},{10,11... | collective-permute-start | bytes 3538952 | tf_op jit(solution)/shard_map/ppermute | solution.py:1197
  132.4 8.5 %collective-permute-start.2 = (bf16[768,768]{1,0:T(8,128)(2,1)}, bf16[768,768]{1,0:T(8,128)(2,1)S(1)}, u32[]{:S(2)}, u32[]{:S(2)}) collective-permute-start(bf16[768,768]{1,0:T(8,128)(2,1)} %refs_10_.1), channel_id=1, source_target_pairs={{0,1},{1,0},{2,3},{3,2},{4,5},{5,4},{6,7},{7,6},{8,9},{9,8},{10,11... | collective-permute-start | bytes 3538952 | tf_op jit(solution)/shard_map/ppermute | solution.py:1197
  132.9 8.0 %collective-permute-start.5 = (bf16[768,768]{1,0:T(8,128)(2,1)S(1)}, bf16[768,768]{1,0:T(8,128)(2,1)S(1)}, u32[]{:S(2)}, u32[]{:S(2)}) collective-permute-start(bf16[768,768]{1,0:T(8,128)(2,1)S(1)} %copy-done.2), channel_id=1, source_target_pairs={{0,1},{1,0},{2,3},{3,2},{4,5},{5,4},{6,7},{7,6},{8,9},{9,8},{10,11... | collective-permute-start | bytes 3538952 | tf_op jit(solution)/shard_map/ppermute | solution.py:1197
  133.0 8.0 %collective-permute-start.4 = (bf16[768,768]{1,0:T(8,128)(2,1)}, bf16[768,768]{1,0:T(8,128)(2,1)S(1)}, u32[]{:S(2)}, u32[]{:S(2)}) collective-permute-start(bf16[768,768]{1,0:T(8,128)(2,1)} %collective-permute-done.refs_8_.refs_12_), channel_id=1, source_target_pairs={{0,1},{1,0},{2,3},{3,2},{4,5},{5,4},{6,7},{7,6},{8,9},{9,8},{10,11... | collective-permute-start | bytes 3538952 | tf_op jit(solution)/shard_map/ppermute | solution.py:1197
  133.4 3.6 collective-permute-start.7
  137.0 1.6 collective-permute-start.6
  138.6 1.7 collective-permute-start.8
  140.9 1.8 copy-start.4
  141.0 2.1 copy-start.11
  183.1 5.7 copy-start.39
  183.1 6.3 copy-start.40
  183.1 6.9 %copy-start.46 = (bf16[768]{0:T(1024)(128)(2,1)S(1)}, bf16[768]{0:T(1024)(128)(2,1)}, u32[]{:S(2)}) copy-start(bf16[768]{0:T(1024)(128)(2,1)} %param.34) | copy-start | bytes 4612
  183.1 7.5 %copy-start.47 = (bf16[768]{0:T(1024)(128)(2,1)S(1)}, bf16[768]{0:T(1024)(128)(2,1)}, u32[]{:S(2)}) copy-start(bf16[768]{0:T(1024)(128)(2,1)} %param.35) | copy-start | bytes 4612
  184.5 54.6 %all-to-all-start.3 = ((bf16[8,15,24,384]{3,2,1,0:T(8,128)(2,1)}), bf16[8,15,24,384]{3,2,1,0:T(8,128)(2,1)}, u32[]{:S(2)}, u32[]{:S(2)}) async-start(bf16[8,15,24,384]{3,2,1,0:T(8,128)(2,1)} %get-tuple-element.86), calls=%async_computation.3 | async-start | bytes 4423680 | tf_op jit(solution)/shard_map/all_to_all | solution.py:1256
  298.9 106.2 %all-to-all-start.4 = ((bf16[8,15,24,768]{3,2,1,0:T(8,128)(2,1)}), bf16[8,15,24,768]{3,2,1,0:T(8,128)(2,1)}, u32[]{:S(2)}, u32[]{:S(2)}) async-start(bf16[8,15,24,768]{3,2,1,0:T(8,128)(2,1)} %get-tuple-element.93), calls=%async_computation.4 | async-start | bytes 8847360 | tf_op jit(solution)/shard_map/all_to_all | solution.py:1256
  316.1 12.9 %collective-permute-start.10 = (bf16[2,768,768]{2,1,0:T(8,128)(2,1)}, bf16[2,768,768]{2,1,0:T(8,128)(2,1)S(1)}, u32[]{:S(2)}, u32[]{:S(2)}) collective-permute-start(bf16[2,768,768]{2,1,0:T(8,128)(2,1)} %shard_map.344), channel_id=1, source_target_pairs={{0,1},{1,0},{2,3},{3,2},{4,5},{5,4},{6,7},{7,6},{8,9},{9,8},{10,11... | collective-permute-start | bytes 7077896 | tf_op jit(solution)/shard_map/ppermute | solution.py:1197
  328.5 16.8 %collective-permute-start.9 = (bf16[2,768,768]{2,1,0:T(8,128)(2,1)}, bf16[2,768,768]{2,1,0:T(8,128)(2,1)S(1)}, u32[]{:S(2)}, u32[]{:S(2)}) collective-permute-start(bf16[2,768,768]{2,1,0:T(8,128)(2,1)} %shard_map.341), channel_id=1, source_target_pairs={{0,1},{1,0},{2,3},{3,2},{4,5},{5,4},{6,7},{7,6},{8,9},{9,8},{10,11... | collective-permute-start | bytes 7077896 | tf_op jit(solution)/shard_map/ppermute | solution.py:1197
  343.8 16.8 %copy-start.48 = (bf16[768]{0:T(1024)(128)(2,1)S(1)}, bf16[768]{0:T(1024)(128)(2,1)}, u32[]{:S(2)}) copy-start(bf16[768]{0:T(1024)(128)(2,1)} %param.39) | copy-start | bytes 4612
  343.8 43.9 %collective-permute-start.12 = (bf16[768,768]{1,0:T(8,128)(2,1)}, bf16[768,768]{1,0:T(8,128)(2,1)S(1)}, u32[]{:S(2)}, u32[]{:S(2)}) collective-permute-start(bf16[768,768]{1,0:T(8,128)(2,1)} %get-tuple-element.104), channel_id=1, source_target_pairs={{0,2},{1,3},{2,0},{3,1},{4,6},{5,7},{6,4},{7,5},{8,10},{9,11},{10,... | collective-permute-start | bytes 3538952 | tf_op jit(solution)/shard_map/ppermute | solution.py:1197
  360.1 37.1 %collective-permute-start.11 = (bf16[768,768]{1,0:T(8,128)(2,1)}, bf16[768,768]{1,0:T(8,128)(2,1)S(1)}, u32[]{:S(2)}, u32[]{:S(2)}) collective-permute-start(bf16[768,768]{1,0:T(8,128)(2,1)} %get-tuple-element.90.refs_11_), channel_id=1, source_target_pairs={{0,2},{1,3},{2,0},{3,1},{4,6},{5,7},{6,4},{7,5},{8,10},{9,11},{10,... | collective-permute-start | bytes 3538952 | tf_op jit(solution)/shard_map/ppermute | solution.py:1197
  387.7 9.5 %copy-start.21 = (bf16[768,768]{1,0:T(8,128)(2,1)}, bf16[768,768]{1,0:T(8,128)(2,1)S(1)}, u32[]{:S(2)}) copy-start(bf16[768,768]{1,0:T(8,128)(2,1)S(1)} %collective-permute-done.12.refs_4_) | copy-start | bytes 3538948
  403.2 28.8 %collective-permute-start.13 = (bf16[2,384,768]{2,1,0:T(8,128)(2,1)}, bf16[2,384,768]{2,1,0:T(8,128)(2,1)S(1)}, u32[]{:S(2)}, u32[]{:S(2)}) collective-permute-start(bf16[2,384,768]{2,1,0:T(8,128)(2,1)} %get-tuple-element.108), channel_id=1, source_target_pairs={{0,4},{4,0},{8,12},{12,8},{16,20},{20,16},{24,28},{28,24},{1,5},{5... | collective-permute-start | bytes 3538952 | tf_op jit(solution)/shard_map/ppermute | solution.py:1197
  436.6 125.3 %all-to-all-start.5 = ((bf16[8,15,24,768]{3,2,1,0:T(8,128)(2,1)}), bf16[8,15,24,768]{3,2,1,0:T(8,128)(2,1)}, u32[]{:S(2)}, u32[]{:S(2)}) async-start(bf16[8,15,24,768]{3,2,1,0:T(8,128)(2,1)} %shard_map.350), calls=%async_computation.5 | async-start | bytes 8847360 | tf_op jit(solution)/shard_map/all_to_all | solution.py:1256
  442.9 5.2 copy-start.5
  442.9 5.2 copy-start.6
  448.1 3.5 copy-start.17
  448.1 3.5 copy-start.18
  451.6 3.5 copy-start.7
  451.6 3.5 copy-start.16
  458.7 5.5 copy-start.25
  464.2 2.5 collective-permute-start.14
  464.2 61.0 %collective-permute-start.17 = (bf16[2,192,768]{2,1,0:T(8,128)(2,1)S(1)}, bf16[2,192,768]{2,1,0:T(8,128)(2,1)S(1)}, u32[]{:S(2)}, u32[]{:S(2)}) collective-permute-start(bf16[2,192,768]{2,1,0:T(8,128)(2,1)S(1)} %copy-done.25), channel_id=1, source_target_pairs={{0,8},{4,12},{8,0},{12,4},{16,24},{20,28},{24,16},{28,20},{1,9},{5... | collective-permute-start | bytes 1769480 | tf_op jit(solution)/shard_map/ppermute | solution.py:1197
  470.0 11.4 %collective-permute-start.15 = (f32[128,768]{1,0:T(8,128)}, f32[128,768]{1,0:T(8,128)S(1)}, u32[]{:S(2)}, u32[]{:S(2)}) collective-permute-start(f32[128,768]{1,0:T(8,128)} %get-tuple-element.127), channel_id=1, source_target_pairs={{0,2},{1,3},{2,0},{3,1},{4,6},{5,7},{6,4},{7,5},{8,10},{9,11},{10,... | collective-permute-start | bytes 1179656 | tf_op jit(solution)/shard_map/ppermute | solution.py:1197
  484.0 69.9 %copy-start.32 = (f32[64,768]{1,0:T(8,128)S(1)}, f32[64,768]{1,0:T(8,128)}, u32[]{:S(2)}) copy-start(f32[64,768]{1,0:T(8,128)} %get-tuple-element.129.refs_3_) | copy-start | bytes 589828
  528.6 22.7 %collective-permute-start.18 = (bf16[2,96,768]{2,1,0:T(8,128)(2,1)}, bf16[2,96,768]{2,1,0:T(8,128)(2,1)S(1)}, u32[]{:S(2)}, u32[]{:S(2)}) collective-permute-start(bf16[2,96,768]{2,1,0:T(8,128)(2,1)} %get-tuple-element.132), channel_id=1, source_target_pairs={{0,16},{4,20},{8,24},{12,28},{16,0},{20,4},{24,8},{28,12},{1,17},{... | collective-permute-start | bytes 884744 | tf_op jit(solution)/shard_map/ppermute | solution.py:1197
  553.9 22.0 %collective-permute-start.23 = (bf16[2,96,768]{2,1,0:T(8,128)(2,1)}, bf16[2,96,768]{2,1,0:T(8,128)(2,1)S(1)}, u32[]{:S(2)}, u32[]{:S(2)}) collective-permute-start(bf16[2,96,768]{2,1,0:T(8,128)(2,1)} %shard_map.358.refs_7_.refs_1_), channel_id=1, source_target_pairs={{0,16},{4,20},{8,24},{12,28},{16,0},{20,4},{24,8},{28,12},{1,17},{... | collective-permute-start | bytes 884744 | tf_op jit(solution)/shard_map/ppermute | solution.py:1197
  553.9 5.7 collective-permute-start.16
  576.6 6.3 copy-start.19
  578.5 36.9 %collective-permute-start.24 = (bf16[2,192,768]{2,1,0:T(8,128)(2,1)}, bf16[2,192,768]{2,1,0:T(8,128)(2,1)S(1)}, u32[]{:S(2)}, u32[]{:S(2)}) collective-permute-start(bf16[2,192,768]{2,1,0:T(8,128)(2,1)} %shard_map.361.refs_1_), channel_id=1, source_target_pairs={{0,4},{4,0},{8,12},{12,8},{16,20},{20,16},{24,28},{28,24},{1,5},{5... | collective-permute-start | bytes 1769480 | tf_op jit(solution)/shard_map/ppermute | solution.py:1197
  580.2 39.9 %collective-permute-start.26 = (bf16[2,192,768]{2,1,0:T(8,128)(2,1)}, bf16[2,192,768]{2,1,0:T(8,128)(2,1)S(1)}, u32[]{:S(2)}, u32[]{:S(2)}) collective-permute-start(bf16[2,192,768]{2,1,0:T(8,128)(2,1)} %shard_map.361.refs_1_), channel_id=1, source_target_pairs={{0,8},{4,12},{8,0},{12,4},{16,24},{20,28},{24,16},{28,20},{1,9},{5... | collective-permute-start | bytes 1769480 | tf_op jit(solution)/shard_map/ppermute | solution.py:1197
  582.9 22.8 %collective-permute-start.19 = (f32[64,768]{1,0:T(8,128)S(1)}, f32[64,768]{1,0:T(8,128)S(1)}, u32[]{:S(2)}, u32[]{:S(2)}) collective-permute-start(f32[64,768]{1,0:T(8,128)S(1)} %copy-done.19), channel_id=1, source_target_pairs={{0,8},{4,12},{8,0},{12,4},{16,24},{20,28},{24,16},{28,20},{1,9},{5... | collective-permute-start | bytes 589832 | tf_op jit(solution)/shard_map/ppermute | solution.py:1197
  582.9 22.8 %collective-permute-start.20 = (f32[64,768]{1,0:T(8,128)S(1)}, f32[64,768]{1,0:T(8,128)S(1)}, u32[]{:S(2)}, u32[]{:S(2)}) collective-permute-start(f32[64,768]{1,0:T(8,128)S(1)} %copy-done.19), channel_id=1, source_target_pairs={{0,16},{4,20},{8,24},{12,28},{16,0},{20,4},{24,8},{28,12},{1,17},{... | collective-permute-start | bytes 589832 | tf_op jit(solution)/shard_map/ppermute | solution.py:1197
  585.0 23.1 %collective-permute-start.21 = (f32[64,768]{1,0:T(8,128)S(1)}, f32[64,768]{1,0:T(8,128)S(1)}, u32[]{:S(2)}, u32[]{:S(2)}) collective-permute-start(f32[64,768]{1,0:T(8,128)S(1)} %copy-done.19), channel_id=1, source_target_pairs={{0,24},{4,28},{8,16},{12,20},{16,8},{20,12},{24,0},{28,4},{1,25},{... | collective-permute-start | bytes 589832 | tf_op jit(solution)/shard_map/ppermute | solution.py:1197
  605.7 2.4 copy-start.35
  605.7 2.4 copy-start.36
  610.7 4.8 collective-permute-start.22
  618.6 5.9 collective-permute-start.25
  620.1 4.4 copy-start.14
  620.1 10.4 %collective-permute-start.28 = (bf16[2,192,768]{2,1,0:T(8,128)(2,1)S(1)}, bf16[2,192,768]{2,1,0:T(8,128)(2,1)S(1)}, u32[]{:S(2)}, u32[]{:S(2)}) collective-permute-start(bf16[2,192,768]{2,1,0:T(8,128)(2,1)S(1)} %collective-permute-done.26.refs_3_), channel_id=1, source_target_pairs={{0,4},{4,0},{8,12},{12,8},{16,20},{20,16},{24,28},{28,24},{1,5},{5... | collective-permute-start | bytes 1769480 | tf_op jit(solution)/shard_map/ppermute | solution.py:1197
  627.0 8.5 %collective-permute-start.27 = (bf16[256,768]{1,0:T(8,128)(2,1)}, bf16[256,768]{1,0:T(8,128)(2,1)S(1)}, u32[]{:S(2)}, u32[]{:S(2)}) collective-permute-start(bf16[256,768]{1,0:T(8,128)(2,1)} %shard_map.363.refs_1_), channel_id=1, source_target_pairs={{0,1},{1,0},{2,3},{3,2},{4,5},{5,4},{6,7},{7,6},{8,9},{9,8},{10,11... | collective-permute-start | bytes 1179656 | tf_op jit(solution)/shard_map/ppermute | solution.py:1197
  (20 other events, 19.2 us)

commit v4 on v3

--- a/solution.py
+++ b/solution.py
@@ -1096,7 +1096,7 @@
     size = plan.points // steps
 
     def body(index, carry):
-        rows = pl.ds(pl.multiple_of(index * size, size), size)
+        rows = slice(index * size, (index + 1) * size)
         pre_one = dot(zed[rows, :], w1[...]) + b1[...]
         cdf = 0.5 * (1.0 + lax.erf(pre_one * ROOT_HALF))
         hidden = (pre_one * cdf).astype(BF16)
@@ -1110,7 +1110,8 @@
         slope2[rows, :] = (bent * bent).astype(BF16)
         return carry
 
-    lax.fori_loop(0, steps, body, 0)
+    for index in range(steps):
+        body(index, 0)
     from_points(plan, shrunk, (tat, tbt), (pa, pb))
     repack(plan, pa, pb, out)
 
@@ -1125,7 +1126,7 @@
     sums[...] = jnp.zeros_like(sums)
 
     def body(index, carry):
-        rows = pl.ds(pl.multiple_of(index * size, size), size)
+        rows = slice(index * size, (index + 1) * size)
         two = (work[rows, :].astype(F32) * slope2[rows, :].astype(F32)).astype(BF16)
         grad2[rows, :] = two
         one = (dot_t(two, w2[...]) * slope1[rows, :].astype(F32)).astype(BF16)
@@ -1135,7 +1136,8 @@
         sums[...] += row_sums(one.astype(F32), two.astype(F32), grad * zed[rows, :].astype(F32))
         return carry
 
-    lax.fori_loop(0, steps, body, 0)
+    for index in range(steps):
+        body(index, 0)
     for which, start in enumerate((0, plan.points_a)):
         sums[3 + which : 4 + which] = work[start : start + 16, :].astype(F32)[:1]
         sums[5 + which : 6 + which] = zed[start : start + 16, :].astype(F32)[:1]
@@ -1517,7 +1519,8 @@
         after=2,
     )(xa, xb, returned, dmid, gain1, fwd_w_t, pack, shared)
 
-    shared = join(place, at(high_link), shared, high_got, grad_a)
+    pack = total(place, [pack] + layers, grad_a, kind=BF16)
+    shared = join(place, at(high_link), shared, high_got, pack)
     low_got = over(shared, low_link)
     row_got = over(shared, row_link)
     reduce_sum, expand_sum = corners(
@@ -1525,7 +1528,6 @@
         (at(row_link), at(low_link)),
         (shared, row_got, low_got, over(low_got, row_link)),
     )
-    pack = total(place, [pack] + layers, grad_a, kind=BF16)
     pack = join(place, at(row_link), pack, over(pack, row_link), row_got)
     pack = join(place, at(column_link), pack, over(pack, column_link), low_got)
     inner_grad, outer_grad, small = last_join(

time: 650 us -> 647 us (level)
  starting transfers between devices: 62 us -> 75.8 us
    all_to_all x6, starting transfers between devices: 31.1 us -> 43.7 us  [exchange(): return [lax.all_to_all(part, 'wide', 0, 0, tiled=True) for part in parts]]
    ppermute x29, waiting for transfers between devices: 141 us -> 133 us  [swap(): return lax.ppermute(value, axis, [(i, i ^ distance) for i in range(size)])]
    unnamed x104 -> x100, local copies, waits for them, and re-layouts: 21.2 us -> 21.3 us
  transfers between devices with their start and end apart: 35 -> 35, of which waited for: 18 -> 17; matrix products, arithmetic and copies ran while one was open for 6% -> 6% of each run, Pallas kernels for 32% -> 31%
where the time goes in v4:
time: 647 us; the launch traced here: 644 us
  Pallas kernels  278 us (43%)
  waiting for transfers between devices  226 us (35%)
  starting transfers between devices  75.8 us (12%)
  local copies, waits for them, and re-layouts  39.3 us (6%)
  matrix products  15.8 us (2%)
    ppermute x29, waiting for transfers between devices, swap(): return lax.ppermute(value, axis, [(i, i ^ distance) for i in range(size)])  133 us
    all_to_all x6, waiting for transfers between devices, exchange(): return [lax.all_to_all(part, 'wide', 0, 0, tiled=True) for part in parts]  93.3 us
    pallas_call x1, Pallas kernels, fast_device(): call(functools.partial(middle_kernel, plan), (plan.steps,), [plan.spec_a(...  59.8 us
    all_to_all x6, starting transfers between devices, exchange(): return [lax.all_to_all(part, 'wide', 0, 0, tiled=True) for part in parts]  43.7 us
    ppermute x29, starting transfers between devices, swap(): return lax.ppermute(value, axis, [(i, i ^ distance) for i in range(size)])  32.1 us
    pallas_call x12, Pallas kernels, flat_call(): call(kernel, (), [SMEM] + [spec(item) for item in operands], [spec(item)...  30.7 us
    pallas_call x2, Pallas kernels, products(): call(kernel, (2,), [chunk, flat, each], [whole_out] * 2, [one] * 2)  26.7 us
    pallas_call x1, Pallas kernels, fast_device(): call(functools.partial(mixed_kernel, plan), (plan.steps,), [count_spec, p...  25.7 us
  transfers between devices with their start and end apart: 35, of which 17 were waited for; matrix products, arithmetic and copies ran while one was open for 6% of the time, Pallas kernels for 31%

profile of v4, /device:TPU:0, one launch (start us, length us, event | category | flops | bytes accessed | tf_op | source)
XLA Modules:
  0.0 644.4 jit_solution(2251590483106655338)
XLA Ops:
  0.6 11.9 %shard_map.333 = (bf16[8,15,24,384]{3,2,1,0:T(8,128)(2,1)}, bf16[8,15,24,384]{3,2,1,0:T(8,128)(2,1)}) custom-call(bf16[12,180,768]{2,1,0:T(8,128)(2,1)} %bitcast.56, bf16[6,90,768]{2,1,0:T(8,128)(2,1)} %bitcast.60, bf16[768]{0:T(1024)(128)(2,1)} %refs_2_.2, bf16[768]{0:T(1024)(128)(2,1)} %refs_3_.1, bf16[2,2,192,192]{3,2,1,0:T(8,128)(2,1)} %constant.65.clone.refs_4_), custom_call_target="tpu_custom_call" | custom-call | tf_op jit(solution)/shard_map/pallas_call | solution.py:1260
  12.5 7.4 %all-to-all-start = ((bf16[8,15,24,384]{3,2,1,0:T(8,128)(2,1)}), bf16[8,15,24,384]{3,2,1,0:T(8,128)(2,1)S(1)}, u32[]{:S(2)}, u32[]{:S(2)}) async-start(bf16[8,15,24,384]{3,2,1,0:T(8,128)(2,1)} %get-tuple-element.78), calls=%async_computation | async-start | bytes 4423680 | tf_op jit(solution)/shard_map/all_to_all | solution.py:1258
  23.3 1.7 copy.61
  25.1 1.8 reshape.684
  26.8 1.7 copy.62
  35.7 3.7 shard_map.334
  43.2 6.1 shard_map.336
  50.7 22.3 %collective-permute-done.refs_8_.refs_12_ = bf16[768,768]{1,0:T(8,128)(2,1)} collective-permute-done((bf16[768,768]{1,0:T(8,128)(2,1)}, bf16[768,768]{1,0:T(8,128)(2,1)}, u32[]{:S(2)}, u32[]{:S(2)}) %collective-permute-start) | collective-permute-done | bytes 1179680 | tf_op jit(solution)/shard_map/ppermute | solution.py:1199
  73.0 6.0 all-to-all-start.2
  80.2 11.7 %shard_map.335 = (bf16[8,15,24,384]{3,2,1,0:T(8,128)(2,1)}, bf16[1440,768]{1,0:T(8,128)(2,1)}, bf16[1440,768]{1,0:T(8,128)(2,1)}, bf16[1440,768]{1,0:T(8,128)(2,...) custom-call(bf16[8,15,24,384]{3,2,1,0:T(8,128)(2,1)} %copy-done.8, ...), custom_call_target="tpu_custom_call" | custom-call | tf_op jit(solution)/shard_map/pallas_call | solution.py:1329
  91.9 36.3 %all-to-all-done.2.refs_0_ = bf16[8,15,24,384]{3,2,1,0:T(8,128)(2,1)} async-done(((bf16[8,15,24,384]{3,2,1,0:T(8,128)(2,1)}), bf16[8,15,24,384]{3,2,1,0:T(8,128)(2,1)}, u32[]{:S(2)}, u32[]{:S(2)}) %all-to-all-start.2) | async-done | bytes 2211872 | tf_op jit(solution)/shard_map/all_to_all | solution.py:1258
  128.2 4.0 all-to-all-start.1
  134.8 2.1 collective-permute-done.7
  136.9 1.6 collective-permute-done.6
  143.0 11.7 %shard_map.338 = (bf16[8,15,24,384]{3,2,1,0:T(8,128)(2,1)}, bf16[1440,768]{1,0:T(8,128)(2,1)}, bf16[1440,768]{1,0:T(8,128)(2,1)}, bf16[1440,768]{1,0:T(8,128)(2,...) custom-call(bf16[8,15,24,384]{3,2,1,0:T(8,128)(2,1)} %all-to-all-done.2.refs_0_, ...), custom_call_target="tpu_custom_call" | custom-call | tf_op jit(solution)/shard_map/pallas_call | solution.py:1329
  154.7 28.4 %all-to-all-done.1.refs_5_.refs_2_ = bf16[8,15,24,384]{3,2,1,0:T(8,128)(2,1)S(1)} async-done(((bf16[8,15,24,384]{3,2,1,0:T(8,128)(2,1)}), bf16[8,15,24,384]{3,2,1,0:T(8,128)(2,1)S(1)}, u32[]{:S(2)}, u32[]{:S(2)}) %all-to-all-start.1) | async-done | bytes 2211872 | tf_op jit(solution)/shard_map/all_to_all | solution.py:1258
  184.4 4.7 all-to-all-start.3
  191.5 19.3 %shard_map.339.refs_15_ = bf16[4,2880,768]{2,1,0:T(8,128)(2,1)} custom-call(bf16[2880,768]{1,0:T(8,128)(2,1)} %get-tuple-element.84.refs_3_.refs_0_.refs_16_.refs_1_, bf16[768,768]{1,0:T(8,128)(2,1)} %refs_2_.3, bf16[768,768]{1,0:T(8,128)(2,1)} %copy-done.3, bf16[768,768]{1,0:T(8,128)(2,1)} %copy-done.1, bf16[768,768]{1,0:T(8,128)(2,1)} %copy-done.4, ...), custom_call_target="tpu_custom_call" | custom-call | tf_op jit(solution)/shard_map/pallas_call | solution.py:1341
  210.7 28.6 %all-to-all-done.3.refs_3_ = bf16[8,15,24,384]{3,2,1,0:T(8,128)(2,1)} async-done(((bf16[8,15,24,384]{3,2,1,0:T(8,128)(2,1)}), bf16[8,15,24,384]{3,2,1,0:T(8,128)(2,1)}, u32[]{:S(2)}, u32[]{:S(2)}) %all-to-all-start.3) | async-done | bytes 2211872 | tf_op jit(solution)/shard_map/all_to_all | solution.py:1258
  239.4 59.8 %shard_map.340 = (f32[2880,768]{1,0:T(8,128)}, bf16[2880,768]{1,0:T(8,128)(2,1)}, bf16[4,2880,768]{2,1,0:T(8,128)(2,1)}, bf16[4,2880,768]{2,1,0:T(8,128)(2,1)}, ...) custom-call(bf16[12,180,768]{2,1,0:T(8,128)(2,1)} %bitcast.57, ...), custom_call_target="tpu_custom_call" | custom-call | tf_op jit(solution)/shard_map/pallas_call | solution.py:1352
  299.1 15.9 %all-to-all-start.4 = ((bf16[8,15,24,768]{3,2,1,0:T(8,128)(2,1)}), bf16[8,15,24,768]{3,2,1,0:T(8,128)(2,1)}, u32[]{:S(2)}, u32[]{:S(2)}) async-start(bf16[8,15,24,768]{3,2,1,0:T(8,128)(2,1)} %get-tuple-element.93), calls=%async_computation.4 | async-start | bytes 8847360 | tf_op jit(solution)/shard_map/all_to_all | solution.py:1258
  315.0 12.4 %shard_map.344 = bf16[2,768,768]{2,1,0:T(8,128)(2,1)} custom-call(bf16[4,2880,768]{2,1,0:T(8,128)(2,1)} %get-tuple-element.101.refs_0_, bf16[2880,768]{1,0:T(8,128)(2,1)} %get-tuple-element.102.refs_1_), custom_call_target="tpu_custom_call" | custom-call | tf_op jit(solution)/shard_map/pallas_call | solution.py:836
  327.5 12.4 %shard_map.341 = bf16[2,768,768]{2,1,0:T(8,128)(2,1)} custom-call(bf16[4,2880,768]{2,1,0:T(8,128)(2,1)} %get-tuple-element.87.refs_0_.refs_1_, bf16[2880,768]{1,0:T(8,128)(2,1)} %get-tuple-element.84.refs_3_.refs_0_.refs_16_.refs_1_), custom_call_target="tpu_custom_call" | custom-call | tf_op jit(solution)/shard_map/pallas_call | solution.py:836
  341.7 13.3 %shard_map.345 = (bf16[768,768]{1,0:T(8,128)(2,1)}, bf16[768,768]{1,0:T(8,128)(2,1)}) custom-call(bf16[4,2880,768]{2,1,0:T(8,128)(2,1)} %get-tuple-element.101.refs_0_, bf16[2880,768]{1,0:T(8,128)(2,1)} %get-tuple-element.102.refs_1_, bf16[2,768,768]{2,1,0:T(8,128)(2,1)} %copy-done.13), custom_call_target="tpu_custom_call" | custom-call | tf_op jit(solution)/shard_map/pallas_call | solution.py:839
  358.0 13.4 %shard_map.342 = (bf16[768,768]{1,0:T(8,128)(2,1)}, bf16[768,768]{1,0:T(8,128)(2,1)}) custom-call(bf16[4,2880,768]{2,1,0:T(8,128)(2,1)} %get-tuple-element.87.refs_0_.refs_1_, bf16[2880,768]{1,0:T(8,128)(2,1)} %get-tuple-element.84.refs_3_.refs_0_.refs_16_.refs_1_, bf16[2,768,768]{2,1,0:T(8,128)(2,1)} %copy-done.12), custom_call_target="tpu_custom_call" | custom-call | tf_op jit(solution)/shard_map/pallas_call | solution.py:839
  373.1 25.7 %shard_map.343 = (bf16[12,1,180,768]{3,2,1,0:T(8,128)(2,1)}, bf16[6,1,90,768]{3,2,1,0:T(8,128)(2,1)}, f32[8,768]{1,0:T(8,128)}) custom-call(s32[2]{0:T(128)} %pad_add_fusion.refs_0_, bf16[4,2880,768]{2,1,0:T(8,128)(2,1)} %get-tuple-element.87.refs_0_.refs_1_, bf16[768,768]{1,0:T(8,128)(2,1)} %refs_2_.3, bf16[768,768]{1,0:T(8,128)(2,1)} %copy-done.3, ...), custom_call_target="tpu_custom_call" | custom-call | tf_op jit(solution)/shard_map/pallas_call | solution.py:1409
  398.8 9.7 %collective-permute-done.11.refs_3_ = bf16[768,768]{1,0:T(8,128)(2,1)S(1)} collective-permute-done((bf16[768,768]{1,0:T(8,128)(2,1)}, bf16[768,768]{1,0:T(8,128)(2,1)S(1)}, u32[]{:S(2)}, u32[]{:S(2)}) %collective-permute-start.11) | collective-permute-done | bytes 1179680 | tf_op jit(solution)/shard_map/ppermute | solution.py:1199
  409.5 5.4 shard_map.346
  414.9 1.7 collective-permute-start.13
  416.6 12.1 %shard_map.347 = (bf16[8,15,24,768]{3,2,1,0:T(8,128)(2,1)}, bf16[1440,768]{1,0:T(8,128)(2,1)}, bf16[1440,768]{1,0:T(8,128)(2,1)}, f32[8,768]{1,0:T(8,128)}) custom-call(bf16[8,15,24,768]{3,2,1,0:T(8,128)(2,1)} %all-to-all-done.4.got, bf16[2,192,192]{2,1,0:T(8,128)(2,1)} %pad_maximum_fusion.1.refs_1_.refs_4_.ta, ...), custom_call_target="tpu_custom_call" | custom-call | tf_op jit(solution)/shard_map/pallas_call | solution.py:1445
  428.7 12.1 %shard_map.348 = (bf16[8,15,24,768]{3,2,1,0:T(8,128)(2,1)}, bf16[1440,768]{1,0:T(8,128)(2,1)}, bf16[1440,768]{1,0:T(8,128)(2,1)}, f32[8,768]{1,0:T(8,128)}) custom-call(bf16[8,15,24,768]{3,2,1,0:T(8,128)(2,1)} %all-to-all-done.4.got, bf16[2,192,192]{2,1,0:T(8,128)(2,1)} %pad_maximum_fusion.1.refs_1_.refs_4_.ta, ...), custom_call_target="tpu_custom_call", output_to_operand_aliasing={{0}: (10, {})} | custom-call | tf_op jit(solution)/shard_map/pallas_call | solution.py:1445
  443.3 3.4 shard_map.349
  446.7 5.7 all-to-all-start.5
  452.4 1.6 copy-done.9
  454.1 5.2 fusion.24.refs_2_
  459.3 3.5 fusion.23.refs_1_
  462.8 3.5 fusion.26.refs_4_
  466.3 3.6 fusion.25.refs_3_
  469.9 5.5 shard_map.353
  475.4 2.1 collective-permute-start.17
  478.8 2.4 shard_map.354
  482.7 9.9 %collective-permute-done.15.refs_2_ = f32[128,768]{1,0:T(8,128)S(1)} collective-permute-done((f32[128,768]{1,0:T(8,128)}, f32[128,768]{1,0:T(8,128)S(1)}, u32[]{:S(2)}, u32[]{:S(2)}) %collective-permute-start.15) | collective-permute-done | bytes 393248 | tf_op jit(solution)/shard_map/ppermute | solution.py:1199
  493.3 1.9 shard_map.355
  495.2 40.4 %collective-permute-done.17.refs_2_ = bf16[2,192,768]{2,1,0:T(8,128)(2,1)S(1)} collective-permute-done((bf16[2,192,768]{2,1,0:T(8,128)(2,1)S(1)}, bf16[2,192,768]{2,1,0:T(8,128)(2,1)S(1)}, u32[]{:S(2)}, u32[]{:S(2)}) %collective-permute-start.17) | collective-permute-done | bytes 589856 | tf_op jit(solution)/shard_map/ppermute | solution.py:1199
  536.4 2.6 shard_map.357
  539.0 4.0 collective-permute-start.18
  544.4 17.3 %collective-permute-done.18.refs_2_ = bf16[2,96,768]{2,1,0:T(8,128)(2,1)S(1)} collective-permute-done((bf16[2,96,768]{2,1,0:T(8,128)(2,1)}, bf16[2,96,768]{2,1,0:T(8,128)(2,1)S(1)}, u32[]{:S(2)}, u32[]{:S(2)}) %collective-permute-start.18) | collective-permute-done | bytes 294944 | tf_op jit(solution)/shard_map/ppermute | solution.py:1199
  562.4 1.8 shard_map.358.refs_7_.refs_1_
  564.9 1.7 shard_map.356.refs_6_.refs_1_
  566.6 2.8 collective-permute-start.19
  569.6 2.3 collective-permute-start.21
  571.8 13.9 %shard_map.359 = (f32[12,180,1,768]{3,2,1,0:T(1,128)}, f32[6,90,1,768]{3,2,1,0:T(1,128)}) custom-call(bf16[12,180,768]{2,1,0:T(8,128)(2,1)} %bitcast.59, bf16[6,90,768]{2,1,0:T(8,128)(2,1)} %bitcast.63, bf16[8,15,24,768]{3,2,1,0:T(8,128)(2,1)} %all-to-all-done.5.refs_2_, f32[2880,768]{1,0:T(8,128)} %get-tuple-element.89.refs_8_.refs_3_, ...), custom_call_target="tpu_custom_call" | custom-call | tf_op jit(solution)/shard_map/pallas_call | solution.py:1508
  585.8 6.8 %collective-permute-done.20.refs_3_ = f32[64,768]{1,0:T(8,128)S(1)} collective-permute-done((f32[64,768]{1,0:T(8,128)}, f32[64,768]{1,0:T(8,128)S(1)}, u32[]{:S(2)}, u32[]{:S(2)}) %collective-permute-start.20) | collective-permute-done | bytes 196640 | tf_op jit(solution)/shard_map/ppermute | solution.py:1199
  593.3 1.9 shard_map.360.refs_3_.refs_1_
  595.9 1.9 shard_map.361.refs_1_
  598.9 4.6 collective-permute-start.26
  603.6 11.1 %collective-permute-done.22.refs_2_ = bf16[64,768]{1,0:T(8,128)(2,1)S(1)} collective-permute-done((bf16[64,768]{1,0:T(8,128)(2,1)}, bf16[64,768]{1,0:T(8,128)(2,1)S(1)}, u32[]{:S(2)}, u32[]{:S(2)}) %collective-permute-start.22) | collective-permute-done | bytes 98336 | tf_op jit(solution)/shard_map/ppermute | solution.py:1199
  616.1 1.7 shard_map.362.refs_1_
  619.3 1.7 collective-permute-start.28
  621.0 2.6 collective-permute-done.25.refs_2_
  624.3 1.8 shard_map.363.refs_1_
  626.2 7.1 %collective-permute-done.28.refs_4_ = bf16[2,192,768]{2,1,0:T(8,128)(2,1)S(1)} collective-permute-done((bf16[2,192,768]{2,1,0:T(8,128)(2,1)S(1)}, bf16[2,192,768]{2,1,0:T(8,128)(2,1)S(1)}, u32[]{:S(2)}, u32[]{:S(2)}) %collective-permute-start.28) | collective-permute-done | bytes 589856 | tf_op jit(solution)/shard_map/ppermute | solution.py:1199
  634.1 4.1 shard_map.364
  639.0 2.3 shard_map.365
  (192 shorter events, 53.1 us)
Async XLA Ops:
  12.5 9.4 %copy-start.39 = (s32[9]{0:T(128)S(1)}, s32[9]{0:T(128)}, u32[]{:S(2)}) copy-start(s32[9]{0:T(128)} %param.26) | copy-start | bytes 112
  12.5 16.0 %copy-start.40 = (s32[9]{0:T(128)S(1)}, s32[9]{0:T(128)}, u32[]{:S(2)}) copy-start(s32[9]{0:T(128)} %param.27) | copy-start | bytes 112
  12.5 60.4 %all-to-all-start = ((bf16[8,15,24,384]{3,2,1,0:T(8,128)(2,1)}), bf16[8,15,24,384]{3,2,1,0:T(8,128)(2,1)S(1)}, u32[]{:S(2)}, u32[]{:S(2)}) async-start(bf16[8,15,24,384]{3,2,1,0:T(8,128)(2,1)} %get-tuple-element.78), calls=%async_computation | async-start | bytes 4423680 | tf_op jit(solution)/shard_map/all_to_all | solution.py:1258
  19.9 30.7 %collective-permute-start.1 = (bf16[768,768]{1,0:T(8,128)(2,1)}, bf16[768,768]{1,0:T(8,128)(2,1)S(1)}, u32[]{:S(2)}, u32[]{:S(2)}) collective-permute-start(bf16[768,768]{1,0:T(8,128)(2,1)} %refs_2_.3), channel_id=1, source_target_pairs={{0,2},{1,3},{2,0},{3,1},{4,6},{5,7},{6,4},{7,5},{8,10},{9,11},{10,... | collective-permute-start | bytes 3538952 | tf_op jit(solution)/shard_map/ppermute | solution.py:1199
  21.4 51.5 %collective-permute-start = (bf16[768,768]{1,0:T(8,128)(2,1)}, bf16[768,768]{1,0:T(8,128)(2,1)}, u32[]{:S(2)}, u32[]{:S(2)}) collective-permute-start(bf16[768,768]{1,0:T(8,128)(2,1)} %refs_10_.1), channel_id=1, source_target_pairs={{0,2},{1,3},{2,0},{3,1},{4,6},{5,7},{6,4},{7,5},{8,10},{9,11},{10,... | collective-permute-start | bytes 3538952 | tf_op jit(solution)/shard_map/ppermute | solution.py:1199
  43.2 6.7 %copy-start.23 = (f32[1,192,192]{2,1,0:T(8,128)S(1)}, f32[1,192,192]{2,1,0:T(8,128)}, u32[]{:S(2)}) copy-start(f32[1,192,192]{2,1,0:T(8,128)} %copy.62) | copy-start | bytes 442372
  50.7 22.3 %copy-start.1 = (bf16[768,768]{1,0:T(8,128)(2,1)}, bf16[768,768]{1,0:T(8,128)(2,1)S(1)}, u32[]{:S(2)}) copy-start(bf16[768,768]{1,0:T(8,128)(2,1)S(1)} %collective-permute-done.1.refs_9_.refs_3_.refs_4_) | copy-start | bytes 3538948
  72.9 6.0 copy-start.41
  73.0 6.6 %copy-start.42 = (bf16[2,768]{1,0:T(2,128)(2,1)S(1)}, bf16[2,768]{1,0:T(2,128)(2,1)}, u32[]{:S(2)}) copy-start(bf16[2,768]{1,0:T(2,128)(2,1)} %param.33) | copy-start | bytes 9220
  73.0 6.0 copy-start.8
  73.0 55.2 %all-to-all-start.2 = ((bf16[8,15,24,384]{3,2,1,0:T(8,128)(2,1)}), bf16[8,15,24,384]{3,2,1,0:T(8,128)(2,1)}, u32[]{:S(2)}, u32[]{:S(2)}) async-start(bf16[8,15,24,384]{3,2,1,0:T(8,128)(2,1)} %shard_map.337), calls=%async_computation.2 | async-start | bytes 4423680 | tf_op jit(solution)/shard_map/all_to_all | solution.py:1258
  128.2 4.6 copy-start.2
  128.2 5.1 copy-start.43
  128.2 54.9 %all-to-all-start.1 = ((bf16[8,15,24,384]{3,2,1,0:T(8,128)(2,1)}), bf16[8,15,24,384]{3,2,1,0:T(8,128)(2,1)S(1)}, u32[]{:S(2)}, u32[]{:S(2)}) async-start(bf16[8,15,24,384]{3,2,1,0:T(8,128)(2,1)} %get-tuple-element.81), calls=%async_computation.1 | async-start | bytes 4423680 | tf_op jit(solution)/shard_map/all_to_all | solution.py:1258
  132.2 8.6 %collective-permute-start.3 = (bf16[768,768]{1,0:T(8,128)(2,1)}, bf16[768,768]{1,0:T(8,128)(2,1)S(1)}, u32[]{:S(2)}, u32[]{:S(2)}) collective-permute-start(bf16[768,768]{1,0:T(8,128)(2,1)} %refs_2_.3), channel_id=1, source_target_pairs={{0,1},{1,0},{2,3},{3,2},{4,5},{5,4},{6,7},{7,6},{8,9},{9,8},{10,11... | collective-permute-start | bytes 3538952 | tf_op jit(solution)/shard_map/ppermute | solution.py:1199
  132.3 8.5 %collective-permute-start.2 = (bf16[768,768]{1,0:T(8,128)(2,1)}, bf16[768,768]{1,0:T(8,128)(2,1)S(1)}, u32[]{:S(2)}, u32[]{:S(2)}) collective-permute-start(bf16[768,768]{1,0:T(8,128)(2,1)} %refs_10_.1), channel_id=1, source_target_pairs={{0,1},{1,0},{2,3},{3,2},{4,5},{5,4},{6,7},{7,6},{8,9},{9,8},{10,11... | collective-permute-start | bytes 3538952 | tf_op jit(solution)/shard_map/ppermute | solution.py:1199
  132.8 8.0 %collective-permute-start.5 = (bf16[768,768]{1,0:T(8,128)(2,1)S(1)}, bf16[768,768]{1,0:T(8,128)(2,1)S(1)}, u32[]{:S(2)}, u32[]{:S(2)}) collective-permute-start(bf16[768,768]{1,0:T(8,128)(2,1)S(1)} %copy-done.2), channel_id=1, source_target_pairs={{0,1},{1,0},{2,3},{3,2},{4,5},{5,4},{6,7},{7,6},{8,9},{9,8},{10,11... | collective-permute-start | bytes 3538952 | tf_op jit(solution)/shard_map/ppermute | solution.py:1199
  132.9 8.0 %collective-permute-start.4 = (bf16[768,768]{1,0:T(8,128)(2,1)}, bf16[768,768]{1,0:T(8,128)(2,1)S(1)}, u32[]{:S(2)}, u32[]{:S(2)}) collective-permute-start(bf16[768,768]{1,0:T(8,128)(2,1)} %collective-permute-done.refs_8_.refs_12_), channel_id=1, source_target_pairs={{0,1},{1,0},{2,3},{3,2},{4,5},{5,4},{6,7},{7,6},{8,9},{9,8},{10,11... | collective-permute-start | bytes 3538952 | tf_op jit(solution)/shard_map/ppermute | solution.py:1199
  133.3 3.6 collective-permute-start.7
  136.9 1.6 collective-permute-start.6
  138.5 1.7 collective-permute-start.8
  140.8 1.4 copy-start.10
  140.9 1.8 copy-start.4
  140.9 2.1 copy-start.11
  183.1 6.1 copy-start.37
  183.1 6.6 %copy-start.38 = (bf16[768]{0:T(1024)(128)(2,1)S(1)}, bf16[768]{0:T(1024)(128)(2,1)}, u32[]{:S(2)}) copy-start(bf16[768]{0:T(1024)(128)(2,1)} %refs_3_.1) | copy-start | bytes 4612
  183.1 7.2 %copy-start.44 = (bf16[768]{0:T(1024)(128)(2,1)S(1)}, bf16[768]{0:T(1024)(128)(2,1)}, u32[]{:S(2)}) copy-start(bf16[768]{0:T(1024)(128)(2,1)} %param.34) | copy-start | bytes 4612
  183.1 7.8 %copy-start.45 = (bf16[768]{0:T(1024)(128)(2,1)S(1)}, bf16[768]{0:T(1024)(128)(2,1)}, u32[]{:S(2)}) copy-start(bf16[768]{0:T(1024)(128)(2,1)} %param.35) | copy-start | bytes 4612
  184.4 55.0 %all-to-all-start.3 = ((bf16[8,15,24,384]{3,2,1,0:T(8,128)(2,1)}), bf16[8,15,24,384]{3,2,1,0:T(8,128)(2,1)}, u32[]{:S(2)}, u32[]{:S(2)}) async-start(bf16[8,15,24,384]{3,2,1,0:T(8,128)(2,1)} %get-tuple-element.86), calls=%async_computation.3 | async-start | bytes 4423680 | tf_op jit(solution)/shard_map/all_to_all | solution.py:1258
  299.1 117.5 %all-to-all-start.4 = ((bf16[8,15,24,768]{3,2,1,0:T(8,128)(2,1)}), bf16[8,15,24,768]{3,2,1,0:T(8,128)(2,1)}, u32[]{:S(2)}, u32[]{:S(2)}) async-start(bf16[8,15,24,768]{3,2,1,0:T(8,128)(2,1)} %get-tuple-element.93), calls=%async_computation.4 | async-start | bytes 8847360 | tf_op jit(solution)/shard_map/all_to_all | solution.py:1258
  327.4 12.9 %collective-permute-start.10 = (bf16[2,768,768]{2,1,0:T(8,128)(2,1)}, bf16[2,768,768]{2,1,0:T(8,128)(2,1)S(1)}, u32[]{:S(2)}, u32[]{:S(2)}) collective-permute-start(bf16[2,768,768]{2,1,0:T(8,128)(2,1)} %shard_map.344), channel_id=1, source_target_pairs={{0,1},{1,0},{2,3},{3,2},{4,5},{5,4},{6,7},{7,6},{8,9},{9,8},{10,11... | collective-permute-start | bytes 7077896 | tf_op jit(solution)/shard_map/ppermute | solution.py:1199
  339.8 16.8 %collective-permute-start.9 = (bf16[2,768,768]{2,1,0:T(8,128)(2,1)}, bf16[2,768,768]{2,1,0:T(8,128)(2,1)S(1)}, u32[]{:S(2)}, u32[]{:S(2)}) collective-permute-start(bf16[2,768,768]{2,1,0:T(8,128)(2,1)} %shard_map.341), channel_id=1, source_target_pairs={{0,1},{1,0},{2,3},{3,2},{4,5},{5,4},{6,7},{7,6},{8,9},{9,8},{10,11... | collective-permute-start | bytes 7077896 | tf_op jit(solution)/shard_map/ppermute | solution.py:1199
  340.3 1.4 copy-start.13
  355.1 16.8 %copy-start.46 = (bf16[768]{0:T(1024)(128)(2,1)S(1)}, bf16[768]{0:T(1024)(128)(2,1)}, u32[]{:S(2)}) copy-start(bf16[768]{0:T(1024)(128)(2,1)} %param.39) | copy-start | bytes 4612
  355.1 43.7 %collective-permute-start.12 = (bf16[768,768]{1,0:T(8,128)(2,1)}, bf16[768,768]{1,0:T(8,128)(2,1)S(1)}, u32[]{:S(2)}, u32[]{:S(2)}) collective-permute-start(bf16[768,768]{1,0:T(8,128)(2,1)} %get-tuple-element.104), channel_id=1, source_target_pairs={{0,2},{1,3},{2,0},{3,1},{4,6},{5,7},{6,4},{7,5},{8,10},{9,11},{10,... | collective-permute-start | bytes 3538952 | tf_op jit(solution)/shard_map/ppermute | solution.py:1199
  371.4 37.1 %collective-permute-start.11 = (bf16[768,768]{1,0:T(8,128)(2,1)}, bf16[768,768]{1,0:T(8,128)(2,1)S(1)}, u32[]{:S(2)}, u32[]{:S(2)}) collective-permute-start(bf16[768,768]{1,0:T(8,128)(2,1)} %get-tuple-element.90.refs_11_), channel_id=1, source_target_pairs={{0,2},{1,3},{2,0},{3,1},{4,6},{5,7},{6,4},{7,5},{8,10},{9,11},{10,... | collective-permute-start | bytes 3538952 | tf_op jit(solution)/shard_map/ppermute | solution.py:1199
  398.8 9.7 %copy-start.20 = (bf16[768,768]{1,0:T(8,128)(2,1)}, bf16[768,768]{1,0:T(8,128)(2,1)S(1)}, u32[]{:S(2)}) copy-start(bf16[768,768]{1,0:T(8,128)(2,1)S(1)} %collective-permute-done.12.refs_4_) | copy-start | bytes 3538948
  414.9 27.4 %collective-permute-start.13 = (bf16[2,384,768]{2,1,0:T(8,128)(2,1)}, bf16[2,384,768]{2,1,0:T(8,128)(2,1)S(1)}, u32[]{:S(2)}, u32[]{:S(2)}) collective-permute-start(bf16[2,384,768]{2,1,0:T(8,128)(2,1)} %get-tuple-element.108), channel_id=1, source_target_pairs={{0,4},{4,0},{8,12},{12,8},{16,20},{20,16},{24,28},{28,24},{1,5},{5... | collective-permute-start | bytes 3538952 | tf_op jit(solution)/shard_map/ppermute | solution.py:1199
  446.7 125.1 %all-to-all-start.5 = ((bf16[8,15,24,768]{3,2,1,0:T(8,128)(2,1)}), bf16[8,15,24,768]{3,2,1,0:T(8,128)(2,1)}, u32[]{:S(2)}, u32[]{:S(2)}) async-start(bf16[8,15,24,768]{3,2,1,0:T(8,128)(2,1)} %shard_map.350), calls=%async_computation.5 | async-start | bytes 8847360 | tf_op jit(solution)/shard_map/all_to_all | solution.py:1258
  452.4 1.6 copy-start.9
  454.0 5.2 copy-start.5
  454.0 5.2 copy-start.6
  459.3 3.5 copy-start.17
  459.3 3.5 copy-start.18
  462.8 3.5 copy-start.7
  462.8 3.5 copy-start.16
  469.9 5.5 copy-start.24
  475.4 2.5 collective-permute-start.14
  475.4 60.1 %collective-permute-start.17 = (bf16[2,192,768]{2,1,0:T(8,128)(2,1)S(1)}, bf16[2,192,768]{2,1,0:T(8,128)(2,1)S(1)}, u32[]{:S(2)}, u32[]{:S(2)}) collective-permute-start(bf16[2,192,768]{2,1,0:T(8,128)(2,1)S(1)} %copy-done.24), channel_id=1, source_target_pairs={{0,8},{4,12},{8,0},{12,4},{16,24},{20,28},{24,16},{28,20},{1,9},{5... | collective-permute-start | bytes 1769480 | tf_op jit(solution)/shard_map/ppermute | solution.py:1199
  481.2 11.4 %collective-permute-start.15 = (f32[128,768]{1,0:T(8,128)}, f32[128,768]{1,0:T(8,128)S(1)}, u32[]{:S(2)}, u32[]{:S(2)}) collective-permute-start(f32[128,768]{1,0:T(8,128)} %get-tuple-element.127), channel_id=1, source_target_pairs={{0,2},{1,3},{2,0},{3,1},{4,6},{5,7},{6,4},{7,5},{8,10},{9,11},{10,... | collective-permute-start | bytes 1179656 | tf_op jit(solution)/shard_map/ppermute | solution.py:1199
  539.0 22.7 %collective-permute-start.18 = (bf16[2,96,768]{2,1,0:T(8,128)(2,1)}, bf16[2,96,768]{2,1,0:T(8,128)(2,1)S(1)}, u32[]{:S(2)}, u32[]{:S(2)}) collective-permute-start(bf16[2,96,768]{2,1,0:T(8,128)(2,1)} %get-tuple-element.132), channel_id=1, source_target_pairs={{0,16},{4,20},{8,24},{12,28},{16,0},{20,4},{24,8},{28,12},{1,17},{... | collective-permute-start | bytes 884744 | tf_op jit(solution)/shard_map/ppermute | solution.py:1199
  542.9 21.3 %collective-permute-start.16 = (f32[64,768]{1,0:T(8,128)}, f32[64,768]{1,0:T(8,128)S(1)}, u32[]{:S(2)}, u32[]{:S(2)}) collective-permute-start(f32[64,768]{1,0:T(8,128)} %get-tuple-element.129.refs_3_), channel_id=1, source_target_pairs={{0,4},{4,0},{8,12},{12,8},{16,20},{20,16},{24,28},{28,24},{1,5},{5... | collective-permute-start | bytes 589832 | tf_op jit(solution)/shard_map/ppermute | solution.py:1199
  564.2 31.0 %collective-permute-start.23 = (bf16[2,96,768]{2,1,0:T(8,128)(2,1)}, bf16[2,96,768]{2,1,0:T(8,128)(2,1)S(1)}, u32[]{:S(2)}, u32[]{:S(2)}) collective-permute-start(bf16[2,96,768]{2,1,0:T(8,128)(2,1)} %shard_map.358.refs_7_.refs_1_), channel_id=1, source_target_pairs={{0,16},{4,20},{8,24},{12,28},{16,0},{20,4},{24,8},{28,12},{1,17},{... | collective-permute-start | bytes 884744 | tf_op jit(solution)/shard_map/ppermute | solution.py:1199
  566.6 19.1 %collective-permute-start.19 = (f32[64,768]{1,0:T(8,128)}, f32[64,768]{1,0:T(8,128)S(1)}, u32[]{:S(2)}, u32[]{:S(2)}) collective-permute-start(f32[64,768]{1,0:T(8,128)} %shard_map.356.refs_6_.refs_1_), channel_id=1, source_target_pairs={{0,8},{4,12},{8,0},{12,4},{16,24},{20,28},{24,16},{28,20},{1,9},{5... | collective-permute-start | bytes 589832 | tf_op jit(solution)/shard_map/ppermute | solution.py:1199
  569.5 23.1 %collective-permute-start.20 = (f32[64,768]{1,0:T(8,128)}, f32[64,768]{1,0:T(8,128)S(1)}, u32[]{:S(2)}, u32[]{:S(2)}) collective-permute-start(f32[64,768]{1,0:T(8,128)} %shard_map.356.refs_6_.refs_1_), channel_id=1, source_target_pairs={{0,16},{4,20},{8,24},{12,28},{16,0},{20,4},{24,8},{28,12},{1,17},{... | collective-permute-start | bytes 589832 | tf_op jit(solution)/shard_map/ppermute | solution.py:1199
  569.6 23.0 %collective-permute-start.21 = (f32[64,768]{1,0:T(8,128)}, f32[64,768]{1,0:T(8,128)S(1)}, u32[]{:S(2)}, u32[]{:S(2)}) collective-permute-start(f32[64,768]{1,0:T(8,128)} %shard_map.356.refs_6_.refs_1_), channel_id=1, source_target_pairs={{0,24},{4,28},{8,16},{12,20},{16,8},{20,12},{24,0},{28,4},{1,25},{... | collective-permute-start | bytes 589832 | tf_op jit(solution)/shard_map/ppermute | solution.py:1199
  585.8 6.8 %copy-start.33 = (f32[64,768]{1,0:T(8,128)}, f32[64,768]{1,0:T(8,128)S(1)}, u32[]{:S(2)}) copy-start(f32[64,768]{1,0:T(8,128)S(1)} %collective-permute-done.19.refs_2_) | copy-start | bytes 589828
  597.9 16.8 %collective-permute-start.24 = (bf16[2,192,768]{2,1,0:T(8,128)(2,1)}, bf16[2,192,768]{2,1,0:T(8,128)(2,1)S(1)}, u32[]{:S(2)}, u32[]{:S(2)}) collective-permute-start(bf16[2,192,768]{2,1,0:T(8,128)(2,1)} %shard_map.361.refs_1_), channel_id=1, source_target_pairs={{0,4},{4,0},{8,12},{12,8},{16,20},{20,16},{24,28},{28,24},{1,5},{5... | collective-permute-start | bytes 1769480 | tf_op jit(solution)/shard_map/ppermute | solution.py:1199
  598.9 20.3 %collective-permute-start.26 = (bf16[2,192,768]{2,1,0:T(8,128)(2,1)}, bf16[2,192,768]{2,1,0:T(8,128)(2,1)S(1)}, u32[]{:S(2)}, u32[]{:S(2)}) collective-permute-start(bf16[2,192,768]{2,1,0:T(8,128)(2,1)} %shard_map.361.refs_1_), channel_id=1, source_target_pairs={{0,8},{4,12},{8,0},{12,4},{16,24},{20,28},{24,16},{28,20},{1,9},{5... | collective-permute-start | bytes 1769480 | tf_op jit(solution)/shard_map/ppermute | solution.py:1199
  603.6 11.1 %collective-permute-start.22 = (bf16[64,768]{1,0:T(8,128)(2,1)}, bf16[64,768]{1,0:T(8,128)(2,1)S(1)}, u32[]{:S(2)}, u32[]{:S(2)}) collective-permute-start(bf16[64,768]{1,0:T(8,128)(2,1)} %shard_map.360.refs_3_.refs_1_), channel_id=1, source_target_pairs={{0,4},{4,0},{8,12},{12,8},{16,20},{20,16},{24,28},{28,24},{1,5},{5... | collective-permute-start | bytes 294920 | tf_op jit(solution)/shard_map/ppermute | solution.py:1199
  617.8 5.9 collective-permute-start.25
  619.3 4.4 copy-start.14
  619.3 14.0 %collective-permute-start.28 = (bf16[2,192,768]{2,1,0:T(8,128)(2,1)S(1)}, bf16[2,192,768]{2,1,0:T(8,128)(2,1)S(1)}, u32[]{:S(2)}, u32[]{:S(2)}) collective-permute-start(bf16[2,192,768]{2,1,0:T(8,128)(2,1)S(1)} %collective-permute-done.26.refs_3_), channel_id=1, source_target_pairs={{0,4},{4,0},{8,12},{12,8},{16,20},{20,16},{24,28},{28,24},{1,5},{5... | collective-permute-start | bytes 1769480 | tf_op jit(solution)/shard_map/ppermute | solution.py:1199
  626.2 12.0 %collective-permute-start.27 = (bf16[256,768]{1,0:T(8,128)(2,1)}, bf16[256,768]{1,0:T(8,128)(2,1)S(1)}, u32[]{:S(2)}, u32[]{:S(2)}) collective-permute-start(bf16[256,768]{1,0:T(8,128)(2,1)} %shard_map.363.refs_1_), channel_id=1, source_target_pairs={{0,1},{1,0},{2,3},{3,2},{4,5},{5,4},{6,7},{7,6},{8,9},{9,8},{10,11... | collective-permute-start | bytes 1179656 | tf_op jit(solution)/shard_map/ppermute | solution.py:1199
  (18 other events, 15.5 us)
